TPU v7x, 256 devices: a whole 4x4x8 slice. The times are simulated.
256 devices in a mesh: gx: 8 (over x, z_hi), gy: 32 (over y, z_lo, core).
Axes of the slice: x: 4, y: 4, z: 8 (z_hi: 2, z_lo: 4; z = z_hi * 4 + z_lo), core: 2. Of those that a mesh axis runs over, the one named last changes fastest.
Arguments:
- density: float32 [1, 2048, 2048], P(None, 'gy', 'gx'), may hold values from 0.35 to 2.5, as said below
- xmomentum: float32 [1, 2048, 2048], P(None, 'gy', 'gx'), may hold values from -2.5 to 2.5
- ymomentum: float32 [1, 2048, 2048], P(None, 'gy', 'gx'), may hold values from -2.5 to 2.5
- shear_shift: int32 [1], replicated, may hold values from 0 to 2047
Outputs:
- density_new: float32 [1, 2048, 2048], P(None, 'gy', 'gx')
- xmomentum_new: float32 [1, 2048, 2048], P(None, 'gy', 'gx')
- ymomentum_new: float32 [1, 2048, 2048], P(None, 'gy', 'gx')
- potential: float32 [1, 2048, 2048], P(None, 'gy', 'gx')
Inputs may be any that keep to these rules, and one draw needn't show every extreme that they name: Every density is positive.
All inputs are finite; a program needn't handle non-finite values.
Results may differ from a plain program's by a relative error of at most 0.00065.
Values sent between devices are 32-bit elements; how exact they have to be, the bound alone decides.
No kernel may reach another device: no remote copies, remote signals or barrier semaphores. Data moves between devices by JAX's collectives and lax.ppermute only.
A program may use at most 64 MiB of HBM per device.

v0:
```python
import functools

import jax
import jax.numpy as jnp
import ml_dtypes
import numpy as np
from jax import lax
from jax.experimental import pallas as pl
from jax.experimental.pallas import tpu as pltpu
from jax.sharding import PartitionSpec as P

NX = 2048
NY = 2048
ROWS = 64
COLS = 256
GX = 8
GY = 32

time_step = 0.15
omega_rate = 0.5
shear_rate = 1.5
thickness = 0.5

BF = jnp.bfloat16
F32 = jnp.float32


def halves(table):
    table = np.asarray(table, np.float32)
    head = table.astype(ml_dtypes.bfloat16)
    rest = (table - head.astype(np.float32)).astype(ml_dtypes.bfloat16)
    return head, rest


def turn(index, length):
    angle = 2.0 * np.pi * (np.asarray(index) % length) / length
    return np.cos(angle), np.sin(angle)


@functools.cache
def host_tables():
    out = {}
    eye8 = np.eye(8)
    cos32, sin32 = turn(np.outer(np.arange(32), np.arange(32)), 32)

    def spread(table):
        return np.einsum("jm,ab->ajmb", table, eye8).reshape(256, 256)

    out["blocks"] = halves(np.concatenate([spread(cos32), spread(-sin32)], 1))
    m1 = np.repeat(np.arange(32), 8)
    tc, ts = turn(np.outer(np.arange(64), m1), NY)
    out["twist_cos"] = tc.astype(np.float32)
    out["twist_sin"] = ts.astype(np.float32)
    c64, s64 = turn(np.outer(np.arange(32), np.arange(64)), 64)
    last = np.zeros((16, 128))
    last[0, :64] = 1.0 - 2.0 * (np.arange(64) % 2)
    out["inner"] = halves(
        np.concatenate([np.concatenate([c64, s64], 1), np.concatenate([-s64, c64], 1), last])
    )
    rows = np.arange(256)
    c256, s256 = turn(np.outer(rows, rows), 256)
    out["groups"] = halves(np.concatenate([c256, s256]))
    lane = np.arange(128)
    sign = np.where(lane < 64, 1.0, -1.0)
    tc, ts = turn(np.outer(rows, lane % 8), NX)
    out["radial_cos"] = tc.astype(np.float32)
    out["radial_sin"] = (ts * sign).astype(np.float32)
    c8, s8 = turn(np.outer(np.arange(8), np.arange(8)), 8)
    lines = np.eye(8)
    ck, sk = np.kron(lines, c8), np.kron(lines, s8)
    out["cells"] = halves(np.block([[ck, -sk], [sk, ck]]))
    out["cells_back"] = halves(np.block([[ck, sk], [-sk, ck]]))
    order = rows // 32 + 8 * (rows % 32)
    c256, s256 = turn(np.outer(rows, order), 256)
    out["groups_back"] = halves(np.concatenate([c256, s256]))
    tc, ts = turn(np.outer(order, lane % 8), NX)
    out["return_cos"] = tc.astype(np.float32)
    out["return_sin"] = (ts * sign).astype(np.float32)
    c64, s64 = turn(np.outer(np.arange(64), np.arange(32)), 64)
    out["inner_back"] = halves(np.concatenate([c64, s64]))
    pair = np.arange(512) // 128
    part = np.arange(512) % 128 // 64
    which = np.arange(512) % 64 // 8
    m1 = pair * 8 + which
    q = np.arange(512) % 8
    tc, ts = turn(np.outer(np.arange(64), m1), NY)
    out["back_cos"] = tc.astype(np.float32)
    out["back_sin"] = (ts * np.where(part == 0, 1.0, -1.0)).astype(np.float32)
    j = np.repeat(np.arange(32), 8)
    own = np.tile(np.arange(8), 32)
    c32, s32 = turn(np.outer(j, m1), 32)
    weight = np.where(part == 0, c32, -s32)
    weight = np.where((part == 1) & (m1 == 0), 1.0, weight)
    out["blocks_back"] = halves(weight * (own[:, None] == q[None, :]))
    return out


def split(value):
    head = value.astype(BF)
    rest = (value - head.astype(F32)).astype(BF)
    return head, rest


NN = (((1,), (0,)), ((), ()))
NT = (((1,), (1,)), ((), ()))


def product(table_head, table_rest, value, dims=NN):
    head, rest = split(value)
    dot = functools.partial(lax.dot_general, dimension_numbers=dims, preferred_element_type=F32)
    return dot(table_head, head) + (dot(table_head, rest) + dot(table_rest, head))


def product_right(value, table_head, table_rest):
    head, rest = split(value)
    dot = functools.partial(lax.dot_general, dimension_numbers=NN, preferred_element_type=F32)
    return dot(head, table_head) + (dot(rest, table_head) + dot(head, table_rest))


def roll(value, shift, axis):
    return pltpu.roll(value, shift % value.shape[axis], axis)


def lanes_of(shape):
    return lax.broadcasted_iota(jnp.int32, shape, 1)


def rows_of(shape):
    return lax.broadcasted_iota(jnp.int32, shape, 0)


def interface(left, right, normal, parts=3):
    speed = jnp.maximum(jnp.abs(left[3]), jnp.abs(right[3])) + 1.0
    fluxes = []
    for part in range(parts):
        f_left = left[part] * left[3]
        f_right = right[part] * right[3]
        if part == normal:
            f_left = f_left + left[0]
            f_right = f_right + right[0]
        fluxes.append(0.5 * (f_left + f_right) - 0.5 * speed * (right[part] - left[part]))
    return fluxes


def with_speed(fields, normal):
    return (*fields, fields[normal] / fields[0])


def inner_fluxes(state, parts):
    lane = lanes_of((ROWS, COLS))
    row = rows_of((ROWS, COLS))
    mid = with_speed(state, 1)
    west = interface([roll(v, 1, 1) for v in mid], mid, 1, parts)
    mid = with_speed(state, 2)
    south = interface([roll(v, 1, 0) for v in mid], mid, 2, parts)
    return [jnp.where(lane == 0, 0.0, v) for v in west], [jnp.where(row == 0, 0.0, v) for v in south]


def pack_kernel(scalars, rho, mx, my, out):
    state = (rho[...], mx[...], my[...])
    (west,), (south,) = inner_fluxes(state, 1)
    change = roll(west, -1, 1) - west + roll(south, -1, 0) - south
    partial = state[0] - time_step * change
    row = rows_of((8, COLS))
    edges = jnp.zeros((8, COLS), F32)
    for f in range(3):
        edges = jnp.where(row == f, state[f][0:1, :], edges)
        edges = jnp.where(row == 3 + f, state[f][ROWS - 1 : ROWS, :], edges)
    tall = jnp.concatenate([partial, edges, jnp.zeros((56, COLS), F32)], 0).T
    lane = lanes_of((ROWS, 128))
    low = jnp.zeros((ROWS, 128), F32)
    high = jnp.zeros((ROWS, 128), F32)
    for f in range(3):
        low = jnp.where(lane == 72 + f, state[f][:, 0:1], low)
        high = jnp.where(lane == 75 + f, state[f][:, COLS - 1 : COLS], high)
    out[0:ROWS, :] = tall[0:ROWS] + low + pltpu.roll(high, scalars[0], 0)
    out[ROWS:, :] = tall[ROWS:]


def finish_kernel(scalars, rho, mx, my, arrived, rho_out, mx_out, my_out):
    state = (rho[...], mx[...], my[...])
    lane = lanes_of((ROWS, COLS))
    row = rows_of((ROWS, COLS))
    west, south = inner_fluxes(state, 3)
    across = arrived[...].T[32:40]
    beside = arrived[0:ROWS, :]
    beside_high = pltpu.roll(beside, scalars[1], 0)
    new = []
    for f in range(3):
        east = jnp.where(lane == COLS - 1, beside_high[:, 41 + f : 42 + f], roll(west[f], -1, 1))
        north = jnp.where(row == ROWS - 1, across[3 + f : 4 + f, :], roll(south[f], -1, 0))
        west_f = jnp.where(lane == 0, beside[:, 38 + f : 39 + f], west[f])
        south_f = jnp.where(row == 0, across[f : f + 1, :], south[f])
        new.append(state[f] - time_step * (east - west_f + north - south_f))
    rho_out[...] = new[0]
    mx_out[...] = new[1] + time_step * 2.0 * omega_rate * state[2]
    my_out[...] = new[2] - time_step * (2.0 - shear_rate) * omega_rate * state[1]


def forward_kernel(
    scalars, arrived, blocks_h, blocks_l, twist_cos, twist_sin, inner_h, inner_l, out, ride
):
    row = scalars[4]
    narrow = lanes_of((32, 128))
    last = arrived[224:256, :]
    wrapped = pltpu.roll(last, scalars[2], 0)
    last = jnp.where((narrow >= 75) & (narrow < 78), wrapped, last)
    tall = jnp.concatenate([arrived[0:224, :], last], 0).T
    lane = lanes_of((8, 256))
    upper = tall[64:72]
    before = jnp.where(lane % 32 == 0, roll(upper, -31, 1), roll(upper, 1, 1))
    south = interface(
        with_speed([before[3 + f : 4 + f] for f in range(3)], 2),
        with_speed([upper[f : f + 1] for f in range(3)], 2),
        2,
    )
    valid = jnp.zeros((1, 256), jnp.int32) + row >= 0
    side = tall[72:80]
    before = roll(side, 32, 1)
    left = [before[3 + f : 4 + f] for f in range(3)]
    right = [side[f : f + 1] for f in range(3)]
    left[0] = jnp.where(valid, left[0], 1.0)
    right[0] = jnp.where(valid, right[0], 1.0)
    west = interface(with_speed(left, 1), with_speed(right, 1), 1)
    west = [jnp.where(valid, v, 0.0) for v in west]
    line = lanes_of((1, 256))
    north = [jnp.where(line % 32 == 31, roll(v, 31, 1), roll(v, -1, 1)) for v in south]
    east = [roll(v, -32, 1) for v in west]
    rows8 = rows_of((8, 256))
    rows16 = rows_of((16, 256))
    rows64 = rows_of((64, 256))
    fluxes = jnp.zeros((16, 256), F32)
    for at, value in enumerate(south + north + west + east):
        fluxes = jnp.where(rows16 == at, value, fluxes)
    back = jnp.concatenate([jnp.zeros((32, 256), F32), fluxes, jnp.zeros((80, 256), F32)], 0).T
    last = back[224:256]
    wrapped = pltpu.roll(last, scalars[3], 0)
    ride[0:224, :] = back[0:224]
    ride[224:256, :] = jnp.where((narrow >= 41) & (narrow < 44), wrapped, last)
    density = tall[0:64]
    density = density + jnp.where(rows64 == 0, time_step * south[0], 0.0)
    density = density - jnp.where(rows64 == 63, time_step * north[0], 0.0)
    edge = jnp.where(rows8 == 0, time_step * west[0], 0.0)
    first = product_right(jnp.concatenate([density, edge], 0), blocks_h[...], blocks_l[...])
    tc = twist_cos[...]
    ts = twist_sin[...]
    re, im = first[:64, :256], first[:64, 256:]
    main = jnp.concatenate([re * tc + im * ts, im * tc - re * ts], 0)
    re, im = first[64:65, :256], first[64:65, 256:]
    here = rows64 == row
    edge = jnp.concatenate(
        [jnp.where(here, re * tc + im * ts, 0.0), jnp.where(here, im * tc - re * ts, 0.0)], 0
    )
    waves = product(inner_h[...], inner_l[...], jnp.concatenate([main, edge], 1))
    rows32 = rows_of((32, 128))
    for g in range(8):
        place = 32 * (g % 4)
        pieces = []
        for start in (0, 256):
            tile = slice(start + g // 4 * 128, start + g // 4 * 128 + 128)
            real = waves[0:32, tile]
            imag = waves[32:64, tile]
            if g == 0:
                imag = jnp.where((rows32 == 0) & (narrow < 8), waves[64:65, tile], imag)
            pieces.append((real, imag))
        both = roll(pieces[1][1], 96 - place, 1)
        both = jnp.where(narrow < 96, roll(pieces[0][1], 64 - place, 1), both)
        both = jnp.where(narrow < 64, roll(pieces[1][0], 32 - place, 1), both)
        both = jnp.where(narrow < 32, roll(pieces[0][0], -place, 1), both)
        out[g * 32 : (g + 1) * 32, :] = both


def radial_kernel(
    scalars,
    arrived,
    ride,
    theta_cos,
    theta_sin,
    theta_cos_back,
    theta_sin_back,
    weights,
    wrap_cos,
    wrap_sin,
    groups_h,
    groups_l,
    radial_cos,
    radial_sin,
    cells_h,
    cells_l,
    cells_back_h,
    cells_back_l,
    groups_back_h,
    groups_back_l,
    return_cos,
    return_sin,
    out,
):
    shape = (256, 128)
    half = functools.partial(roll, shift=64, axis=1)

    def apart(value):
        lane = lanes_of(value.shape)
        first = jnp.zeros(value.shape, jnp.int32) + scalars[5] == 1
        value = jnp.where(lane % 64 < 32, value, 0.0)
        fifth = roll(value, -32, 1)
        slot = (lane >= 64) & (lane < 72) & first
        return jnp.where((lane >= 32) & (lane < 40), fifth, jnp.where(slot, 0.0, value))

    lane = lanes_of(shape)
    row = rows_of(shape)
    sign = jnp.where(lane < 64, 1.0, -1.0)
    value = arrived[...]
    edge = jnp.sum(value[0:ROWS], axis=0, keepdims=True)
    edge = apart(roll(jnp.broadcast_to(edge, (8, 128)), -32, 1))
    lane8 = lanes_of((8, 128))
    beside = jnp.where(lane8 % 8 == 7, roll(edge, 7, 1), roll(edge, -1, 1))
    beside = beside * wrap_cos[...] + half(beside) * wrap_sin[...]
    value = apart(value)
    value = value + jnp.where(row == 0, edge[0:1], 0.0) - jnp.where(row == 255, beside[0:1], 0.0)
    value = value * theta_cos[...] + half(value) * theta_sin[...]
    value = product_right(value, cells_h[...], cells_l[...])
    value = value * radial_cos[...] + half(value) * radial_sin[...]
    both = product(groups_h[...], groups_l[...], value)
    value = both[:256] + sign * half(both[256:])
    value = value * weights[...]
    blocks = [value[32 * k : 32 * k + 32] for k in range(8)]
    narrow = lanes_of((32, 128))
    for bit in (1, 2, 4):
        swapped = list(blocks)
        for k in range(8):
            if k & bit == 0:
                a, b = blocks[k], blocks[k + bit]
                low = narrow & bit == 0
                swapped[k] = jnp.where(low, a, roll(b, bit, 1))
                swapped[k + bit] = jnp.where(low, roll(a, -bit, 1), b)
        blocks = swapped
    value = jnp.concatenate(blocks, 0)
    value = product_right(value, cells_back_h[...], cells_back_l[...])
    value = value * return_cos[...] - half(value) * return_sin[...]
    both = product(groups_back_h[...], groups_back_l[...], value)
    value = both[:256] - sign * half(both[256:])
    value = value * theta_cos_back[...] - half(value) * theta_sin_back[...]
    first = jnp.zeros(shape, jnp.int32) + scalars[5] == 1
    value = jnp.where((lane >= 64) & (lane < 72) & first, roll(value, 32, 1), value)
    out[...] = jnp.where((lane >= 32) & (lane < 44), ride[...], value)


def backward_kernel(arrived, inner_h, inner_l, back_cos, back_sin, blocks_h, blocks_l, out):
    lane = lanes_of((32, 128))
    low = lane % 64 < 32
    pairs = []
    for h in range(4):
        even = arrived[64 * h : 64 * h + 32, :]
        odd = arrived[64 * h + 32 : 64 * h + 64, :]
        pairs.append(jnp.where(low, even, roll(odd, 32, 1)))
    value = jnp.concatenate(pairs, 1)
    both = product(inner_h[...], inner_l[...], value)
    wide = lanes_of((64, 128))
    row = rows_of((64, 128))
    sign = jnp.where(wide < 64, 1.0, -1.0)
    parity = jnp.where(row % 2 == 0, 1.0, -1.0)
    turned = []
    for h in range(4):
        tile = slice(128 * h, 128 * h + 128)
        part = both[:64, tile] - sign * roll(both[64:, tile], 64, 1)
        part = part * back_cos[:, tile] - roll(part, 64, 1) * back_sin[:, tile]
        if h == 0:
            part = jnp.where((wide >= 64) & (wide < 72), parity * pairs[0][0:1, :], part)
        turned.append(part)
    turned = jnp.concatenate(turned, 1)
    turned = jnp.concatenate([turned, turned], 0)
    out[...] = product(blocks_h[...], blocks_l[...], turned, NT)


def last_kernel(arrived, out):
    out[...] = arrived[...].T[:ROWS]


VMEM = pl.BlockSpec(memory_space=pltpu.VMEM)
SMEM = pl.BlockSpec(memory_space=pltpu.SMEM)


def call(kernel, shapes, *args, name, smem=0):
    many = isinstance(shapes, list)
    outs = [jax.ShapeDtypeStruct(s, F32) for s in (shapes if many else [shapes])]
    return pl.pallas_call(
        kernel,
        out_shape=outs if many else outs[0],
        in_specs=[SMEM] * smem + [VMEM] * (len(args) - smem),
        out_specs=[VMEM] * len(outs) if many else VMEM,
        name=name,
        compiler_params=pltpu.CompilerParams(vmem_limit_bytes=32 * 1024 * 1024),
        cost_estimate=pl.CostEstimate(flops=100_000_000, bytes_accessed=1_000_000, transcendentals=0),
    )(*args)


def radial_tables(shift):
    shape = (256, 128)
    row = lax.broadcasted_iota(jnp.int32, shape, 0)
    lane = lax.broadcasted_iota(jnp.int32, shape, 1)
    line = lane % 64 // 8
    inside = lane % 8
    wave = lax.axis_index("gx") * 4 + line + GY * lax.axis_index("gy")
    wave = jnp.where(line < 4, wave, NY // 2)
    sigma = wave * shift % NY
    sign = jnp.where(lane < 64, 1.0, -1.0)

    def phase(cell):
        angle = (sigma * cell % (NX * NY)).astype(F32) * (2.0 * jnp.pi / (NX * NY))
        return jnp.cos(angle), jnp.sin(angle) * sign

    there = phase(row + COLS * inside)
    back = phase(row * 8 + inside)
    n = inside + 8 * row
    n = jnp.where(n < NX // 2, n, n - NX)
    kx = 2.0 * jnp.pi / NX * (n.astype(F32) + sigma.astype(F32) / NY)
    ky = 2.0 * jnp.pi / NY * wave.astype(F32)
    size = jnp.sqrt(kx * kx + ky * ky)
    anchor = (wave == 0) & (n == 0)
    size = jnp.where(anchor, 1.0, size)
    single = (wave == 0) | (wave == NY // 2)
    scale = jnp.where(single, 1.0, 2.0) / (NX * NY)
    weights = jnp.where(anchor, 0.0, -jnp.exp(-thickness * size) / size) * scale
    angle = sigma[:8].astype(F32) * (2.0 * jnp.pi / NY)
    last = inside[:8] == 7
    wrap_cos = jnp.where(last, jnp.cos(angle), 1.0)
    wrap_sin = jnp.where(last, jnp.sin(angle) * sign[:8], 0.0)
    return *there, *back, weights, wrap_cos, wrap_sin


def shards(density, xmomentum, ymomentum, shear_shift):
    t = host_tables()
    rho, mx, my = density[0], xmomentum[0], ymomentum[0]
    shift = shear_shift[0]
    radial = lax.axis_index("gx")
    flat = radial * GY + lax.axis_index("gy")
    off = shift % ROWS
    wrap_off = jnp.where(radial == GX - 1, off, 0)
    hop = (shift // ROWS + (flat % ROWS + off) // ROWS) % GY
    scalars = jnp.stack(
        [
            (ROWS - wrap_off) % ROWS,
            wrap_off,
            (GY - hop) % GY,
            hop,
            jnp.where(flat < ROWS, flat, -1),
            (flat == 0).astype(jnp.int32),
        ]
    ).astype(jnp.int32)
    everyone = ("gx", "gy")
    block = (ROWS, COLS)
    table = (256, 128)
    columns = call(pack_kernel, table, scalars, rho, mx, my, name="pack", smem=1)
    columns = lax.all_to_all(columns, everyone, 0, 0, tiled=True)
    waves, ride = call(
        forward_kernel,
        [table, table],
        scalars,
        columns,
        *t["blocks"],
        t["twist_cos"],
        t["twist_sin"],
        *t["inner"],
        name="forward",
        smem=1,
    )
    waves = lax.all_to_all(waves, everyone, 0, 0, tiled=True)
    solved = call(
        radial_kernel,
        table,
        scalars,
        waves,
        ride,
        *radial_tables(shift),
        *t["groups"],
        t["radial_cos"],
        t["radial_sin"],
        *t["cells"],
        *t["cells_back"],
        *t["groups_back"],
        t["return_cos"],
        t["return_sin"],
        name="radial",
        smem=1,
    )
    solved = lax.all_to_all(solved, everyone, 0, 0, tiled=True)
    lines = call(
        backward_kernel,
        table,
        solved,
        *t["inner_back"],
        t["back_cos"],
        t["back_sin"],
        *t["blocks_back"],
        name="backward",
    )
    lines = lax.all_to_all(lines, "gy", 0, 0, tiled=True)
    rho_new, mx_new, my_new = call(
        finish_kernel, [block, block, block], scalars, rho, mx, my, solved, name="finish", smem=1
    )
    potential = call(last_kernel, block, lines, name="last")
    return rho_new[None], mx_new[None], my_new[None], potential[None]


def solution(mesh):
    spec = P(None, "gy", "gx")
    return jax.shard_map(
        shards,
        mesh=mesh,
        in_specs=(spec, spec, spec, P()),
        out_specs=(spec, spec, spec, spec),
        check_vma=False,
    )
```

profile of v0, /device:TPU:1, one launch (start us, length us, event | category | flops | bytes accessed | tf_op | source)
XLA Modules:
  0.0 90.1 jit_solution(9842879358742603481)
XLA Ops:
  0.6 0.0 copy-start.26
  1.4 0.0 copy-start.24
  1.4 0.0 copy-start.25
  1.5 0.1 stack.31.scalars
  1.5 0.0 copy-done.26
  1.5 0.7 copy-done.24
  2.2 0.0 copy-done.25
  2.2 1.5 %pack.1 = f32[256,128]{1,0:T(8,128)} custom-call(s32[6]{0:T(128)S(1)} %stack.31.scalars, f32[64,256]{1,0:T(8,128)S(1)} %bitcast.40, f32[64,256]{1,0:T(8,128)S(1)} %bitcast.42, f32[64,256]{1,0:T(8,128)S(1)} %bitcast.44), custom_call_target="tpu_custom_call" | custom-call | flops 100000000 | bytes 1000000 | tf_op jit(solution)/shard_map/pack/pallas_call | solution.py:386
  3.8 15.7 %all-to-all-start = ((f32[256,1,128]{2,1,0:T(1,128)}), f32[256,1,128]{2,1,0:T(1,128)S(1)}, u32[]{:S(2)}, u32[]{:S(2)}) async-start(f32[256,1,128]{2,1,0:T(1,128)} %bitcast.11), calls=%async_computation | async-start | bytes 262144 | tf_op jit(solution)/shard_map/all_to_all | solution.py:454
  19.5 0.0 copy-start.23
  19.5 0.0 copy-start.22
  19.6 12.7 %all-to-all-done = f32[256,1,128]{2,1,0:T(1,128)S(1)} async-done(((f32[256,1,128]{2,1,0:T(1,128)}), f32[256,1,128]{2,1,0:T(1,128)S(1)}, u32[]{:S(2)}, u32[]{:S(2)}) %all-to-all-start) | async-done | bytes 131104 | tf_op jit(solution)/shard_map/all_to_all | solution.py:454
  32.4 0.0 copy-done.14
  32.4 0.0 copy-done.15
  32.4 0.0 copy-done.6
  32.4 0.0 copy-done.7
  32.4 0.0 copy-done.23
  32.4 0.0 copy-done.22
  32.4 0.0 copy-start.5
  32.4 0.0 copy-start.11
  32.4 0.0 copy-start.12
  32.4 0.0 copy-start.13
  32.5 0.0 copy-start.16
  32.5 0.0 copy-start.17
  32.5 0.0 copy-start.18
  32.5 0.0 copy-start.19
  32.5 2.0 %forward.1 = (f32[256,128]{1,0:T(8,128)}, f32[256,128]{1,0:T(8,128)S(1)}) custom-call(s32[6]{0:T(128)S(1)} %stack.31.scalars, f32[256,128]{1,0:T(8,128)S(1)} %bitcast.38, bf16[256,512]{1,0:T(8,128)(2,1)S(1)} %copy-done.7, bf16[256,512]{1,0:T(8,128)(2,1)S(1)} %copy-done.6, f32[64,256]{1,0:T(8,128)S(1)} %copy-done.15, f32[64,256]{1,0:T(8,128)S(1)} %copy-done.14, ...), custom_call_target="tpu_custom_call" | custom-call | flops 100000000 | bytes 1000000 | tf_op jit(solution)/shard_map/forward/pallas_call | solution.py:386
  34.5 5.7 %all-to-all-start.1 = ((f32[256,1,128]{2,1,0:T(1,128)}), f32[256,1,128]{2,1,0:T(1,128)S(1)}, u32[]{:S(2)}, u32[]{:S(2)}) async-start(f32[256,1,128]{2,1,0:T(1,128)} %bitcast.14), calls=%async_computation.1 | async-start | bytes 262144 | tf_op jit(solution)/shard_map/all_to_all | solution.py:467
  40.2 0.0 copy-start.2
  40.2 0.0 copy-start.3
  40.2 0.0 copy-start.10
  40.2 1.2 %multiply_multiply_fusion = (f32[256,128]{1,0:T(8,128)S(1)}, f32[256,128]{1,0:T(8,128)S(1)}, f32[256,128]{1,0:T(8,128)S(1)}, f32[256,128]{1,0:T(8,128)S(1)}, f32[256,128]{1,0:T(8,128)S(1)}) fusion(s32[256]{0:T(256)S(1)} %iota_multiply_fusion, s32[128]{0:T(128)S(1)} %get-tuple-element.23, s32[128]{0:T(128)S(1)} %get-tuple-element.25, ...), kind=kLoop, calls=%fused_computation.28 | loop fusion | flops 3014656 | bytes 659212 | tf_op jit(solution)/shard_map/mul | solution.py:423
  41.5 11.8 %all-to-all-done.1 = f32[256,1,128]{2,1,0:T(1,128)S(1)} async-done(((f32[256,1,128]{2,1,0:T(1,128)}), f32[256,1,128]{2,1,0:T(1,128)S(1)}, u32[]{:S(2)}, u32[]{:S(2)}) %all-to-all-start.1) | async-done | bytes 131104 | tf_op jit(solution)/shard_map/all_to_all | solution.py:467
  53.3 0.0 copy-done.5
  53.4 0.0 copy-start.1
  53.4 0.0 copy-start.8
  53.4 0.0 copy-start.9
  53.4 0.0 copy-start.20
  53.4 0.0 copy-start.21
  53.4 2.9 %radial.1 = f32[256,128]{1,0:T(8,128)S(1)} custom-call(s32[6]{0:T(128)S(1)} %stack.31.scalars, f32[256,128]{1,0:T(8,128)S(1)} %bitcast.34, f32[256,128]{1,0:T(8,128)S(1)} %get-tuple-element.10.ride, f32[256,128]{1,0:T(8,128)S(1)} %get-tuple-element.20.theta_cos, f32[256,128]{1,0:T(8,128)S(1)} %get-tuple-element.19.theta_sin, ...), custom_call_target="tpu_custom_call" | custom-call | flops 100000000 | bytes 1000000 | tf_op jit(solution)/shard_map/radial/pallas_call | solution.py:386
  56.3 0.0 copy-start
  56.4 18.5 %all_to_all.44 = f32[256,1,128]{2,1,0:T(1,128)S(1)} all-to-all(f32[256,1,128]{2,1,0:T(1,128)S(1)} %bitcast.35), channel_id=1, replica_groups=mesh['gx'=8,'gy'=32] {'gx','gy'}, dimensions={0} | all-to-all | bytes 262144 | tf_op jit(solution)/shard_map/all_to_all | solution.py:486
  74.9 0.0 copy-done.1
  74.9 1.5 %backward.1 = f32[256,128]{1,0:T(8,128)} custom-call(f32[256,128]{1,0:T(8,128)S(1)} %bitcast.36, bf16[128,32]{1,0:T(8,128)(2,1)S(1)} %copy-done.21, bf16[128,32]{1,0:T(8,128)(2,1)S(1)} %copy-done.20, f32[64,512]{1,0:T(8,128)S(1)} %copy-done.9, f32[64,512]{1,0:T(8,128)S(1)} %copy-done.8, bf16[256,512]{1,0:T(8,128)(2,1)S(1)} %copy-done.1, ...), custom_call_target="tpu_custom_call" | custom-call | flops 100000000 | bytes 1000000 | tf_op jit(solution)/shard_map/backward/pallas_call | solution.py:386
  76.4 4.1 %all-to-all-start.3 = ((f32[32,8,128]{2,1,0:T(8,128)}), f32[32,8,128]{2,1,0:T(8,128)S(1)}, u32[]{:S(2)}, u32[]{:S(2)}) async-start(f32[32,8,128]{2,1,0:T(8,128)} %bitcast.22), calls=%async_computation.3 | async-start | bytes 262144 | tf_op jit(solution)/shard_map/all_to_all | solution.py:497
  80.5 1.6 %finish.1 = (f32[64,256]{1,0:T(8,128)}, f32[64,256]{1,0:T(8,128)}, f32[64,256]{1,0:T(8,128)}) custom-call(s32[6]{0:T(128)S(1)} %stack.31.scalars, f32[64,256]{1,0:T(8,128)S(1)} %bitcast.41, f32[64,256]{1,0:T(8,128)S(1)} %bitcast.43, f32[64,256]{1,0:T(8,128)S(1)} %bitcast.45, f32[256,128]{1,0:T(8,128)S(1)} %bitcast.37), custom_call_target="tpu_custom_call" | custom-call | flops 100000000 | bytes 1000000 | tf_op jit(solution)/shard_map/finish/pallas_call | solution.py:386
  82.1 7.2 %all-to-all-done.3 = f32[32,8,128]{2,1,0:T(8,128)S(1)} async-done(((f32[32,8,128]{2,1,0:T(8,128)}), f32[32,8,128]{2,1,0:T(8,128)S(1)}, u32[]{:S(2)}, u32[]{:S(2)}) %all-to-all-start.3) | async-done | bytes 131104 | tf_op jit(solution)/shard_map/all_to_all | solution.py:497
  89.3 0.7 last.1
  (30 shorter events, 0.2 us)
Async XLA Ops:
  0.6 0.9 %copy-start.26 = (f32[1,64,256]{2,1,0:T(8,128)S(1)}, f32[1,64,256]{2,1,0:T(8,128)}, u32[]{:S(2)}) copy-start(f32[1,64,256]{2,1,0:T(8,128)} %param.30) | copy-start | bytes 196612
  1.4 0.8 copy-start.24
  1.4 0.9 copy-start.25
  2.2 30.1 %copy-start.14 = (f32[64,256]{1,0:T(8,128)S(1)}, f32[64,256]{1,0:T(8,128)}, u32[]{:S(2)}) copy-start(f32[64,256]{1,0:T(8,128)} %constant.213.clone.twist_sin) | copy-start | bytes 196612
  2.2 30.1 %copy-start.15 = (f32[64,256]{1,0:T(8,128)S(1)}, f32[64,256]{1,0:T(8,128)}, u32[]{:S(2)}) copy-start(f32[64,256]{1,0:T(8,128)} %constant.212.clone.twist_cos) | copy-start | bytes 196612
  3.7 28.6 %copy-start.6 = (bf16[256,512]{1,0:T(8,128)(2,1)S(1)}, bf16[256,512]{1,0:T(8,128)(2,1)}, u32[]{:S(2)}) copy-start(bf16[256,512]{1,0:T(8,128)(2,1)} %constant.211.clone.blocks_l) | copy-start | bytes 786436
  3.8 28.6 %copy-start.7 = (bf16[256,512]{1,0:T(8,128)(2,1)S(1)}, bf16[256,512]{1,0:T(8,128)(2,1)}, u32[]{:S(2)}) copy-start(bf16[256,512]{1,0:T(8,128)(2,1)} %constant.210.clone.blocks_h) | copy-start | bytes 786436
  3.8 28.6 %all-to-all-start = ((f32[256,1,128]{2,1,0:T(1,128)}), f32[256,1,128]{2,1,0:T(1,128)S(1)}, u32[]{:S(2)}, u32[]{:S(2)}) async-start(f32[256,1,128]{2,1,0:T(1,128)} %bitcast.11), calls=%async_computation | async-start | bytes 262144 | tf_op jit(solution)/shard_map/all_to_all | solution.py:454
  19.5 12.9 %copy-start.23 = (bf16[80,128]{1,0:T(8,128)(2,1)S(1)}, bf16[80,128]{1,0:T(8,128)(2,1)}, u32[]{:S(2)}) copy-start(bf16[80,128]{1,0:T(8,128)(2,1)} %constant.214.clone.inner_h) | copy-start | bytes 61444
  19.5 12.9 %copy-start.22 = (bf16[80,128]{1,0:T(8,128)(2,1)S(1)}, bf16[80,128]{1,0:T(8,128)(2,1)}, u32[]{:S(2)}) copy-start(bf16[80,128]{1,0:T(8,128)(2,1)} %constant.215.clone.inner_l) | copy-start | bytes 61444
  32.4 20.9 %copy-start.5 = (bf16[512,256]{1,0:T(8,128)(2,1)S(1)}, bf16[512,256]{1,0:T(8,128)(2,1)}, u32[]{:S(2)}) copy-start(bf16[512,256]{1,0:T(8,128)(2,1)} %constant.216.clone.groups_h) | copy-start | bytes 786436
  32.4 20.9 %copy-start.11 = (f32[256,128]{1,0:T(8,128)S(1)}, f32[256,128]{1,0:T(8,128)}, u32[]{:S(2)}) copy-start(f32[256,128]{1,0:T(8,128)} %constant.226.clone.return_cos) | copy-start | bytes 393220
  32.4 20.9 %copy-start.12 = (f32[256,128]{1,0:T(8,128)S(1)}, f32[256,128]{1,0:T(8,128)}, u32[]{:S(2)}) copy-start(f32[256,128]{1,0:T(8,128)} %constant.219.clone.radial_sin) | copy-start | bytes 393220
  32.4 20.9 %copy-start.13 = (f32[256,128]{1,0:T(8,128)S(1)}, f32[256,128]{1,0:T(8,128)}, u32[]{:S(2)}) copy-start(f32[256,128]{1,0:T(8,128)} %constant.218.clone.radial_cos) | copy-start | bytes 393220
  32.5 20.9 %copy-start.16 = (bf16[128,128]{1,0:T(8,128)(2,1)S(1)}, bf16[128,128]{1,0:T(8,128)(2,1)}, u32[]{:S(2)}) copy-start(bf16[128,128]{1,0:T(8,128)(2,1)} %constant.223.clone.cells_back_l) | copy-start | bytes 98308
  32.5 20.8 %copy-start.17 = (bf16[128,128]{1,0:T(8,128)(2,1)S(1)}, bf16[128,128]{1,0:T(8,128)(2,1)}, u32[]{:S(2)}) copy-start(bf16[128,128]{1,0:T(8,128)(2,1)} %constant.222.clone.cells_back_h) | copy-start | bytes 98308
  32.5 20.8 %copy-start.18 = (bf16[128,128]{1,0:T(8,128)(2,1)S(1)}, bf16[128,128]{1,0:T(8,128)(2,1)}, u32[]{:S(2)}) copy-start(bf16[128,128]{1,0:T(8,128)(2,1)} %constant.221.clone.cells_l) | copy-start | bytes 98308
  32.5 20.8 %copy-start.19 = (bf16[128,128]{1,0:T(8,128)(2,1)S(1)}, bf16[128,128]{1,0:T(8,128)(2,1)}, u32[]{:S(2)}) copy-start(bf16[128,128]{1,0:T(8,128)(2,1)} %constant.220.clone.cells_h) | copy-start | bytes 98308
  34.5 18.9 %copy-start.4 = (bf16[512,256]{1,0:T(8,128)(2,1)S(1)}, bf16[512,256]{1,0:T(8,128)(2,1)}, u32[]{:S(2)}) copy-start(bf16[512,256]{1,0:T(8,128)(2,1)} %constant.217.clone.groups_l) | copy-start | bytes 786436
  34.5 18.8 %all-to-all-start.1 = ((f32[256,1,128]{2,1,0:T(1,128)}), f32[256,1,128]{2,1,0:T(1,128)S(1)}, u32[]{:S(2)}, u32[]{:S(2)}) async-start(f32[256,1,128]{2,1,0:T(1,128)} %bitcast.14), calls=%async_computation.1 | async-start | bytes 262144 | tf_op jit(solution)/shard_map/all_to_all | solution.py:467
  40.2 13.1 %copy-start.2 = (bf16[512,256]{1,0:T(8,128)(2,1)S(1)}, bf16[512,256]{1,0:T(8,128)(2,1)}, u32[]{:S(2)}) copy-start(bf16[512,256]{1,0:T(8,128)(2,1)} %constant.225.clone.groups_back_l) | copy-start | bytes 786436
  40.2 13.1 %copy-start.3 = (bf16[512,256]{1,0:T(8,128)(2,1)S(1)}, bf16[512,256]{1,0:T(8,128)(2,1)}, u32[]{:S(2)}) copy-start(bf16[512,256]{1,0:T(8,128)(2,1)} %constant.224.clone.groups_back_h) | copy-start | bytes 786436
  40.2 13.1 %copy-start.10 = (f32[256,128]{1,0:T(8,128)S(1)}, f32[256,128]{1,0:T(8,128)}, u32[]{:S(2)}) copy-start(f32[256,128]{1,0:T(8,128)} %constant.227.clone.return_sin) | copy-start | bytes 393220
  53.4 21.5 %copy-start.1 = (bf16[256,512]{1,0:T(8,128)(2,1)S(1)}, bf16[256,512]{1,0:T(8,128)(2,1)}, u32[]{:S(2)}) copy-start(bf16[256,512]{1,0:T(8,128)(2,1)} %constant.232.clone.blocks_h) | copy-start | bytes 786436
  53.4 21.5 %copy-start.8 = (f32[64,512]{1,0:T(8,128)S(1)}, f32[64,512]{1,0:T(8,128)}, u32[]{:S(2)}) copy-start(f32[64,512]{1,0:T(8,128)} %constant.231.clone.back_sin) | copy-start | bytes 393220
  53.4 21.5 %copy-start.9 = (f32[64,512]{1,0:T(8,128)S(1)}, f32[64,512]{1,0:T(8,128)}, u32[]{:S(2)}) copy-start(f32[64,512]{1,0:T(8,128)} %constant.230.clone.back_cos) | copy-start | bytes 393220
  53.4 21.5 %copy-start.20 = (bf16[128,32]{1,0:T(8,128)(2,1)S(1)}, bf16[128,32]{1,0:T(8,128)(2,1)}, u32[]{:S(2)}) copy-start(bf16[128,32]{1,0:T(8,128)(2,1)} %constant.229.clone.inner_l) | copy-start | bytes 24580
  53.4 21.5 %copy-start.21 = (bf16[128,32]{1,0:T(8,128)(2,1)S(1)}, bf16[128,32]{1,0:T(8,128)(2,1)}, u32[]{:S(2)}) copy-start(bf16[128,32]{1,0:T(8,128)(2,1)} %constant.228.clone.inner_h) | copy-start | bytes 24580
  56.3 18.6 %copy-start = (bf16[256,512]{1,0:T(8,128)(2,1)S(1)}, bf16[256,512]{1,0:T(8,128)(2,1)}, u32[]{:S(2)}) copy-start(bf16[256,512]{1,0:T(8,128)(2,1)} %constant.233.clone.blocks_l) | copy-start | bytes 786436
  76.4 12.9 %all-to-all-start.3 = ((f32[32,8,128]{2,1,0:T(8,128)}), f32[32,8,128]{2,1,0:T(8,128)S(1)}, u32[]{:S(2)}, u32[]{:S(2)}) async-start(f32[32,8,128]{2,1,0:T(8,128)} %bitcast.22), calls=%async_computation.3 | async-start | bytes 262144 | tf_op jit(solution)/shard_map/all_to_all | solution.py:497
where the time goes:
time: 90.4 us; the launch traced here: 90.1 us
  waiting for transfers between devices  31.7 us (35%)
  starting transfers between devices  25.5 us (28%)
  blocking collectives  18.5 us (20%)
  Pallas kernels  10.2 us (11%)
  between operations  1.82 us (2%)
  other arithmetic  1.39 us (2%)
  local copies, waits for them, and re-layouts  0.94 us (1%)
    all_to_all x1, blocking collectives, shards(): solved = lax.all_to_all(solved, everyone, 0, 0, tiled=True)  18.5 us
    all_to_all x1, starting transfers between devices, shards(): columns = lax.all_to_all(columns, everyone, 0, 0, tiled=True)  15.7 us
    all_to_all x1, waiting for transfers between devices, shards(): columns = lax.all_to_all(columns, everyone, 0, 0, tiled=True)  12.7 us
    all_to_all x1, waiting for transfers between devices, shards(): waves = lax.all_to_all(waves, everyone, 0, 0, tiled=True)  11.8 us
    pallas_call x6, Pallas kernels, call(): pl.pallas_call(kernel, out_shape=outs if many else outs[0], in_specs=[SME...  10.2 us
    all_to_all x1, waiting for transfers between devices, shards(): lines = lax.all_to_all(lines, 'gy', 0, 0, tiled=True)  7.21 us
    all_to_all x1, starting transfers between devices, shards(): waves = lax.all_to_all(waves, everyone, 0, 0, tiled=True)  5.71 us
    all_to_all x1, starting transfers between devices, shards(): lines = lax.all_to_all(lines, 'gy', 0, 0, tiled=True)  4.11 us
  transfers between devices with their start and end apart: 3, of which 3 were waited for; matrix products, arithmetic and copies ran while one was open for 2% of the time, Pallas kernels for 2%

commit v1 on v0

--- a/solution.py
+++ b/solution.py
@@ -32,6 +32,11 @@
     return head, rest
 
 
+def both_parts(table):
+    head, rest = halves(table)
+    return np.block([[head, rest], [head, np.zeros_like(rest)]])
+
+
 def turn(index, length):
     angle = 2.0 * np.pi * (np.asarray(index) % length) / length
     return np.cos(angle), np.sin(angle)
@@ -54,9 +59,10 @@
     c64, s64 = turn(np.outer(np.arange(32), np.arange(64)), 64)
     last = np.zeros((16, 128))
     last[0, :64] = 1.0 - 2.0 * (np.arange(64) % 2)
-    out["inner"] = halves(
+    head, rest = halves(
         np.concatenate([np.concatenate([c64, s64], 1), np.concatenate([-s64, c64], 1), last])
     )
+    out["inner"] = np.concatenate([head, head], 1), rest
     rows = np.arange(256)
     c256, s256 = turn(np.outer(rows, rows), 256)
     out["groups"] = halves(np.concatenate([c256, s256]))
@@ -68,16 +74,17 @@
     c8, s8 = turn(np.outer(np.arange(8), np.arange(8)), 8)
     lines = np.eye(8)
     ck, sk = np.kron(lines, c8), np.kron(lines, s8)
-    out["cells"] = halves(np.block([[ck, -sk], [sk, ck]]))
-    out["cells_back"] = halves(np.block([[ck, sk], [-sk, ck]]))
-    order = rows // 32 + 8 * (rows % 32)
-    c256, s256 = turn(np.outer(rows, order), 256)
+    out["cells"] = both_parts(np.block([[ck, -sk], [sk, ck]]))
+    out["cells_back"] = both_parts(np.block([[ck, sk], [-sk, ck]]))
+    order = rows // 128 * 128 + rows // 32 % 4 + 4 * (rows % 32)
+    c256, s256 = turn(np.outer(order, rows), 256)
     out["groups_back"] = halves(np.concatenate([c256, s256]))
     tc, ts = turn(np.outer(order, lane % 8), NX)
     out["return_cos"] = tc.astype(np.float32)
     out["return_sin"] = (ts * sign).astype(np.float32)
     c64, s64 = turn(np.outer(np.arange(64), np.arange(32)), 64)
-    out["inner_back"] = halves(np.concatenate([c64, s64]))
+    head, rest = halves(np.concatenate([c64, s64]))
+    out["inner_back"] = np.concatenate([head, head, rest], 1)
     pair = np.arange(512) // 128
     part = np.arange(512) % 128 // 64
     which = np.arange(512) % 64 // 8
@@ -86,8 +93,8 @@
     tc, ts = turn(np.outer(np.arange(64), m1), NY)
     out["back_cos"] = tc.astype(np.float32)
     out["back_sin"] = (ts * np.where(part == 0, 1.0, -1.0)).astype(np.float32)
-    j = np.repeat(np.arange(32), 8)
-    own = np.tile(np.arange(8), 32)
+    j = np.tile(np.repeat(np.arange(32), 4), 2)
+    own = np.repeat([0, 4], 128) + np.tile(np.arange(4), 64)
     c32, s32 = turn(np.outer(j, m1), 32)
     weight = np.where(part == 0, c32, -s32)
     weight = np.where((part == 1) & (m1 == 0), 1.0, weight)
@@ -105,15 +112,23 @@
 NT = (((1,), (1,)), ((), ()))
 
 
-def product(table_head, table_rest, value, dims=NN):
+def dot(left, right, dims=NN):
+    return lax.dot_general(left, right, dims, preferred_element_type=F32)
+
+
+def product_rows(table_head, table_rest, value):
     head, rest = split(value)
-    dot = functools.partial(lax.dot_general, dimension_numbers=dims, preferred_element_type=F32)
-    return dot(table_head, head) + (dot(table_head, rest) + dot(table_rest, head))
+    both = dot(table_head, jnp.concatenate([head, rest], 1))
+    return both[:, :128] + both[:, 128:] + dot(table_rest, head)
+
+
+def product_lanes(value, table):
+    both = dot(jnp.concatenate(split(value), 1), table)
+    return both[:, :128] + both[:, 128:]
 
 
 def product_right(value, table_head, table_rest):
     head, rest = split(value)
-    dot = functools.partial(lax.dot_general, dimension_numbers=NN, preferred_element_type=F32)
     return dot(head, table_head) + (dot(rest, table_head) + dot(head, table_rest))
 
 
@@ -156,8 +171,17 @@
     return [jnp.where(lane == 0, 0.0, v) for v in west], [jnp.where(row == 0, 0.0, v) for v in south]
 
 
-def pack_kernel(scalars, rho, mx, my, out):
-    state = (rho[...], mx[...], my[...])
+def pack_kernel(place, shift, rho, mx, my, out, held, shift_held, ready):
+    copies = [
+        pltpu.make_async_copy(source, held.at[f], ready.at[f])
+        for f, source in enumerate((rho, mx, my))
+    ]
+    copies.append(pltpu.make_async_copy(shift, shift_held, ready.at[3]))
+    for copy in copies:
+        copy.start()
+    for copy in copies:
+        copy.wait()
+    state = (held[0], held[1], held[2])
     (west,), (south,) = inner_fluxes(state, 1)
     change = roll(west, -1, 1) - west + roll(south, -1, 0) - south
     partial = state[0] - time_step * change
@@ -173,7 +197,8 @@
     for f in range(3):
         low = jnp.where(lane == 72 + f, state[f][:, 0:1], low)
         high = jnp.where(lane == 75 + f, state[f][:, COLS - 1 : COLS], high)
-    out[0:ROWS, :] = tall[0:ROWS] + low + pltpu.roll(high, scalars[0], 0)
+    slide = jnp.where(place[0] == GX - 1, (ROWS - (shift_held[0] & (ROWS - 1))) & (ROWS - 1), 0)
+    out[0:ROWS, :] = tall[0:ROWS] + low + pltpu.roll(high, slide, 0)
     out[ROWS:, :] = tall[ROWS:]
 
 
@@ -197,9 +222,7 @@
     my_out[...] = new[2] - time_step * (2.0 - shear_rate) * omega_rate * state[1]
 
 
-def forward_kernel(
-    scalars, arrived, blocks_h, blocks_l, twist_cos, twist_sin, inner_h, inner_l, out, ride
-):
+def edge_fluxes(scalars, arrived, parts):
     row = scalars[4]
     narrow = lanes_of((32, 128))
     last = arrived[224:256, :]
@@ -213,6 +236,7 @@
         with_speed([before[3 + f : 4 + f] for f in range(3)], 2),
         with_speed([upper[f : f + 1] for f in range(3)], 2),
         2,
+        parts,
     )
     valid = jnp.zeros((1, 256), jnp.int32) + row >= 0
     side = tall[72:80]
@@ -221,14 +245,18 @@
     right = [side[f : f + 1] for f in range(3)]
     left[0] = jnp.where(valid, left[0], 1.0)
     right[0] = jnp.where(valid, right[0], 1.0)
-    west = interface(with_speed(left, 1), with_speed(right, 1), 1)
+    west = interface(with_speed(left, 1), with_speed(right, 1), 1, parts)
     west = [jnp.where(valid, v, 0.0) for v in west]
     line = lanes_of((1, 256))
     north = [jnp.where(line % 32 == 31, roll(v, 31, 1), roll(v, -1, 1)) for v in south]
+    return tall, west, south, north
+
+
+def edges_kernel(scalars, arrived, ride):
+    _, west, south, north = edge_fluxes(scalars, arrived, 3)
     east = [roll(v, -32, 1) for v in west]
-    rows8 = rows_of((8, 256))
+    narrow = lanes_of((32, 128))
     rows16 = rows_of((16, 256))
-    rows64 = rows_of((64, 256))
     fluxes = jnp.zeros((16, 256), F32)
     for at, value in enumerate(south + north + west + east):
         fluxes = jnp.where(rows16 == at, value, fluxes)
@@ -237,6 +265,13 @@
     wrapped = pltpu.roll(last, scalars[3], 0)
     ride[0:224, :] = back[0:224]
     ride[224:256, :] = jnp.where((narrow >= 41) & (narrow < 44), wrapped, last)
+
+
+def forward_kernel(scalars, arrived, blocks_h, blocks_l, twist_cos, twist_sin, inner_h, inner_l, out):
+    tall, west, south, north = edge_fluxes(scalars, arrived, 1)
+    narrow = lanes_of((32, 128))
+    rows8 = rows_of((8, 256))
+    rows64 = rows_of((64, 256))
     density = tall[0:64]
     density = density + jnp.where(rows64 == 0, time_step * south[0], 0.0)
     density = density - jnp.where(rows64 == 63, time_step * north[0], 0.0)
@@ -247,11 +282,12 @@
     re, im = first[:64, :256], first[:64, 256:]
     main = jnp.concatenate([re * tc + im * ts, im * tc - re * ts], 0)
     re, im = first[64:65, :256], first[64:65, 256:]
-    here = rows64 == row
+    here = rows64 == scalars[4]
     edge = jnp.concatenate(
         [jnp.where(here, re * tc + im * ts, 0.0), jnp.where(here, im * tc - re * ts, 0.0)], 0
     )
-    waves = product(inner_h[...], inner_l[...], jnp.concatenate([main, edge], 1))
+    head, rest = split(jnp.concatenate([main, edge], 1))
+    waves = dot(inner_h[...], jnp.concatenate([head, rest], 0)) + dot(inner_l[...], head)
     rows32 = rows_of((32, 128))
     for g in range(8):
         place = 32 * (g % 4)
@@ -285,10 +321,8 @@
     groups_l,
     radial_cos,
     radial_sin,
-    cells_h,
-    cells_l,
-    cells_back_h,
-    cells_back_l,
+    cells,
+    cells_back,
     groups_back_h,
     groups_back_l,
     return_cos,
@@ -318,11 +352,18 @@
     value = apart(value)
     value = value + jnp.where(row == 0, edge[0:1], 0.0) - jnp.where(row == 255, beside[0:1], 0.0)
     value = value * theta_cos[...] + half(value) * theta_sin[...]
-    value = product_right(value, cells_h[...], cells_l[...])
+    value = product_lanes(value, cells[...])
     value = value * radial_cos[...] + half(value) * radial_sin[...]
-    both = product(groups_h[...], groups_l[...], value)
+    both = product_rows(groups_h[...], groups_l[...], value)
     value = both[:256] + sign * half(both[256:])
     value = value * weights[...]
+    both = product_rows(groups_back_h[...], groups_back_l[...], value)
+    value = both[:256] - sign * half(both[256:])
+    value = value * return_cos[...] - half(value) * return_sin[...]
+    value = product_lanes(value, cells_back[...])
+    value = value * theta_cos_back[...] - half(value) * theta_sin_back[...]
+    first = jnp.zeros(shape, jnp.int32) + scalars[5] == 1
+    value = jnp.where((lane >= 64) & (lane < 72) & first, roll(value, 32, 1), value)
     blocks = [value[32 * k : 32 * k + 32] for k in range(8)]
     narrow = lanes_of((32, 128))
     for bit in (1, 2, 4):
@@ -335,17 +376,10 @@
                 swapped[k + bit] = jnp.where(low, roll(a, -bit, 1), b)
         blocks = swapped
     value = jnp.concatenate(blocks, 0)
-    value = product_right(value, cells_back_h[...], cells_back_l[...])
-    value = value * return_cos[...] - half(value) * return_sin[...]
-    both = product(groups_back_h[...], groups_back_l[...], value)
-    value = both[:256] - sign * half(both[256:])
-    value = value * theta_cos_back[...] - half(value) * theta_sin_back[...]
-    first = jnp.zeros(shape, jnp.int32) + scalars[5] == 1
-    value = jnp.where((lane >= 64) & (lane < 72) & first, roll(value, 32, 1), value)
     out[...] = jnp.where((lane >= 32) & (lane < 44), ride[...], value)
 
 
-def backward_kernel(arrived, inner_h, inner_l, back_cos, back_sin, blocks_h, blocks_l, out):
+def backward_kernel(arrived, inner, back_cos, back_sin, blocks_h, blocks_l, out):
     lane = lanes_of((32, 128))
     low = lane % 64 < 32
     pairs = []
@@ -354,7 +388,8 @@
         odd = arrived[64 * h + 32 : 64 * h + 64, :]
         pairs.append(jnp.where(low, even, roll(odd, 32, 1)))
     value = jnp.concatenate(pairs, 1)
-    both = product(inner_h[...], inner_l[...], value)
+    head, rest = split(value)
+    both = dot(inner[...], jnp.concatenate([head, rest, head], 0))
     wide = lanes_of((64, 128))
     row = rows_of((64, 128))
     sign = jnp.where(wide < 64, 1.0, -1.0)
@@ -367,29 +402,36 @@
         if h == 0:
             part = jnp.where((wide >= 64) & (wide < 72), parity * pairs[0][0:1, :], part)
         turned.append(part)
-    turned = jnp.concatenate(turned, 1)
-    turned = jnp.concatenate([turned, turned], 0)
-    out[...] = product(blocks_h[...], blocks_l[...], turned, NT)
+    head, rest = split(jnp.concatenate(turned, 1))
+    full = dot(blocks_h[...], jnp.concatenate([head, rest], 0), NT)
+    full = full + roll(full, 64, 1)
+    full = full + dot(blocks_l[...], jnp.concatenate([head, head], 0), NT)
+    square = lanes_of((128, 128))
+    out[...] = jnp.where(square < 64, full[:128], full[128:])
 
 
 def last_kernel(arrived, out):
-    out[...] = arrived[...].T[:ROWS]
+    tall = arrived[...].T
+    out[:, :128] = tall[:ROWS]
+    out[:, 128:] = tall[ROWS:]
 
 
 VMEM = pl.BlockSpec(memory_space=pltpu.VMEM)
 SMEM = pl.BlockSpec(memory_space=pltpu.SMEM)
-
-
-def call(kernel, shapes, *args, name, smem=0):
+HBM = pl.BlockSpec(memory_space=pltpu.HBM)
+
+
+def call(kernel, shapes, *args, name, smem=0, hbm=0, scratch=(), room=32):
     many = isinstance(shapes, list)
     outs = [jax.ShapeDtypeStruct(s, F32) for s in (shapes if many else [shapes])]
     return pl.pallas_call(
         kernel,
         out_shape=outs if many else outs[0],
-        in_specs=[SMEM] * smem + [VMEM] * (len(args) - smem),
+        in_specs=[SMEM] * smem + [HBM] * hbm + [VMEM] * (len(args) - smem - hbm),
         out_specs=[VMEM] * len(outs) if many else VMEM,
+        scratch_shapes=scratch,
         name=name,
-        compiler_params=pltpu.CompilerParams(vmem_limit_bytes=32 * 1024 * 1024),
+        compiler_params=pltpu.CompilerParams(vmem_limit_bytes=room * 1024 * 1024),
         cost_estimate=pl.CostEstimate(flops=100_000_000, bytes_accessed=1_000_000, transcendentals=0),
     )(*args)
 
@@ -410,7 +452,7 @@
         return jnp.cos(angle), jnp.sin(angle) * sign
 
     there = phase(row + COLS * inside)
-    back = phase(row * 8 + inside)
+    back = phase(row // 128 * 128 + row // 32 % 4 + 4 * (row % 32) + COLS * inside)
     n = inside + 8 * row
     n = jnp.where(n < NX // 2, n, n - NX)
     kx = 2.0 * jnp.pi / NX * (n.astype(F32) + sigma.astype(F32) / NY)
@@ -450,11 +492,29 @@
     everyone = ("gx", "gy")
     block = (ROWS, COLS)
     table = (256, 128)
-    columns = call(pack_kernel, table, scalars, rho, mx, my, name="pack", smem=1)
+    place = radial.astype(jnp.int32).reshape(1)
+    columns = call(
+        pack_kernel,
+        table,
+        place,
+        shear_shift,
+        rho,
+        mx,
+        my,
+        name="pack",
+        smem=1,
+        hbm=4,
+        room=62,
+        scratch=(
+            pltpu.VMEM((3, *block), F32),
+            pltpu.SMEM((1,), jnp.int32),
+            pltpu.SemaphoreType.DMA((4,)),
+        ),
+    )
     columns = lax.all_to_all(columns, everyone, 0, 0, tiled=True)
-    waves, ride = call(
+    waves = call(
         forward_kernel,
-        [table, table],
+        table,
         scalars,
         columns,
         *t["blocks"],
@@ -465,6 +525,7 @@
         smem=1,
     )
     waves = lax.all_to_all(waves, everyone, 0, 0, tiled=True)
+    ride = call(edges_kernel, table, scalars, columns, name="edges", smem=1)
     solved = call(
         radial_kernel,
         table,
@@ -475,8 +536,8 @@
         *t["groups"],
         t["radial_cos"],
         t["radial_sin"],
-        *t["cells"],
-        *t["cells_back"],
+        t["cells"],
+        t["cells_back"],
         *t["groups_back"],
         t["return_cos"],
         t["return_sin"],
@@ -486,9 +547,9 @@
     solved = lax.all_to_all(solved, everyone, 0, 0, tiled=True)
     lines = call(
         backward_kernel,
-        table,
+        (128, 128),
         solved,
-        *t["inner_back"],
+        t["inner_back"],
         t["back_cos"],
         t["back_sin"],
         *t["blocks_back"],

time: 90.4 us -> 88.5 us (0.979)
  waiting for transfers between devices: 31.7 us -> 28.9 us
    mul x1 -> x2, other arithmetic: 0.01 us -> 1.2 us  [the longest x1 1.2 us: phase(): return (jnp.cos(angle), jnp.sin(angle) * sign)]
    all_to_all x1, waiting for transfers between devices: 12.7 us -> 11.8 us  [shards(): columns = lax.all_to_all(columns, everyone, 0, 0, tiled=True)]
    all_to_all x1, waiting for transfers between devices: 7.21 us -> 6.27 us  [shards(): lines = lax.all_to_all(lines, 'gy', 0, 0, tiled=True)]
    pallas_call x6 -> x7, Pallas kernels: 10.2 us -> 10.9 us  [call(): pl.pallas_call(kernel, out_shape=outs if many else outs[0], in_specs=[SME...]
  transfers between devices with their start and end apart: 3 -> 3, of which waited for: 3 -> 3; matrix products, arithmetic and copies ran while one was open for 2% -> 2% of each run, Pallas kernels for 2% -> 3%
where the time goes in v1:
time: 88.5 us; the launch traced here: 88.2 us
  waiting for transfers between devices  28.9 us (33%)
  starting transfers between devices  25.7 us (29%)
  blocking collectives  18.5 us (21%)
  Pallas kernels  10.9 us (12%)
  other arithmetic  2.03 us (2%)
  between operations  1.84 us (2%)
    all_to_all x1, blocking collectives, shards(): solved = lax.all_to_all(solved, everyone, 0, 0, tiled=True)  18.5 us
    all_to_all x1, starting transfers between devices, shards(): columns = lax.all_to_all(columns, everyone, 0, 0, tiled=True)  15.7 us
    all_to_all x1, waiting for transfers between devices, shards(): columns = lax.all_to_all(columns, everyone, 0, 0, tiled=True)  11.8 us
    all_to_all x1, waiting for transfers between devices, shards(): waves = lax.all_to_all(waves, everyone, 0, 0, tiled=True)  10.9 us
    pallas_call x7, Pallas kernels, call(): pl.pallas_call(kernel, out_shape=outs if many else outs[0], in_specs=[SME...  10.9 us
    all_to_all x1, waiting for transfers between devices, shards(): lines = lax.all_to_all(lines, 'gy', 0, 0, tiled=True)  6.27 us
    all_to_all x1, starting transfers between devices, shards(): waves = lax.all_to_all(waves, everyone, 0, 0, tiled=True)  5.76 us
    all_to_all x1, starting transfers between devices, shards(): lines = lax.all_to_all(lines, 'gy', 0, 0, tiled=True)  4.26 us
  transfers between devices with their start and end apart: 3, of which 3 were waited for; matrix products, arithmetic and copies ran while one was open for 2% of the time, Pallas kernels for 3%

profile of v1, /device:TPU:1, one launch (start us, length us, event | category | flops | bytes accessed | tf_op | source)
XLA Modules:
  0.0 88.2 jit_solution(4668305329967445712)
XLA Ops:
  1.3 1.9 %pack.1 = f32[256,128]{1,0:T(8,128)} custom-call(s32[1]{0:T(128)} %bitcast.10.place, s32[1]{0:T(128)} %copy.32.shift, f32[64,256]{1,0:T(8,128)} %bitcast.43, f32[64,256]{1,0:T(8,128)} %bitcast.45, f32[64,256]{1,0:T(8,128)} %bitcast.47), custom_call_target="tpu_custom_call" | custom-call | flops 100000000 | bytes 1000000 | tf_op jit(solution)/shard_map/pack/pallas_call | solution.py:427
  3.2 15.7 %all-to-all-start = ((f32[256,1,128]{2,1,0:T(1,128)}), f32[256,1,128]{2,1,0:T(1,128)S(1)}, u32[]{:S(2)}, u32[]{:S(2)}) async-start(f32[256,1,128]{2,1,0:T(1,128)} %bitcast.49), calls=%async_computation | async-start | bytes 262144 | tf_op jit(solution)/shard_map/all_to_all | solution.py:514
  19.0 0.0 copy-start.17
  19.0 0.0 copy-start.20
  19.0 0.0 copy-start.5
  19.1 0.0 copy-start.4
  19.3 0.1 stack.31.scalars
  19.4 0.7 multiply_multiply_fusion
  20.1 11.8 %all-to-all-done = f32[256,1,128]{2,1,0:T(1,128)S(1)} async-done(((f32[256,1,128]{2,1,0:T(1,128)}), f32[256,1,128]{2,1,0:T(1,128)S(1)}, u32[]{:S(2)}, u32[]{:S(2)}) %all-to-all-start) | async-done | bytes 131104 | tf_op jit(solution)/shard_map/all_to_all | solution.py:514
  31.8 0.0 copy-done.17
  31.8 0.0 copy-done.20
  31.8 0.0 copy-done.5
  31.8 0.0 copy-done.4
  31.9 0.0 copy-start.8
  31.9 0.0 copy-start.9
  31.9 0.0 copy-start.10
  31.9 0.0 copy-start.11
  31.9 0.0 copy-start.12
  31.9 0.0 copy-start.13
  31.9 2.0 %forward.1 = f32[256,128]{1,0:T(8,128)} custom-call(s32[6]{0:T(128)S(1)} %stack.31.scalars, f32[256,128]{1,0:T(8,128)S(1)} %bitcast.36, bf16[256,512]{1,0:T(8,128)(2,1)S(1)} %copy-done.5, bf16[256,512]{1,0:T(8,128)(2,1)S(1)} %copy-done.4, f32[64,256]{1,0:T(8,128)S(1)} %copy-done.17, f32[64,256]{1,0:T(8,128)S(1)} %copy-done.16, ...), custom_call_target="tpu_custom_call" | custom-call | flops 100000000 | bytes 1000000 | tf_op jit(solution)/shard_map/forward/pallas_call | solution.py:427
  33.9 5.8 %all-to-all-start.1 = ((f32[256,1,128]{2,1,0:T(1,128)}), f32[256,1,128]{2,1,0:T(1,128)S(1)}, u32[]{:S(2)}, u32[]{:S(2)}) async-start(f32[256,1,128]{2,1,0:T(1,128)} %bitcast.15), calls=%async_computation.1 | async-start | bytes 262144 | tf_op jit(solution)/shard_map/all_to_all | solution.py:527
  39.7 0.0 copy-start.1
  39.7 0.0 copy-start.2
  39.7 1.2 %sine_multiply_fusion = (f32[256,128]{1,0:T(8,128)S(1)}, f32[256,128]{1,0:T(8,128)S(1)}, f32[256,128]{1,0:T(8,128)S(1)}) fusion(f32[128]{0:T(128)S(1)} %compare_select_fusion.1, s32[128]{0:T(128)S(1)} %get-tuple-element.19, s32[128]{0:T(128)S(1)} %get-tuple-element.21, pred[128]{0:T(512)(128)(4,1)S(1)} %get-tuple-element.17, s32[256]{0:T(256)S(1)} %get-tuple-element.24, ...), kind=kLoop, calls=%fused_computation.39 | loop fusion | flops 2752512 | bytes 402956 | tf_op jit(solution)/shard_map/mul | solution.py:452
  40.9 0.0 copy-start
  41.0 0.9 %edges.1.ride = f32[256,128]{1,0:T(8,128)S(1)} custom-call(s32[6]{0:T(128)S(1)} %stack.31.scalars, f32[256,128]{1,0:T(8,128)S(1)} %bitcast.37), custom_call_target="tpu_custom_call" | custom-call | flops 100000000 | bytes 1000000 | tf_op jit(solution)/shard_map/edges/pallas_call | solution.py:427
  41.8 10.9 %all-to-all-done.1 = f32[256,1,128]{2,1,0:T(1,128)S(1)} async-done(((f32[256,1,128]{2,1,0:T(1,128)}), f32[256,1,128]{2,1,0:T(1,128)S(1)}, u32[]{:S(2)}, u32[]{:S(2)}) %all-to-all-start.1) | async-done | bytes 131104 | tf_op jit(solution)/shard_map/all_to_all | solution.py:527
  52.8 0.0 copy-done.11
  52.8 0.0 copy-done.12
  52.8 0.0 copy-done.13
  52.8 0.0 copy-done.3
  52.8 0.0 copy-done.1
  52.8 0.0 copy-done.2
  52.8 0.0 copy-done
  52.9 0.0 copy-start.7
  52.9 0.0 copy-start.14
  52.9 0.0 copy-start.15
  52.9 0.0 copy-start.19
  52.9 2.4 %radial.1 = f32[256,128]{1,0:T(8,128)S(1)} custom-call(s32[6]{0:T(128)S(1)} %stack.31.scalars, f32[256,128]{1,0:T(8,128)S(1)} %bitcast.38, f32[256,128]{1,0:T(8,128)S(1)} %edges.1.ride, f32[256,128]{1,0:T(8,128)S(1)} %get-tuple-element.16.theta_cos, f32[256,128]{1,0:T(8,128)S(1)} %get-tuple-element.14.theta_sin, ...), custom_call_target="tpu_custom_call" | custom-call | flops 100000000 | bytes 1000000 | tf_op jit(solution)/shard_map/radial/pallas_call | solution.py:427
  55.3 0.0 copy-start.6
  55.3 18.5 %all_to_all.44 = f32[256,1,128]{2,1,0:T(1,128)S(1)} all-to-all(f32[256,1,128]{2,1,0:T(1,128)S(1)} %bitcast.39), channel_id=1, replica_groups=mesh['gx'=8,'gy'=32] {'gx','gy'}, dimensions={0} | all-to-all | bytes 262144 | tf_op jit(solution)/shard_map/all_to_all | solution.py:547
  73.8 0.0 copy-done.15
  73.9 0.0 copy-start.23
  73.9 1.4 %backward.1 = f32[128,128]{1,0:T(8,128)} custom-call(f32[256,128]{1,0:T(8,128)S(1)} %bitcast.40, bf16[128,96]{1,0:T(8,128)(2,1)S(1)} %copy-done.19, f32[64,512]{1,0:T(8,128)S(1)} %copy-done.15, f32[64,512]{1,0:T(8,128)S(1)} %copy-done.14, bf16[256,512]{1,0:T(8,128)(2,1)S(1)} %copy-done.7, bf16[256,512]{1,0:T(8,128)(2,1)S(1)} %copy-done.6), custom_call_target="tpu_custom_call" | custom-call | flops 100000000 | bytes 1000000 | tf_op jit(solution)/shard_map/backward/pallas_call | solution.py:427
  75.3 4.3 %all-to-all-start.3 = ((f32[32,4,128]{2,1,0:T(4,128)}), f32[32,4,128]{2,1,0:T(4,128)S(1)}, u32[]{:S(2)}, u32[]{:S(2)}) async-start(f32[32,4,128]{2,1,0:T(4,128)} %bitcast.23), calls=%async_computation.3 | async-start | bytes 131072 | tf_op jit(solution)/shard_map/all_to_all | solution.py:558
  79.6 1.6 %finish.1 = (f32[64,256]{1,0:T(8,128)}, f32[64,256]{1,0:T(8,128)}, f32[64,256]{1,0:T(8,128)}) custom-call(s32[6]{0:T(128)S(1)} %stack.31.scalars, f32[64,256]{1,0:T(8,128)S(1)} %bitcast.44, f32[64,256]{1,0:T(8,128)S(1)} %bitcast.46, f32[64,256]{1,0:T(8,128)S(1)} %bitcast.48, f32[256,128]{1,0:T(8,128)S(1)} %bitcast.41), custom_call_target="tpu_custom_call" | custom-call | flops 100000000 | bytes 1000000 | tf_op jit(solution)/shard_map/finish/pallas_call | solution.py:427
  81.2 6.3 %all-to-all-done.3 = f32[32,4,128]{2,1,0:T(4,128)S(1)} async-done(((f32[32,4,128]{2,1,0:T(4,128)}), f32[32,4,128]{2,1,0:T(4,128)S(1)}, u32[]{:S(2)}, u32[]{:S(2)}) %all-to-all-start.3) | async-done | bytes 65568 | tf_op jit(solution)/shard_map/all_to_all | solution.py:558
  87.4 0.7 last.1
  (31 shorter events, 0.2 us)
Async XLA Ops:
  3.2 28.6 %all-to-all-start = ((f32[256,1,128]{2,1,0:T(1,128)}), f32[256,1,128]{2,1,0:T(1,128)S(1)}, u32[]{:S(2)}, u32[]{:S(2)}) async-start(f32[256,1,128]{2,1,0:T(1,128)} %bitcast.49), calls=%async_computation | async-start | bytes 262144 | tf_op jit(solution)/shard_map/all_to_all | solution.py:514
  19.0 12.8 %copy-start.17 = (f32[64,256]{1,0:T(8,128)S(1)}, f32[64,256]{1,0:T(8,128)}, u32[]{:S(2)}) copy-start(f32[64,256]{1,0:T(8,128)} %constant.245.clone.twist_cos) | copy-start | bytes 196612
  19.0 12.8 %copy-start.20 = (bf16[80,128]{1,0:T(8,128)(2,1)S(1)}, bf16[80,128]{1,0:T(8,128)(2,1)}, u32[]{:S(2)}) copy-start(bf16[80,128]{1,0:T(8,128)(2,1)} %constant.248.clone.inner_l) | copy-start | bytes 61444
  19.0 12.8 %copy-start.5 = (bf16[256,512]{1,0:T(8,128)(2,1)S(1)}, bf16[256,512]{1,0:T(8,128)(2,1)}, u32[]{:S(2)}) copy-start(bf16[256,512]{1,0:T(8,128)(2,1)} %constant.243.clone.blocks_h) | copy-start | bytes 786436
  19.1 12.8 %copy-start.4 = (bf16[256,512]{1,0:T(8,128)(2,1)S(1)}, bf16[256,512]{1,0:T(8,128)(2,1)}, u32[]{:S(2)}) copy-start(bf16[256,512]{1,0:T(8,128)(2,1)} %constant.244.clone.blocks_l) | copy-start | bytes 786436
  19.4 12.4 %copy-start.16 = (f32[64,256]{1,0:T(8,128)S(1)}, f32[64,256]{1,0:T(8,128)}, u32[]{:S(2)}) copy-start(f32[64,256]{1,0:T(8,128)} %constant.246.clone.twist_sin) | copy-start | bytes 196612
  19.4 12.4 %copy-start.18 = (bf16[80,256]{1,0:T(8,128)(2,1)S(1)}, bf16[80,256]{1,0:T(8,128)(2,1)}, u32[]{:S(2)}) copy-start(bf16[80,256]{1,0:T(8,128)(2,1)} %constant.247.clone.inner_h) | copy-start | bytes 122884
  31.9 20.9 %copy-start.8 = (f32[256,128]{1,0:T(8,128)S(1)}, f32[256,128]{1,0:T(8,128)}, u32[]{:S(2)}) copy-start(f32[256,128]{1,0:T(8,128)} %constant.258.clone.return_sin) | copy-start | bytes 393220
  31.9 20.9 %copy-start.9 = (f32[256,128]{1,0:T(8,128)S(1)}, f32[256,128]{1,0:T(8,128)}, u32[]{:S(2)}) copy-start(f32[256,128]{1,0:T(8,128)} %constant.257.clone.return_cos) | copy-start | bytes 393220
  31.9 20.9 %copy-start.10 = (bf16[256,256]{1,0:T(8,128)(2,1)S(1)}, bf16[256,256]{1,0:T(8,128)(2,1)}, u32[]{:S(2)}) copy-start(bf16[256,256]{1,0:T(8,128)(2,1)} %constant.254.clone.cells_back) | copy-start | bytes 393220
  31.9 20.9 %copy-start.11 = (bf16[256,256]{1,0:T(8,128)(2,1)S(1)}, bf16[256,256]{1,0:T(8,128)(2,1)}, u32[]{:S(2)}) copy-start(bf16[256,256]{1,0:T(8,128)(2,1)} %constant.253.clone.cells) | copy-start | bytes 393220
  31.9 20.9 %copy-start.12 = (f32[256,128]{1,0:T(8,128)S(1)}, f32[256,128]{1,0:T(8,128)}, u32[]{:S(2)}) copy-start(f32[256,128]{1,0:T(8,128)} %constant.252.clone.radial_sin) | copy-start | bytes 393220
  31.9 20.9 %copy-start.13 = (f32[256,128]{1,0:T(8,128)S(1)}, f32[256,128]{1,0:T(8,128)}, u32[]{:S(2)}) copy-start(f32[256,128]{1,0:T(8,128)} %constant.251.clone.radial_cos) | copy-start | bytes 393220
  33.9 18.9 %copy-start.3 = (bf16[512,256]{1,0:T(8,128)(2,1)S(1)}, bf16[512,256]{1,0:T(8,128)(2,1)}, u32[]{:S(2)}) copy-start(bf16[512,256]{1,0:T(8,128)(2,1)} %constant.249.clone.groups_h) | copy-start | bytes 786436
  33.9 18.8 %all-to-all-start.1 = ((f32[256,1,128]{2,1,0:T(1,128)}), f32[256,1,128]{2,1,0:T(1,128)S(1)}, u32[]{:S(2)}, u32[]{:S(2)}) async-start(f32[256,1,128]{2,1,0:T(1,128)} %bitcast.15), calls=%async_computation.1 | async-start | bytes 262144 | tf_op jit(solution)/shard_map/all_to_all | solution.py:527
  39.7 13.1 %copy-start.1 = (bf16[512,256]{1,0:T(8,128)(2,1)S(1)}, bf16[512,256]{1,0:T(8,128)(2,1)}, u32[]{:S(2)}) copy-start(bf16[512,256]{1,0:T(8,128)(2,1)} %constant.255.clone.groups_back_h) | copy-start | bytes 786436
  39.7 13.1 %copy-start.2 = (bf16[512,256]{1,0:T(8,128)(2,1)S(1)}, bf16[512,256]{1,0:T(8,128)(2,1)}, u32[]{:S(2)}) copy-start(bf16[512,256]{1,0:T(8,128)(2,1)} %constant.250.clone.groups_l) | copy-start | bytes 786436
  40.9 11.9 %copy-start = (bf16[512,256]{1,0:T(8,128)(2,1)S(1)}, bf16[512,256]{1,0:T(8,128)(2,1)}, u32[]{:S(2)}) copy-start(bf16[512,256]{1,0:T(8,128)(2,1)} %constant.256.clone.groups_back_l) | copy-start | bytes 786436
  52.9 21.0 %copy-start.7 = (bf16[256,512]{1,0:T(8,128)(2,1)S(1)}, bf16[256,512]{1,0:T(8,128)(2,1)}, u32[]{:S(2)}) copy-start(bf16[256,512]{1,0:T(8,128)(2,1)} %constant.262.clone.blocks_h) | copy-start | bytes 786436
  52.9 21.0 %copy-start.14 = (f32[64,512]{1,0:T(8,128)S(1)}, f32[64,512]{1,0:T(8,128)}, u32[]{:S(2)}) copy-start(f32[64,512]{1,0:T(8,128)} %constant.261.clone.back_sin) | copy-start | bytes 393220
  52.9 21.0 %copy-start.15 = (f32[64,512]{1,0:T(8,128)S(1)}, f32[64,512]{1,0:T(8,128)}, u32[]{:S(2)}) copy-start(f32[64,512]{1,0:T(8,128)} %constant.260.clone.back_cos) | copy-start | bytes 393220
  52.9 21.0 %copy-start.19 = (bf16[128,96]{1,0:T(8,128)(2,1)S(1)}, bf16[128,96]{1,0:T(8,128)(2,1)}, u32[]{:S(2)}) copy-start(bf16[128,96]{1,0:T(8,128)(2,1)} %constant.259.clone.inner) | copy-start | bytes 73732
  55.3 18.6 %copy-start.6 = (bf16[256,512]{1,0:T(8,128)(2,1)S(1)}, bf16[256,512]{1,0:T(8,128)(2,1)}, u32[]{:S(2)}) copy-start(bf16[256,512]{1,0:T(8,128)(2,1)} %constant.263.clone.blocks_l) | copy-start | bytes 786436
  73.9 5.7 %copy-start.23 = (f32[1,64,256]{2,1,0:T(8,128)S(1)}, f32[1,64,256]{2,1,0:T(8,128)}, u32[]{:S(2)}) copy-start(f32[1,64,256]{2,1,0:T(8,128)} %param.27) | copy-start | bytes 196612
  75.3 4.3 %copy-start.21 = (f32[1,64,256]{2,1,0:T(8,128)S(1)}, f32[1,64,256]{2,1,0:T(8,128)}, u32[]{:S(2)}) copy-start(f32[1,64,256]{2,1,0:T(8,128)} %param.25) | copy-start | bytes 196612
  75.3 4.3 %copy-start.22 = (f32[1,64,256]{2,1,0:T(8,128)S(1)}, f32[1,64,256]{2,1,0:T(8,128)}, u32[]{:S(2)}) copy-start(f32[1,64,256]{2,1,0:T(8,128)} %param.26) | copy-start | bytes 196612
  75.3 12.2 %all-to-all-start.3 = ((f32[32,4,128]{2,1,0:T(4,128)}), f32[32,4,128]{2,1,0:T(4,128)S(1)}, u32[]{:S(2)}, u32[]{:S(2)}) async-start(f32[32,4,128]{2,1,0:T(4,128)} %bitcast.23), calls=%async_computation.3 | async-start | bytes 131072 | tf_op jit(solution)/shard_map/all_to_all | solution.py:558

commit v2 on v1

--- a/solution.py
+++ b/solution.py
@@ -20,6 +20,7 @@
 omega_rate = 0.5
 shear_rate = 1.5
 thickness = 0.5
+middle = 1.0
 
 BF = jnp.bfloat16
 F32 = jnp.float32
@@ -144,6 +145,23 @@
     return lax.broadcasted_iota(jnp.int32, shape, 0)
 
 
+def position():
+    return lax.axis_index("gx") * GY + lax.axis_index("gy")
+
+
+def wrap_hop(shifts):
+    row = position() & (ROWS - 1)
+    shifts = jnp.broadcast_to(shifts[0:1, :], (GY, 128))
+    return ((shifts >> 6) + (((shifts & (ROWS - 1)) + row) >> 6)) & (GY - 1)
+
+
+def turn_rows(block, hop, way):
+    for bit in range(5):
+        moved = roll(block, way << bit, 0)
+        block = jnp.where((hop >> bit) & 1 == 1, moved, block)
+    return block
+
+
 def interface(left, right, normal, parts=3):
     speed = jnp.maximum(jnp.abs(left[3]), jnp.abs(right[3])) + 1.0
     fluxes = []
@@ -171,7 +189,7 @@
     return [jnp.where(lane == 0, 0.0, v) for v in west], [jnp.where(row == 0, 0.0, v) for v in south]
 
 
-def pack_kernel(place, shift, rho, mx, my, out, held, shift_held, ready):
+def pack_kernel(shift, rho, mx, my, out, held, shift_held, ready):
     copies = [
         pltpu.make_async_copy(source, held.at[f], ready.at[f])
         for f, source in enumerate((rho, mx, my))
@@ -184,7 +202,7 @@
     state = (held[0], held[1], held[2])
     (west,), (south,) = inner_fluxes(state, 1)
     change = roll(west, -1, 1) - west + roll(south, -1, 0) - south
-    partial = state[0] - time_step * change
+    partial = state[0] - time_step * change - middle
     row = rows_of((8, COLS))
     edges = jnp.zeros((8, COLS), F32)
     for f in range(3):
@@ -197,7 +215,7 @@
     for f in range(3):
         low = jnp.where(lane == 72 + f, state[f][:, 0:1], low)
         high = jnp.where(lane == 75 + f, state[f][:, COLS - 1 : COLS], high)
-    slide = jnp.where(place[0] == GX - 1, (ROWS - (shift_held[0] & (ROWS - 1))) & (ROWS - 1), 0)
+    slide = jnp.where(lax.axis_index("gx") == GX - 1, (ROWS - (shift_held[0] & (ROWS - 1))) & (ROWS - 1), 0)
     out[0:ROWS, :] = tall[0:ROWS] + low + pltpu.roll(high, slide, 0)
     out[ROWS:, :] = tall[ROWS:]
 
@@ -209,7 +227,7 @@
     west, south = inner_fluxes(state, 3)
     across = arrived[...].T[32:40]
     beside = arrived[0:ROWS, :]
-    beside_high = pltpu.roll(beside, scalars[1], 0)
+    beside_high = pltpu.roll(beside, scalars[0], 0)
     new = []
     for f in range(3):
         east = jnp.where(lane == COLS - 1, beside_high[:, 41 + f : 42 + f], roll(west[f], -1, 1))
@@ -222,11 +240,10 @@
     my_out[...] = new[2] - time_step * (2.0 - shear_rate) * omega_rate * state[1]
 
 
-def edge_fluxes(scalars, arrived, parts):
-    row = scalars[4]
+def edge_fluxes(shifts, arrived, parts):
     narrow = lanes_of((32, 128))
     last = arrived[224:256, :]
-    wrapped = pltpu.roll(last, scalars[2], 0)
+    wrapped = turn_rows(last, wrap_hop(shifts), -1)
     last = jnp.where((narrow >= 75) & (narrow < 78), wrapped, last)
     tall = jnp.concatenate([arrived[0:224, :], last], 0).T
     lane = lanes_of((8, 256))
@@ -238,7 +255,7 @@
         2,
         parts,
     )
-    valid = jnp.zeros((1, 256), jnp.int32) + row >= 0
+    valid = jnp.zeros((1, 256), jnp.int32) + position() < ROWS
     side = tall[72:80]
     before = roll(side, 32, 1)
     left = [before[3 + f : 4 + f] for f in range(3)]
@@ -252,8 +269,8 @@
     return tall, west, south, north
 
 
-def edges_kernel(scalars, arrived, ride):
-    _, west, south, north = edge_fluxes(scalars, arrived, 3)
+def edges_kernel(shifts, arrived, ride):
+    _, west, south, north = edge_fluxes(shifts, arrived, 3)
     east = [roll(v, -32, 1) for v in west]
     narrow = lanes_of((32, 128))
     rows16 = rows_of((16, 256))
@@ -262,13 +279,13 @@
         fluxes = jnp.where(rows16 == at, value, fluxes)
     back = jnp.concatenate([jnp.zeros((32, 256), F32), fluxes, jnp.zeros((80, 256), F32)], 0).T
     last = back[224:256]
-    wrapped = pltpu.roll(last, scalars[3], 0)
+    wrapped = turn_rows(last, wrap_hop(shifts), 1)
     ride[0:224, :] = back[0:224]
     ride[224:256, :] = jnp.where((narrow >= 41) & (narrow < 44), wrapped, last)
 
 
-def forward_kernel(scalars, arrived, blocks_h, blocks_l, twist_cos, twist_sin, inner_h, inner_l, out):
-    tall, west, south, north = edge_fluxes(scalars, arrived, 1)
+def forward_kernel(shifts, arrived, blocks_h, blocks_l, twist_cos, twist_sin, inner_h, inner_l, out):
+    tall, west, south, north = edge_fluxes(shifts, arrived, 1)
     narrow = lanes_of((32, 128))
     rows8 = rows_of((8, 256))
     rows64 = rows_of((64, 256))
@@ -282,7 +299,7 @@
     re, im = first[:64, :256], first[:64, 256:]
     main = jnp.concatenate([re * tc + im * ts, im * tc - re * ts], 0)
     re, im = first[64:65, :256], first[64:65, 256:]
-    here = rows64 == scalars[4]
+    here = rows64 == position()
     edge = jnp.concatenate(
         [jnp.where(here, re * tc + im * ts, 0.0), jnp.where(here, im * tc - re * ts, 0.0)], 0
     )
@@ -307,7 +324,6 @@
 
 
 def radial_kernel(
-    scalars,
     arrived,
     ride,
     theta_cos,
@@ -334,7 +350,7 @@
 
     def apart(value):
         lane = lanes_of(value.shape)
-        first = jnp.zeros(value.shape, jnp.int32) + scalars[5] == 1
+        first = jnp.zeros(value.shape, jnp.int32) + position() == 0
         value = jnp.where(lane % 64 < 32, value, 0.0)
         fifth = roll(value, -32, 1)
         slot = (lane >= 64) & (lane < 72) & first
@@ -356,13 +372,15 @@
     value = value * radial_cos[...] + half(value) * radial_sin[...]
     both = product_rows(groups_h[...], groups_l[...], value)
     value = both[:256] + sign * half(both[256:])
+    mean_mode = (row == 0) & (lane == 0) & (jnp.zeros(shape, jnp.int32) + position() == 0)
+    value = value + jnp.where(mean_mode, middle * NX * NY, 0.0)
     value = value * weights[...]
     both = product_rows(groups_back_h[...], groups_back_l[...], value)
     value = both[:256] - sign * half(both[256:])
     value = value * return_cos[...] - half(value) * return_sin[...]
     value = product_lanes(value, cells_back[...])
     value = value * theta_cos_back[...] - half(value) * theta_sin_back[...]
-    first = jnp.zeros(shape, jnp.int32) + scalars[5] == 1
+    first = jnp.zeros(shape, jnp.int32) + position() == 0
     value = jnp.where((lane >= 64) & (lane < 72) & first, roll(value, 32, 1), value)
     blocks = [value[32 * k : 32 * k + 32] for k in range(8)]
     narrow = lanes_of((32, 128))
@@ -475,34 +493,19 @@
     rho, mx, my = density[0], xmomentum[0], ymomentum[0]
     shift = shear_shift[0]
     radial = lax.axis_index("gx")
-    flat = radial * GY + lax.axis_index("gy")
-    off = shift % ROWS
-    wrap_off = jnp.where(radial == GX - 1, off, 0)
-    hop = (shift // ROWS + (flat % ROWS + off) // ROWS) % GY
-    scalars = jnp.stack(
-        [
-            (ROWS - wrap_off) % ROWS,
-            wrap_off,
-            (GY - hop) % GY,
-            hop,
-            jnp.where(flat < ROWS, flat, -1),
-            (flat == 0).astype(jnp.int32),
-        ]
-    ).astype(jnp.int32)
+    scalars = jnp.where(radial == GX - 1, shift % ROWS, 0).astype(jnp.int32).reshape(1)
+    shifts = jnp.broadcast_to(shift, (8, 128))
     everyone = ("gx", "gy")
     block = (ROWS, COLS)
     table = (256, 128)
-    place = radial.astype(jnp.int32).reshape(1)
     columns = call(
         pack_kernel,
         table,
-        place,
         shear_shift,
         rho,
         mx,
         my,
         name="pack",
-        smem=1,
         hbm=4,
         room=62,
         scratch=(
@@ -515,21 +518,19 @@
     waves = call(
         forward_kernel,
         table,
-        scalars,
+        shifts,
         columns,
         *t["blocks"],
         t["twist_cos"],
         t["twist_sin"],
         *t["inner"],
         name="forward",
-        smem=1,
     )
     waves = lax.all_to_all(waves, everyone, 0, 0, tiled=True)
-    ride = call(edges_kernel, table, scalars, columns, name="edges", smem=1)
+    ride = call(edges_kernel, table, shifts, columns, name="edges")
     solved = call(
         radial_kernel,
         table,
-        scalars,
         waves,
         ride,
         *radial_tables(shift),
@@ -542,7 +543,6 @@
         t["return_cos"],
         t["return_sin"],
         name="radial",
-        smem=1,
     )
     solved = lax.all_to_all(solved, everyone, 0, 0, tiled=True)
     lines = call(

time: 88.5 us -> 87.5 us (0.989)
  Pallas kernels: 10.9 us -> 8.75 us
  waiting for transfers between devices: 28.9 us -> 30.2 us
    pallas_call x7, Pallas kernels: 10.9 us -> 8.75 us  [call(): pl.pallas_call(kernel, out_shape=outs if many else outs[0], in_specs=[SME...]
  transfers between devices with their start and end apart: 3 -> 3, of which waited for: 3 -> 3; matrix products, arithmetic and copies ran while one was open for 2% -> 2% of each run, Pallas kernels for 3% -> 2%
where the time goes in v2:
time: 87.5 us; the launch traced here: 87.1 us
  waiting for transfers between devices  30.2 us (35%)
  starting transfers between devices  25.7 us (29%)
  blocking collectives  18.5 us (21%)
  Pallas kernels  8.75 us (10%)
  other arithmetic  2.04 us (2%)
  between operations  1.75 us (2%)
    all_to_all x1, blocking collectives, shards(): solved = lax.all_to_all(solved, everyone, 0, 0, tiled=True)  18.5 us
    all_to_all x1, starting transfers between devices, shards(): columns = lax.all_to_all(columns, everyone, 0, 0, tiled=True)  15.7 us
    all_to_all x1, waiting for transfers between devices, shards(): columns = lax.all_to_all(columns, everyone, 0, 0, tiled=True)  12 us
    all_to_all x1, waiting for transfers between devices, shards(): waves = lax.all_to_all(waves, everyone, 0, 0, tiled=True)  11.5 us
    pallas_call x7, Pallas kernels, call(): pl.pallas_call(kernel, out_shape=outs if many else outs[0], in_specs=[SME...  8.75 us
    all_to_all x1, waiting for transfers between devices, shards(): lines = lax.all_to_all(lines, 'gy', 0, 0, tiled=True)  6.78 us
    all_to_all x1, starting transfers between devices, shards(): waves = lax.all_to_all(waves, everyone, 0, 0, tiled=True)  5.75 us
    all_to_all x1, starting transfers between devices, shards(): lines = lax.all_to_all(lines, 'gy', 0, 0, tiled=True)  4.26 us
  transfers between devices with their start and end apart: 3, of which 3 were waited for; matrix products, arithmetic and copies ran while one was open for 2% of the time, Pallas kernels for 2%

profile of v2, /device:TPU:1, one launch (start us, length us, event | category | flops | bytes accessed | tf_op | source)
XLA Modules:
  0.0 87.1 jit_solution(13179658379912706663)
XLA Ops:
  1.3 1.9 %pack.1 = f32[256,128]{1,0:T(8,128)} custom-call(s32[1]{0:T(128)} %copy.32.shift, f32[64,256]{1,0:T(8,128)} %bitcast.37, f32[64,256]{1,0:T(8,128)} %bitcast.39, f32[64,256]{1,0:T(8,128)} %bitcast.41), custom_call_target="tpu_custom_call" | custom-call | flops 100000000 | bytes 1000000 | tf_op jit(solution)/shard_map/pack/pallas_call | solution.py:445
  3.2 0.0 copy-start.17
  3.2 0.0 copy-start.18
  3.2 0.0 copy-start.20
  3.2 15.7 %all-to-all-start = ((f32[256,1,128]{2,1,0:T(1,128)}), f32[256,1,128]{2,1,0:T(1,128)S(1)}, u32[]{:S(2)}, u32[]{:S(2)}) async-start(f32[256,1,128]{2,1,0:T(1,128)} %bitcast.43), calls=%async_computation | async-start | bytes 262144 | tf_op jit(solution)/shard_map/all_to_all | solution.py:517
  19.0 0.0 copy-start.16
  19.0 0.0 copy-start.2
  19.0 0.0 copy-start.3
  19.2 0.7 multiply_multiply_fusion
  19.9 12.0 %all-to-all-done = f32[256,1,128]{2,1,0:T(1,128)S(1)} async-done(((f32[256,1,128]{2,1,0:T(1,128)}), f32[256,1,128]{2,1,0:T(1,128)S(1)}, u32[]{:S(2)}, u32[]{:S(2)}) %all-to-all-start) | async-done | bytes 131104 | tf_op jit(solution)/shard_map/all_to_all | solution.py:517
  31.9 0.0 copy-done.17
  31.9 0.0 copy-done.18
  31.9 0.0 copy-done.20
  31.9 0.0 copy-done.16
  31.9 0.0 copy-done.2
  31.9 0.0 copy-done.3
  31.9 0.0 copy-start.8
  31.9 0.0 copy-start.9
  31.9 0.0 copy-start.10
  31.9 0.0 copy-start.11
  31.9 0.0 copy-start.12
  32.0 0.0 copy-start.13
  32.0 1.5 %forward.1 = f32[256,128]{1,0:T(8,128)} custom-call(s32[8,128]{1,0:T(8,128)S(1)} %broadcast_in_dim.45.shifts, f32[256,128]{1,0:T(8,128)S(1)} %bitcast.30, bf16[256,512]{1,0:T(8,128)(2,1)S(1)} %copy-done.3, bf16[256,512]{1,0:T(8,128)(2,1)S(1)} %copy-done.2, f32[64,256]{1,0:T(8,128)S(1)} %copy-done.17, f32[64,256]{1,0:T(8,128)S(1)} %copy-done.16, ...), custom_call_target="tpu_custom_call" | custom-call | flops 100000000 | bytes 1000000 | tf_op jit(solution)/shard_map/forward/pallas_call | solution.py:445
  33.4 5.8 %all-to-all-start.1 = ((f32[256,1,128]{2,1,0:T(1,128)}), f32[256,1,128]{2,1,0:T(1,128)S(1)}, u32[]{:S(2)}, u32[]{:S(2)}) async-start(f32[256,1,128]{2,1,0:T(1,128)} %bitcast.9), calls=%async_computation.1 | async-start | bytes 262144 | tf_op jit(solution)/shard_map/all_to_all | solution.py:529
  39.2 0.0 copy-start.5
  39.2 0.0 copy-start.6
  39.2 1.2 %sine_multiply_fusion = (f32[256,128]{1,0:T(8,128)S(1)}, f32[256,128]{1,0:T(8,128)S(1)}, f32[256,128]{1,0:T(8,128)S(1)}) fusion(f32[128]{0:T(128)S(1)} %compare_select_fusion.1, s32[128]{0:T(128)S(1)} %get-tuple-element.19, s32[128]{0:T(128)S(1)} %get-tuple-element.21, pred[128]{0:T(512)(128)(4,1)S(1)} %get-tuple-element.17, s32[256]{0:T(256)S(1)} %get-tuple-element.24, ...), kind=kLoop, calls=%fused_computation.39 | loop fusion | flops 2752512 | bytes 402956 | tf_op jit(solution)/shard_map/mul | solution.py:470
  40.4 0.0 copy-start.4
  40.4 0.4 edges.1.ride
  40.8 11.5 %all-to-all-done.1 = f32[256,1,128]{2,1,0:T(1,128)S(1)} async-done(((f32[256,1,128]{2,1,0:T(1,128)}), f32[256,1,128]{2,1,0:T(1,128)S(1)}, u32[]{:S(2)}, u32[]{:S(2)}) %all-to-all-start.1) | async-done | bytes 131104 | tf_op jit(solution)/shard_map/all_to_all | solution.py:529
  52.3 0.0 copy-done.8
  52.3 0.0 copy-done.9
  52.3 0.0 copy-done.10
  52.3 0.0 copy-done.11
  52.3 0.0 copy-start.1
  52.4 0.0 copy-start.14
  52.4 0.0 copy-start.15
  52.4 0.0 copy-start.19
  52.4 1.8 %radial.1 = f32[256,128]{1,0:T(8,128)S(1)} custom-call(f32[256,128]{1,0:T(8,128)S(1)} %bitcast.32, f32[256,128]{1,0:T(8,128)S(1)} %edges.1.ride, f32[256,128]{1,0:T(8,128)S(1)} %get-tuple-element.16.theta_cos, f32[256,128]{1,0:T(8,128)S(1)} %get-tuple-element.14.theta_sin, f32[256,128]{1,0:T(8,128)S(1)} %get-tuple-element.13.theta_cos_back, ...), custom_call_target="tpu_custom_call" | custom-call | flops 100000000 | bytes 1000000 | tf_op jit(solution)/shard_map/radial/pallas_call | solution.py:445
  54.2 0.0 copy-start
  54.2 18.5 %all_to_all.44 = f32[256,1,128]{2,1,0:T(1,128)S(1)} all-to-all(f32[256,1,128]{2,1,0:T(1,128)S(1)} %bitcast.33), channel_id=1, replica_groups=mesh['gx'=8,'gy'=32] {'gx','gy'}, dimensions={0} | all-to-all | bytes 262144 | tf_op jit(solution)/shard_map/all_to_all | solution.py:547
  72.8 0.0 copy-done.14
  72.8 0.0 copy-start.23
  72.8 1.4 %backward.1 = f32[128,128]{1,0:T(8,128)} custom-call(f32[256,128]{1,0:T(8,128)S(1)} %bitcast.34, bf16[128,96]{1,0:T(8,128)(2,1)S(1)} %copy-done.19, f32[64,512]{1,0:T(8,128)S(1)} %copy-done.15, f32[64,512]{1,0:T(8,128)S(1)} %copy-done.14, bf16[256,512]{1,0:T(8,128)(2,1)S(1)} %copy-done.1, bf16[256,512]{1,0:T(8,128)(2,1)S(1)} %copy-done), custom_call_target="tpu_custom_call" | custom-call | flops 100000000 | bytes 1000000 | tf_op jit(solution)/shard_map/backward/pallas_call | solution.py:445
  74.2 4.3 %all-to-all-start.3 = ((f32[32,4,128]{2,1,0:T(4,128)}), f32[32,4,128]{2,1,0:T(4,128)S(1)}, u32[]{:S(2)}, u32[]{:S(2)}) async-start(f32[32,4,128]{2,1,0:T(4,128)} %bitcast.17), calls=%async_computation.3 | async-start | bytes 131072 | tf_op jit(solution)/shard_map/all_to_all | solution.py:558
  78.6 1.1 %finish.1 = (f32[64,256]{1,0:T(8,128)}, f32[64,256]{1,0:T(8,128)}, f32[64,256]{1,0:T(8,128)}) custom-call(s32[1]{0:T(128)} %bitcast.1.scalars, f32[64,256]{1,0:T(8,128)S(1)} %bitcast.38, f32[64,256]{1,0:T(8,128)S(1)} %bitcast.40, f32[64,256]{1,0:T(8,128)S(1)} %bitcast.42, f32[256,128]{1,0:T(8,128)S(1)} %bitcast.35), custom_call_target="tpu_custom_call" | custom-call | flops 100000000 | bytes 1000000 | tf_op jit(solution)/shard_map/finish/pallas_call | solution.py:445
  79.6 6.8 %all-to-all-done.3 = f32[32,4,128]{2,1,0:T(4,128)S(1)} async-done(((f32[32,4,128]{2,1,0:T(4,128)}), f32[32,4,128]{2,1,0:T(4,128)S(1)}, u32[]{:S(2)}, u32[]{:S(2)}) %all-to-all-start.3) | async-done | bytes 65568 | tf_op jit(solution)/shard_map/all_to_all | solution.py:558
  86.4 0.7 last.1
  (31 shorter events, 0.2 us)
Async XLA Ops:
  3.2 28.7 %copy-start.17 = (f32[64,256]{1,0:T(8,128)S(1)}, f32[64,256]{1,0:T(8,128)}, u32[]{:S(2)}) copy-start(f32[64,256]{1,0:T(8,128)} %constant.210.clone.twist_cos) | copy-start | bytes 196612
  3.2 28.6 %copy-start.18 = (bf16[80,256]{1,0:T(8,128)(2,1)S(1)}, bf16[80,256]{1,0:T(8,128)(2,1)}, u32[]{:S(2)}) copy-start(bf16[80,256]{1,0:T(8,128)(2,1)} %constant.212.clone.inner_h) | copy-start | bytes 122884
  3.2 28.6 %copy-start.20 = (bf16[80,128]{1,0:T(8,128)(2,1)S(1)}, bf16[80,128]{1,0:T(8,128)(2,1)}, u32[]{:S(2)}) copy-start(bf16[80,128]{1,0:T(8,128)(2,1)} %constant.213.clone.inner_l) | copy-start | bytes 61444
  3.2 28.6 %all-to-all-start = ((f32[256,1,128]{2,1,0:T(1,128)}), f32[256,1,128]{2,1,0:T(1,128)S(1)}, u32[]{:S(2)}, u32[]{:S(2)}) async-start(f32[256,1,128]{2,1,0:T(1,128)} %bitcast.43), calls=%async_computation | async-start | bytes 262144 | tf_op jit(solution)/shard_map/all_to_all | solution.py:517
  19.0 12.9 %copy-start.16 = (f32[64,256]{1,0:T(8,128)S(1)}, f32[64,256]{1,0:T(8,128)}, u32[]{:S(2)}) copy-start(f32[64,256]{1,0:T(8,128)} %constant.211.clone.twist_sin) | copy-start | bytes 196612
  19.0 12.9 %copy-start.2 = (bf16[256,512]{1,0:T(8,128)(2,1)S(1)}, bf16[256,512]{1,0:T(8,128)(2,1)}, u32[]{:S(2)}) copy-start(bf16[256,512]{1,0:T(8,128)(2,1)} %constant.209.clone.blocks_l) | copy-start | bytes 786436
  19.0 12.8 %copy-start.3 = (bf16[256,512]{1,0:T(8,128)(2,1)S(1)}, bf16[256,512]{1,0:T(8,128)(2,1)}, u32[]{:S(2)}) copy-start(bf16[256,512]{1,0:T(8,128)(2,1)} %constant.208.clone.blocks_h) | copy-start | bytes 786436
  31.9 20.4 %copy-start.8 = (f32[256,128]{1,0:T(8,128)S(1)}, f32[256,128]{1,0:T(8,128)}, u32[]{:S(2)}) copy-start(f32[256,128]{1,0:T(8,128)} %constant.223.clone.return_sin) | copy-start | bytes 393220
  31.9 20.4 %copy-start.9 = (f32[256,128]{1,0:T(8,128)S(1)}, f32[256,128]{1,0:T(8,128)}, u32[]{:S(2)}) copy-start(f32[256,128]{1,0:T(8,128)} %constant.222.clone.return_cos) | copy-start | bytes 393220
  31.9 20.4 %copy-start.10 = (bf16[256,256]{1,0:T(8,128)(2,1)S(1)}, bf16[256,256]{1,0:T(8,128)(2,1)}, u32[]{:S(2)}) copy-start(bf16[256,256]{1,0:T(8,128)(2,1)} %constant.219.clone.cells_back) | copy-start | bytes 393220
  31.9 20.3 %copy-start.11 = (bf16[256,256]{1,0:T(8,128)(2,1)S(1)}, bf16[256,256]{1,0:T(8,128)(2,1)}, u32[]{:S(2)}) copy-start(bf16[256,256]{1,0:T(8,128)(2,1)} %constant.218.clone.cells) | copy-start | bytes 393220
  31.9 20.3 %copy-start.12 = (f32[256,128]{1,0:T(8,128)S(1)}, f32[256,128]{1,0:T(8,128)}, u32[]{:S(2)}) copy-start(f32[256,128]{1,0:T(8,128)} %constant.217.clone.radial_sin) | copy-start | bytes 393220
  32.0 20.3 %copy-start.13 = (f32[256,128]{1,0:T(8,128)S(1)}, f32[256,128]{1,0:T(8,128)}, u32[]{:S(2)}) copy-start(f32[256,128]{1,0:T(8,128)} %constant.216.clone.radial_cos) | copy-start | bytes 393220
  33.4 18.9 %copy-start.7 = (bf16[512,256]{1,0:T(8,128)(2,1)S(1)}, bf16[512,256]{1,0:T(8,128)(2,1)}, u32[]{:S(2)}) copy-start(bf16[512,256]{1,0:T(8,128)(2,1)} %constant.214.clone.groups_h) | copy-start | bytes 786436
  33.4 18.8 %all-to-all-start.1 = ((f32[256,1,128]{2,1,0:T(1,128)}), f32[256,1,128]{2,1,0:T(1,128)S(1)}, u32[]{:S(2)}, u32[]{:S(2)}) async-start(f32[256,1,128]{2,1,0:T(1,128)} %bitcast.9), calls=%async_computation.1 | async-start | bytes 262144 | tf_op jit(solution)/shard_map/all_to_all | solution.py:529
  39.2 13.1 %copy-start.5 = (bf16[512,256]{1,0:T(8,128)(2,1)S(1)}, bf16[512,256]{1,0:T(8,128)(2,1)}, u32[]{:S(2)}) copy-start(bf16[512,256]{1,0:T(8,128)(2,1)} %constant.220.clone.groups_back_h) | copy-start | bytes 786436
  39.2 13.1 %copy-start.6 = (bf16[512,256]{1,0:T(8,128)(2,1)S(1)}, bf16[512,256]{1,0:T(8,128)(2,1)}, u32[]{:S(2)}) copy-start(bf16[512,256]{1,0:T(8,128)(2,1)} %constant.215.clone.groups_l) | copy-start | bytes 786436
  40.4 11.9 %copy-start.4 = (bf16[512,256]{1,0:T(8,128)(2,1)S(1)}, bf16[512,256]{1,0:T(8,128)(2,1)}, u32[]{:S(2)}) copy-start(bf16[512,256]{1,0:T(8,128)(2,1)} %constant.221.clone.groups_back_l) | copy-start | bytes 786436
  52.3 20.4 %copy-start.1 = (bf16[256,512]{1,0:T(8,128)(2,1)S(1)}, bf16[256,512]{1,0:T(8,128)(2,1)}, u32[]{:S(2)}) copy-start(bf16[256,512]{1,0:T(8,128)(2,1)} %constant.227.clone.blocks_h) | copy-start | bytes 786436
  52.4 20.4 %copy-start.14 = (f32[64,512]{1,0:T(8,128)S(1)}, f32[64,512]{1,0:T(8,128)}, u32[]{:S(2)}) copy-start(f32[64,512]{1,0:T(8,128)} %constant.226.clone.back_sin) | copy-start | bytes 393220
  52.4 20.4 %copy-start.15 = (f32[64,512]{1,0:T(8,128)S(1)}, f32[64,512]{1,0:T(8,128)}, u32[]{:S(2)}) copy-start(f32[64,512]{1,0:T(8,128)} %constant.225.clone.back_cos) | copy-start | bytes 393220
  52.4 20.4 %copy-start.19 = (bf16[128,96]{1,0:T(8,128)(2,1)S(1)}, bf16[128,96]{1,0:T(8,128)(2,1)}, u32[]{:S(2)}) copy-start(bf16[128,96]{1,0:T(8,128)(2,1)} %constant.224.clone.inner) | copy-start | bytes 73732
  54.2 18.6 %copy-start = (bf16[256,512]{1,0:T(8,128)(2,1)S(1)}, bf16[256,512]{1,0:T(8,128)(2,1)}, u32[]{:S(2)}) copy-start(bf16[256,512]{1,0:T(8,128)(2,1)} %constant.228.clone.blocks_l) | copy-start | bytes 786436
  72.8 5.7 %copy-start.23 = (f32[1,64,256]{2,1,0:T(8,128)S(1)}, f32[1,64,256]{2,1,0:T(8,128)}, u32[]{:S(2)}) copy-start(f32[1,64,256]{2,1,0:T(8,128)} %param.27) | copy-start | bytes 196612
  74.2 4.3 %copy-start.21 = (f32[1,64,256]{2,1,0:T(8,128)S(1)}, f32[1,64,256]{2,1,0:T(8,128)}, u32[]{:S(2)}) copy-start(f32[1,64,256]{2,1,0:T(8,128)} %param.25) | copy-start | bytes 196612
  74.2 4.3 %copy-start.22 = (f32[1,64,256]{2,1,0:T(8,128)S(1)}, f32[1,64,256]{2,1,0:T(8,128)}, u32[]{:S(2)}) copy-start(f32[1,64,256]{2,1,0:T(8,128)} %param.26) | copy-start | bytes 196612
  74.2 12.2 %all-to-all-start.3 = ((f32[32,4,128]{2,1,0:T(4,128)}), f32[32,4,128]{2,1,0:T(4,128)S(1)}, u32[]{:S(2)}, u32[]{:S(2)}) async-start(f32[32,4,128]{2,1,0:T(4,128)} %bitcast.17), calls=%async_computation.3 | async-start | bytes 131072 | tf_op jit(solution)/shard_map/all_to_all | solution.py:558

commit v3 on v2

--- a/solution.py
+++ b/solution.py
@@ -220,14 +220,19 @@
     out[ROWS:, :] = tall[ROWS:]
 
 
-def finish_kernel(scalars, rho, mx, my, arrived, rho_out, mx_out, my_out):
+def finish_kernel(shifts, rho, mx, my, arrived, lines, rho_out, mx_out, my_out, potential):
     state = (rho[...], mx[...], my[...])
     lane = lanes_of((ROWS, COLS))
     row = rows_of((ROWS, COLS))
     west, south = inner_fluxes(state, 3)
     across = arrived[...].T[32:40]
     beside = arrived[0:ROWS, :]
-    beside_high = pltpu.roll(beside, scalars[0], 0)
+    beside_high = beside
+    off = jnp.broadcast_to(shifts[0:1, :], (ROWS, 128)) & (ROWS - 1)
+    off = jnp.where(jnp.zeros((ROWS, 128), jnp.int32) + lax.axis_index("gx") == GX - 1, off, 0)
+    for bit in range(6):
+        moved = roll(beside_high, 1 << bit, 0)
+        beside_high = jnp.where((off >> bit) & 1 == 1, moved, beside_high)
     new = []
     for f in range(3):
         east = jnp.where(lane == COLS - 1, beside_high[:, 41 + f : 42 + f], roll(west[f], -1, 1))
@@ -237,6 +242,9 @@
         new.append(state[f] - time_step * (east - west_f + north - south_f))
     rho_out[...] = new[0]
     mx_out[...] = new[1] + time_step * 2.0 * omega_rate * state[2]
+    tall = lines[...].T
+    potential[:, :128] = tall[:ROWS]
+    potential[:, 128:] = tall[ROWS:]
     my_out[...] = new[2] - time_step * (2.0 - shear_rate) * omega_rate * state[1]
 
 
@@ -269,23 +277,13 @@
     return tall, west, south, north
 
 
-def edges_kernel(shifts, arrived, ride):
-    _, west, south, north = edge_fluxes(shifts, arrived, 3)
-    east = [roll(v, -32, 1) for v in west]
-    narrow = lanes_of((32, 128))
+def forward_kernel(shifts, arrived, blocks_h, blocks_l, twist_cos, twist_sin, inner_h, inner_l, out, fluxes):
+    tall, west, south, north = edge_fluxes(shifts, arrived, 3)
     rows16 = rows_of((16, 256))
-    fluxes = jnp.zeros((16, 256), F32)
-    for at, value in enumerate(south + north + west + east):
-        fluxes = jnp.where(rows16 == at, value, fluxes)
-    back = jnp.concatenate([jnp.zeros((32, 256), F32), fluxes, jnp.zeros((80, 256), F32)], 0).T
-    last = back[224:256]
-    wrapped = turn_rows(last, wrap_hop(shifts), 1)
-    ride[0:224, :] = back[0:224]
-    ride[224:256, :] = jnp.where((narrow >= 41) & (narrow < 44), wrapped, last)
-
-
-def forward_kernel(shifts, arrived, blocks_h, blocks_l, twist_cos, twist_sin, inner_h, inner_l, out):
-    tall, west, south, north = edge_fluxes(shifts, arrived, 1)
+    held = jnp.zeros((16, 256), F32)
+    for at, value in enumerate(south + north + west + [roll(v, -32, 1) for v in west]):
+        held = jnp.where(rows16 == at, value, held)
+    fluxes[...] = held
     narrow = lanes_of((32, 128))
     rows8 = rows_of((8, 256))
     rows64 = rows_of((64, 256))
@@ -324,8 +322,9 @@
 
 
 def radial_kernel(
+    shifts,
     arrived,
-    ride,
+    fluxes,
     theta_cos,
     theta_sin,
     theta_cos_back,
@@ -382,8 +381,20 @@
     value = value * theta_cos_back[...] - half(value) * theta_sin_back[...]
     first = jnp.zeros(shape, jnp.int32) + position() == 0
     value = jnp.where((lane >= 64) & (lane < 72) & first, roll(value, 32, 1), value)
+    narrow = lanes_of((32, 128))
+    none = jnp.zeros((32, 128), F32)
+    back = jnp.concatenate(
+        [
+            jnp.concatenate([none, fluxes[:, k : k + 128], none, none, none[:16]], 0).T
+            for k in (0, 128)
+        ],
+        0,
+    )
+    last = back[224:256]
+    wrapped = turn_rows(last, wrap_hop(shifts), 1)
+    ride = [back[32 * k : 32 * k + 32] for k in range(7)]
+    ride.append(jnp.where((narrow >= 41) & (narrow < 44), wrapped, last))
     blocks = [value[32 * k : 32 * k + 32] for k in range(8)]
-    narrow = lanes_of((32, 128))
     for bit in (1, 2, 4):
         swapped = list(blocks)
         for k in range(8):
@@ -393,8 +404,9 @@
                 swapped[k] = jnp.where(low, a, roll(b, bit, 1))
                 swapped[k + bit] = jnp.where(low, roll(a, -bit, 1), b)
         blocks = swapped
-    value = jnp.concatenate(blocks, 0)
-    out[...] = jnp.where((lane >= 32) & (lane < 44), ride[...], value)
+    spare = (narrow >= 32) & (narrow < 44)
+    for k in range(8):
+        out[32 * k : 32 * k + 32, :] = jnp.where(spare, ride[k], blocks[k])
 
 
 def backward_kernel(arrived, inner, back_cos, back_sin, blocks_h, blocks_l, out):
@@ -428,10 +440,352 @@
     out[...] = jnp.where(square < 64, full[:128], full[128:])
 
 
-def last_kernel(arrived, out):
-    tall = arrived[...].T
-    out[:, :128] = tall[:ROWS]
-    out[:, 128:] = tall[ROWS:]
+VMEM = pl.BlockSpec(memory_space=pltpu.VMEM)
+SMEM = pl.BlockSpec(memory_space=pltpu.SMEM)
+HBM = pl.BlockSpec(memory_space=pltpu.HBM)
+
+
+def call(kernel, shapes, *args, name, smem=0, hbm=0, scratch=(), room=32):
+    many = isinstance(shapes, list)
+    outs = [jax.ShapeDtypeStruct(s, F32) for s in (shapes if many else [shapes])]
+    return pl.pallas_call(
+        kernel,
+        out_shape=outs if many else outs[0],
+        in_specs=[SMEM] * smem + [HBM] * hbm + [VMEM] * (len(args) - smem - hbm),
+        out_specs=[VMEM] * len(outs) if many else VMEM,
+        scratch_shapes=scratch,
+        name=name,
+        compiler_params=pltpu.CompilerParams(vmem_limit_bytes=room * 1024 * 1024),
+        cost_estimate=pl.CostEstimate(flops=100_000_000, bytes_accessed=1_000_000, transcendentals=0),
+    )(*args)
+
+
+def radial_tables(shift):
+    shape = (256, 128)
+    row = lax.broadcasted_iota(jnp.int32, shape, 0)
+    lane = lax.broadcasted_iota(jnp.int32, shape, 1)
+    line = lane % 64 // 8
+    inside = lane % 8
+    wave = lax.axis_index("gx") * 4 + line + GY * lax.axis_index("gy")
+    wave = jnp.where(line < 4, wave, NY // 2)
+    sigma = wave * shift % NY
+    sign = jnp.where(lane < 64, 1.0, -1.0)
+
+    def phase(cell):
+        angle = (sigma * cell % (NX * NY)).astype(F32) * (2.0 * jnp.pi / (NX * NY))
+        return jnp.cos(angle), jnp.sin(angle) * sign
+
+    there = phase(row + COLS * inside)
+    back = phase(row // 128 * 128 + row // 32 % 4 + 4 * (row % 32) + COLS * inside)
+    n = inside + 8 * row
+    n = jnp.where(n < NX // 2, n, n - NX)
+    kx = 2.0 * jnp.pi / NX * (n.astype(F32) + sigma.astype(F32) / NY)
+    ky = 2.0 * jnp.pi / NY * wave.astype(F32)
+    size = jnp.sqrt(kx * kx + ky * ky)
+    anchor = (wave == 0) & (n == 0)
+    size = jnp.where(anchor, 1.0, size)
+    single = (wave == 0) | (wave == NY // 2)
+    scale = jnp.where(single, 1.0, 2.0) / (NX * NY)
+    weights = jnp.where(anchor, 0.0, -jnp.exp(-thickness * size) / size) * scale
+    angle = sigma[:8].astype(F32) * (2.0 * jnp.pi / NY)
+    last = inside[:8] == 7
+    wrap_cos = jnp.where(last, jnp.cos(angle), 1.0)
+    wrap_sin = jnp.where(last, jnp.sin(angle) * sign[:8], 0.0)
+    return *there, *back, weights, wrap_cos, wrap_sin
+
+
+def shards(density, xmomentum, ymomentum, shear_shift):
+    t = host_tables()
+    rho, mx, my = density[0], xmomentum[0], ymomentum[0]
+    shift = shear_shift[0]
+    radial = lax.axis_index("gx")
+    shifts = jnp.broadcast_to(shifts[0:1, :], (GY, 128))
+    return ((shifts >> 6) + (((shifts & (ROWS - 1)) + row) >> 6)) & (GY - 1)
+
+
+def turn_rows(block, hop, way):
+    for bit in range(5):
+        moved = roll(block, way << bit, 0)
+        block = jnp.where((hop >> bit) & 1 == 1, moved, block)
+    return block
+
+
+def interface(left, right, normal, parts=3):
+    speed = jnp.maximum(jnp.abs(left[3]), jnp.abs(right[3])) + 1.0
+    fluxes = []
+    for part in range(parts):
+        f_left = left[part] * left[3]
+        f_right = right[part] * right[3]
+        if part == normal:
+            f_left = f_left + left[0]
+            f_right = f_right + right[0]
+        fluxes.append(0.5 * (f_left + f_right) - 0.5 * speed * (right[part] - left[part]))
+    return fluxes
+
+
+def with_speed(fields, normal):
+    return (*fields, fields[normal] / fields[0])
+
+
+def inner_fluxes(state, parts):
+    lane = lanes_of((ROWS, COLS))
+    row = rows_of((ROWS, COLS))
+    mid = with_speed(state, 1)
+    west = interface([roll(v, 1, 1) for v in mid], mid, 1, parts)
+    mid = with_speed(state, 2)
+    south = interface([roll(v, 1, 0) for v in mid], mid, 2, parts)
+    return [jnp.where(lane == 0, 0.0, v) for v in west], [jnp.where(row == 0, 0.0, v) for v in south]
+
+
+def pack_kernel(shift, rho, mx, my, out, held, shift_held, ready):
+    copies = [
+        pltpu.make_async_copy(source, held.at[f], ready.at[f])
+        for f, source in enumerate((rho, mx, my))
+    ]
+    copies.append(pltpu.make_async_copy(shift, shift_held, ready.at[3]))
+    for copy in copies:
+        copy.start()
+    for copy in copies:
+        copy.wait()
+    state = (held[0], held[1], held[2])
+    (west,), (south,) = inner_fluxes(state, 1)
+    change = roll(west, -1, 1) - west + roll(south, -1, 0) - south
+    partial = state[0] - time_step * change - middle
+    row = rows_of((8, COLS))
+    edges = jnp.zeros((8, COLS), F32)
+    for f in range(3):
+        edges = jnp.where(row == f, state[f][0:1, :], edges)
+        edges = jnp.where(row == 3 + f, state[f][ROWS - 1 : ROWS, :], edges)
+    tall = jnp.concatenate([partial, edges, jnp.zeros((56, COLS), F32)], 0).T
+    lane = lanes_of((ROWS, 128))
+    low = jnp.zeros((ROWS, 128), F32)
+    high = jnp.zeros((ROWS, 128), F32)
+    for f in range(3):
+        low = jnp.where(lane == 72 + f, state[f][:, 0:1], low)
+        high = jnp.where(lane == 75 + f, state[f][:, COLS - 1 : COLS], high)
+    slide = jnp.where(lax.axis_index("gx") == GX - 1, (ROWS - (shift_held[0] & (ROWS - 1))) & (ROWS - 1), 0)
+    out[0:ROWS, :] = tall[0:ROWS] + low + pltpu.roll(high, slide, 0)
+    out[ROWS:, :] = tall[ROWS:]
+
+
+def finish_kernel(shifts, rho, mx, my, arrived, lines, rho_out, mx_out, my_out, potential):
+    state = (rho[...], mx[...], my[...])
+    lane = lanes_of((ROWS, COLS))
+    row = rows_of((ROWS, COLS))
+    west, south = inner_fluxes(state, 3)
+    across = arrived[...].T[32:40]
+    beside = arrived[0:ROWS, :]
+    beside_high = beside
+    off = jnp.broadcast_to(shifts[0:1, :], (ROWS, 128)) & (ROWS - 1)
+    off = jnp.where(jnp.zeros((ROWS, 128), jnp.int32) + lax.axis_index("gx") == GX - 1, off, 0)
+    for bit in range(6):
+        moved = roll(beside_high, 1 << bit, 0)
+        beside_high = jnp.where((off >> bit) & 1 == 1, moved, beside_high)
+    new = []
+    for f in range(3):
+        east = jnp.where(lane == COLS - 1, beside_high[:, 41 + f : 42 + f], roll(west[f], -1, 1))
+        north = jnp.where(row == ROWS - 1, across[3 + f : 4 + f, :], roll(south[f], -1, 0))
+        west_f = jnp.where(lane == 0, beside[:, 38 + f : 39 + f], west[f])
+        south_f = jnp.where(row == 0, across[f : f + 1, :], south[f])
+        new.append(state[f] - time_step * (east - west_f + north - south_f))
+    rho_out[...] = new[0]
+    mx_out[...] = new[1] + time_step * 2.0 * omega_rate * state[2]
+    tall = lines[...].T
+    potential[:, :128] = tall[:ROWS]
+    potential[:, 128:] = tall[ROWS:]
+    my_out[...] = new[2] - time_step * (2.0 - shear_rate) * omega_rate * state[1]
+
+
+def edge_fluxes(shifts, arrived, parts):
+    narrow = lanes_of((32, 128))
+    last = arrived[224:256, :]
+    wrapped = turn_rows(last, wrap_hop(shifts), -1)
+    last = jnp.where((narrow >= 75) & (narrow < 78), wrapped, last)
+    tall = jnp.concatenate([arrived[0:224, :], last], 0).T
+    lane = lanes_of((8, 256))
+    upper = tall[64:72]
+    before = jnp.where(lane % 32 == 0, roll(upper, -31, 1), roll(upper, 1, 1))
+    south = interface(
+        with_speed([before[3 + f : 4 + f] for f in range(3)], 2),
+        with_speed([upper[f : f + 1] for f in range(3)], 2),
+        2,
+        parts,
+    )
+    valid = jnp.zeros((1, 256), jnp.int32) + position() < ROWS
+    side = tall[72:80]
+    before = roll(side, 32, 1)
+    left = [before[3 + f : 4 + f] for f in range(3)]
+    right = [side[f : f + 1] for f in range(3)]
+    left[0] = jnp.where(valid, left[0], 1.0)
+    right[0] = jnp.where(valid, right[0], 1.0)
+    west = interface(with_speed(left, 1), with_speed(right, 1), 1, parts)
+    west = [jnp.where(valid, v, 0.0) for v in west]
+    line = lanes_of((1, 256))
+    north = [jnp.where(line % 32 == 31, roll(v, 31, 1), roll(v, -1, 1)) for v in south]
+    return tall, west, south, north
+
+
+def forward_kernel(shifts, arrived, blocks_h, blocks_l, twist_cos, twist_sin, inner_h, inner_l, out, fluxes):
+    tall, west, south, north = edge_fluxes(shifts, arrived, 3)
+    rows16 = rows_of((16, 256))
+    held = jnp.zeros((16, 256), F32)
+    for at, value in enumerate(south + north + west + [roll(v, -32, 1) for v in west]):
+        held = jnp.where(rows16 == at, value, held)
+    fluxes[...] = held
+    narrow = lanes_of((32, 128))
+    rows8 = rows_of((8, 256))
+    rows64 = rows_of((64, 256))
+    density = tall[0:64]
+    density = density + jnp.where(rows64 == 0, time_step * south[0], 0.0)
+    density = density - jnp.where(rows64 == 63, time_step * north[0], 0.0)
+    edge = jnp.where(rows8 == 0, time_step * west[0], 0.0)
+    first = product_right(jnp.concatenate([density, edge], 0), blocks_h[...], blocks_l[...])
+    tc = twist_cos[...]
+    ts = twist_sin[...]
+    re, im = first[:64, :256], first[:64, 256:]
+    main = jnp.concatenate([re * tc + im * ts, im * tc - re * ts], 0)
+    re, im = first[64:65, :256], first[64:65, 256:]
+    here = rows64 == position()
+    edge = jnp.concatenate(
+        [jnp.where(here, re * tc + im * ts, 0.0), jnp.where(here, im * tc - re * ts, 0.0)], 0
+    )
+    head, rest = split(jnp.concatenate([main, edge], 1))
+    waves = dot(inner_h[...], jnp.concatenate([head, rest], 0)) + dot(inner_l[...], head)
+    rows32 = rows_of((32, 128))
+    for g in range(8):
+        place = 32 * (g % 4)
+        pieces = []
+        for start in (0, 256):
+            tile = slice(start + g // 4 * 128, start + g // 4 * 128 + 128)
+            real = waves[0:32, tile]
+            imag = waves[32:64, tile]
+            if g == 0:
+                imag = jnp.where((rows32 == 0) & (narrow < 8), waves[64:65, tile], imag)
+            pieces.append((real, imag))
+        both = roll(pieces[1][1], 96 - place, 1)
+        both = jnp.where(narrow < 96, roll(pieces[0][1], 64 - place, 1), both)
+        both = jnp.where(narrow < 64, roll(pieces[1][0], 32 - place, 1), both)
+        both = jnp.where(narrow < 32, roll(pieces[0][0], -place, 1), both)
+        out[g * 32 : (g + 1) * 32, :] = both
+
+
+def radial_kernel(
+    shifts,
+    arrived,
+    fluxes,
+    theta_cos,
+    theta_sin,
+    theta_cos_back,
+    theta_sin_back,
+    weights,
+    wrap_cos,
+    wrap_sin,
+    groups_h,
+    groups_l,
+    radial_cos,
+    radial_sin,
+    cells,
+    cells_back,
+    groups_back_h,
+    groups_back_l,
+    return_cos,
+    return_sin,
+    out,
+):
+    shape = (256, 128)
+    half = functools.partial(roll, shift=64, axis=1)
+
+    def apart(value):
+        lane = lanes_of(value.shape)
+        first = jnp.zeros(value.shape, jnp.int32) + position() == 0
+        value = jnp.where(lane % 64 < 32, value, 0.0)
+        fifth = roll(value, -32, 1)
+        slot = (lane >= 64) & (lane < 72) & first
+        return jnp.where((lane >= 32) & (lane < 40), fifth, jnp.where(slot, 0.0, value))
+
+    lane = lanes_of(shape)
+    row = rows_of(shape)
+    sign = jnp.where(lane < 64, 1.0, -1.0)
+    value = arrived[...]
+    edge = jnp.sum(value[0:ROWS], axis=0, keepdims=True)
+    edge = apart(roll(jnp.broadcast_to(edge, (8, 128)), -32, 1))
+    lane8 = lanes_of((8, 128))
+    beside = jnp.where(lane8 % 8 == 7, roll(edge, 7, 1), roll(edge, -1, 1))
+    beside = beside * wrap_cos[...] + half(beside) * wrap_sin[...]
+    value = apart(value)
+    value = value + jnp.where(row == 0, edge[0:1], 0.0) - jnp.where(row == 255, beside[0:1], 0.0)
+    value = value * theta_cos[...] + half(value) * theta_sin[...]
+    value = product_lanes(value, cells[...])
+    value = value * radial_cos[...] + half(value) * radial_sin[...]
+    both = product_rows(groups_h[...], groups_l[...], value)
+    value = both[:256] + sign * half(both[256:])
+    mean_mode = (row == 0) & (lane == 0) & (jnp.zeros(shape, jnp.int32) + position() == 0)
+    value = value + jnp.where(mean_mode, middle * NX * NY, 0.0)
+    value = value * weights[...]
+    both = product_rows(groups_back_h[...], groups_back_l[...], value)
+    value = both[:256] - sign * half(both[256:])
+    value = value * return_cos[...] - half(value) * return_sin[...]
+    value = product_lanes(value, cells_back[...])
+    value = value * theta_cos_back[...] - half(value) * theta_sin_back[...]
+    first = jnp.zeros(shape, jnp.int32) + position() == 0
+    value = jnp.where((lane >= 64) & (lane < 72) & first, roll(value, 32, 1), value)
+    narrow = lanes_of((32, 128))
+    none = jnp.zeros((32, 128), F32)
+    back = jnp.concatenate(
+        [
+            jnp.concatenate([none, fluxes[:, k : k + 128], none, none, none[:16]], 0).T
+            for k in (0, 128)
+        ],
+        0,
+    )
+    last = back[224:256]
+    wrapped = turn_rows(last, wrap_hop(shifts), 1)
+    ride = [back[32 * k : 32 * k + 32] for k in range(7)]
+    ride.append(jnp.where((narrow >= 41) & (narrow < 44), wrapped, last))
+    blocks = [value[32 * k : 32 * k + 32] for k in range(8)]
+    for bit in (1, 2, 4):
+        swapped = list(blocks)
+        for k in range(8):
+            if k & bit == 0:
+                a, b = blocks[k], blocks[k + bit]
+                low = narrow & bit == 0
+                swapped[k] = jnp.where(low, a, roll(b, bit, 1))
+                swapped[k + bit] = jnp.where(low, roll(a, -bit, 1), b)
+        blocks = swapped
+    spare = (narrow >= 32) & (narrow < 44)
+    for k in range(8):
+        out[32 * k : 32 * k + 32, :] = jnp.where(spare, ride[k], blocks[k])
+
+
+def backward_kernel(arrived, inner, back_cos, back_sin, blocks_h, blocks_l, out):
+    lane = lanes_of((32, 128))
+    low = lane % 64 < 32
+    pairs = []
+    for h in range(4):
+        even = arrived[64 * h : 64 * h + 32, :]
+        odd = arrived[64 * h + 32 : 64 * h + 64, :]
+        pairs.append(jnp.where(low, even, roll(odd, 32, 1)))
+    value = jnp.concatenate(pairs, 1)
+    head, rest = split(value)
+    both = dot(inner[...], jnp.concatenate([head, rest, head], 0))
+    wide = lanes_of((64, 128))
+    row = rows_of((64, 128))
+    sign = jnp.where(wide < 64, 1.0, -1.0)
+    parity = jnp.where(row % 2 == 0, 1.0, -1.0)
+    turned = []
+    for h in range(4):
+        tile = slice(128 * h, 128 * h + 128)
+        part = both[:64, tile] - sign * roll(both[64:, tile], 64, 1)
+        part = part * back_cos[:, tile] - roll(part, 64, 1) * back_sin[:, tile]
+        if h == 0:
+            part = jnp.where((wide >= 64) & (wide < 72), parity * pairs[0][0:1, :], part)
+        turned.append(part)
+    head, rest = split(jnp.concatenate(turned, 1))
+    full = dot(blocks_h[...], jnp.concatenate([head, rest], 0), NT)
+    full = full + roll(full, 64, 1)
+    full = full + dot(blocks_l[...], jnp.concatenate([head, head], 0), NT)
+    square = lanes_of((128, 128))
+    out[...] = jnp.where(square < 64, full[:128], full[128:])
 
 
 VMEM = pl.BlockSpec(memory_space=pltpu.VMEM)
@@ -515,9 +869,10 @@
         ),
     )
     columns = lax.all_to_all(columns, everyone, 0, 0, tiled=True)
-    waves = call(
+    columns, tables = lax.optimization_barrier((columns, radial_tables(shift)))
+    waves, fluxes = call(
         forward_kernel,
-        table,
+        [table, (16, 256)],
         shifts,
         columns,
         *t["blocks"],
@@ -527,13 +882,13 @@
         name="forward",
     )
     waves = lax.all_to_all(waves, everyone, 0, 0, tiled=True)
-    ride = call(edges_kernel, table, shifts, columns, name="edges")
     solved = call(
         radial_kernel,
         table,
+        shifts,
         waves,
-        ride,
-        *radial_tables(shift),
+        fluxes,
+        *tables,
         *t["groups"],
         t["radial_cos"],
         t["radial_sin"],
@@ -556,10 +911,9 @@
         name="backward",
     )
     lines = lax.all_to_all(lines, "gy", 0, 0, tiled=True)
-    rho_new, mx_new, my_new = call(
-        finish_kernel, [block, block, block], scalars, rho, mx, my, solved, name="finish", smem=1
-    )
-    potential = call(last_kernel, block, lines, name="last")
+    rho_new, mx_new, my_new, potential = call(
+        finish_kernel, [block] * 4, shifts, rho, mx, my, solved, lines, name="finish"
+    )
     return rho_new[None], mx_new[None], my_new[None], potential[None]
 
 

time: 87.5 us -> 86 us (0.983)
  blocking collectives: 18.5 us -> 48.9 us
  waiting for transfers between devices: 30.2 us -> 10.7 us
  starting transfers between devices: 25.7 us -> 15.7 us
  Pallas kernels: 8.75 us -> 6.45 us
    all_to_all x0 -> x2, blocking collectives: none -> 30.3 us  [the longest x1 18.5 us: shards(): waves = lax.all_to_all(waves, everyone, 0, 0, tiled=True)]
    all_to_all x2 -> x0, waiting for transfers between devices: 18.2 us -> none  [the longest x1 11.5 us: shards(): waves = lax.all_to_all(waves, everyone, 0, 0, tiled=True)]
    all_to_all x2 -> x0, starting transfers between devices: 10 us -> none  [the longest x1 5.75 us: shards(): waves = lax.all_to_all(waves, everyone, 0, 0, tiled=True)]
    pallas_call x7 -> x5, Pallas kernels: 8.75 us -> 6.45 us  [call(): pl.pallas_call(kernel, out_shape=outs if many else outs[0], in_specs=[SME...]
    all_to_all x1, waiting for transfers between devices: 12 us -> 10.7 us  [shards(): columns = lax.all_to_all(columns, everyone, 0, 0, tiled=True)]
  transfers between devices with their start and end apart: 3 -> 1, of which waited for: 3 -> 1; matrix products, arithmetic and copies ran while one was open for 2% -> 2% of each run, Pallas kernels for 2% -> 0%
where the time goes in v3:
time: 86 us; the launch traced here: 85.6 us
  blocking collectives  48.9 us (57%)
  starting transfers between devices  15.7 us (18%)
  waiting for transfers between devices  10.7 us (12%)
  Pallas kernels  6.45 us (8%)
  other arithmetic  2.04 us (2%)
  between operations  1.72 us (2%)
    all_to_all x1, blocking collectives, shards(): solved = lax.all_to_all(solved, everyone, 0, 0, tiled=True)  18.5 us
    all_to_all x1, blocking collectives, shards(): waves = lax.all_to_all(waves, everyone, 0, 0, tiled=True)  18.5 us
    all_to_all x1, starting transfers between devices, shards(): columns = lax.all_to_all(columns, everyone, 0, 0, tiled=True)  15.7 us
    all_to_all x1, blocking collectives, shards(): lines = lax.all_to_all(lines, 'gy', 0, 0, tiled=True)  11.8 us
    all_to_all x1, waiting for transfers between devices, shards(): columns = lax.all_to_all(columns, everyone, 0, 0, tiled=True)  10.7 us
    pallas_call x5, Pallas kernels, call(): pl.pallas_call(kernel, out_shape=outs if many else outs[0], in_specs=[SME...  6.45 us
  transfers between devices with their start and end apart: 1, of which 1 were waited for; matrix products, arithmetic and copies ran while one was open for 2% of the time, Pallas kernels for 0%

profile of v3, /device:TPU:1, one launch (start us, length us, event | category | flops | bytes accessed | tf_op | source)
XLA Modules:
  0.0 85.6 jit_solution(924204377677450738)
XLA Ops:
  1.3 0.0 copy-start.20
  1.3 0.0 copy-start.21
  1.3 0.0 copy-start.23
  1.3 1.9 %pack.1 = f32[256,128]{1,0:T(8,128)} custom-call(s32[1]{0:T(128)} %copy.32.shift, f32[64,256]{1,0:T(8,128)} %bitcast.34, f32[64,256]{1,0:T(8,128)} %bitcast.36, f32[64,256]{1,0:T(8,128)} %bitcast.38), custom_call_target="tpu_custom_call" | custom-call | flops 100000000 | bytes 1000000 | tf_op jit(solution)/shard_map/pack/pallas_call | solution.py:799
  3.3 0.0 copy-start.12
  3.3 0.0 copy-start.13
  3.3 15.7 %all-to-all-start = ((f32[256,1,128]{2,1,0:T(1,128)}), f32[256,1,128]{2,1,0:T(1,128)S(1)}, u32[]{:S(2)}, u32[]{:S(2)}) async-start(f32[256,1,128]{2,1,0:T(1,128)} %bitcast.40), calls=%async_computation | async-start | bytes 262144 | tf_op jit(solution)/shard_map/all_to_all | solution.py:871
  19.0 0.0 copy-start.19
  19.1 0.0 copy-start.11
  19.1 0.0 copy-start.10
  19.3 0.0 copy-start.1
  19.3 0.0 copy-start.9
  19.3 0.7 multiply_multiply_fusion
  19.9 0.0 copy-start
  20.0 0.0 copy-start.8
  20.0 1.2 %sine_multiply_fusion = (f32[256,128]{1,0:T(8,128)S(1)}, f32[256,128]{1,0:T(8,128)S(1)}, f32[256,128]{1,0:T(8,128)S(1)}) fusion(f32[128]{0:T(128)S(1)} %compare_select_fusion.1, s32[128]{0:T(128)S(1)} %get-tuple-element.41, s32[128]{0:T(128)S(1)} %get-tuple-element.43, pred[128]{0:T(512)(128)(4,1)S(1)} %get-tuple-element.39, s32[256]{0:T(256)S(1)} %get-tuple-element.46, ...), kind=kLoop, calls=%fused_computation.39 | loop fusion | flops 2752512 | bytes 402956 | tf_op jit(solution)/shard_map/mul | solution.py:824
  21.2 10.7 %all-to-all-done = f32[256,1,128]{2,1,0:T(1,128)S(1)} async-done(((f32[256,1,128]{2,1,0:T(1,128)}), f32[256,1,128]{2,1,0:T(1,128)S(1)}, u32[]{:S(2)}, u32[]{:S(2)}) %all-to-all-start) | async-done | bytes 131104 | tf_op jit(solution)/shard_map/all_to_all | solution.py:871
  31.9 0.0 copy-done.20
  31.9 0.0 copy-done.21
  31.9 0.0 copy-done.23
  31.9 0.0 copy-done.19
  31.9 0.0 copy-done.1
  31.9 0.0 copy-done
  31.9 0.0 copy-start.5
  32.0 0.0 copy-start.6
  32.0 0.0 copy-start.7
  32.0 0.8 forward.1
  32.8 0.0 copy-start.4
  32.8 18.5 %all_to_all.45 = f32[256,1,128]{2,1,0:T(1,128)S(1)} all-to-all(f32[256,1,128]{2,1,0:T(1,128)S(1)} %bitcast.33), channel_id=1, replica_groups=mesh['gx'=8,'gy'=32] {'gx','gy'}, dimensions={0} | all-to-all | bytes 262144 | tf_op jit(solution)/shard_map/all_to_all | solution.py:884
  51.4 0.0 copy-done.12
  51.4 0.0 copy-done.13
  51.4 0.0 copy-done.11
  51.4 0.0 copy-start.3
  51.5 0.0 copy-start.14
  51.5 0.0 copy-start.15
  51.5 0.0 copy-start.22
  51.5 1.9 %radial.1 = f32[256,128]{1,0:T(8,128)S(1)} custom-call(s32[8,128]{1,0:T(8,128)S(1)} %broadcast_in_dim.45.shifts, f32[256,128]{1,0:T(8,128)S(1)} %bitcast.28, f32[16,256]{1,0:T(8,128)S(1)} %get-tuple-element.20.fluxes, f32[256,128]{1,0:T(8,128)S(1)} %get-tuple-element.21.theta_cos, f32[256,128]{1,0:T(8,128)S(1)} %get-tuple-element.22.theta_sin, ...), custom_call_target="tpu_custom_call" | custom-call | flops 100000000 | bytes 1000000 | tf_op jit(solution)/shard_map/radial/pallas_call | solution.py:799
  53.4 0.0 copy-start.2
  53.4 18.5 %all_to_all.46 = f32[256,1,128]{2,1,0:T(1,128)S(1)} all-to-all(f32[256,1,128]{2,1,0:T(1,128)S(1)} %bitcast.29), channel_id=1, replica_groups=mesh['gx'=8,'gy'=32] {'gx','gy'}, dimensions={0} | all-to-all | bytes 262144 | tf_op jit(solution)/shard_map/all_to_all | solution.py:902
  71.9 0.0 copy-done.22
  72.0 0.0 copy-done.2
  72.0 0.0 copy-start.18
  72.0 0.8 backward.1
  72.7 0.0 copy-start.16
  72.8 0.0 copy-start.17
  72.8 11.8 %all_to_all.47 = f32[32,4,128]{2,1,0:T(4,128)S(1)} all-to-all(f32[32,4,128]{2,1,0:T(4,128)S(1)} %bitcast.32), channel_id=1, replica_groups=mesh['gx'=8,'gy'=32] {'gy'}, dimensions={0} | all-to-all | bytes 131072 | tf_op jit(solution)/shard_map/all_to_all | solution.py:913
  84.6 0.0 copy-done.18
  84.6 1.1 %finish.1 = (f32[64,256]{1,0:T(8,128)}, f32[64,256]{1,0:T(8,128)}, f32[64,256]{1,0:T(8,128)}, f32[64,256]{1,0:T(8,128)}) custom-call(s32[8,128]{1,0:T(8,128)S(1)} %broadcast_in_dim.45.shifts, f32[64,256]{1,0:T(8,128)S(1)} %bitcast.35, f32[64,256]{1,0:T(8,128)S(1)} %bitcast.37, f32[64,256]{1,0:T(8,128)S(1)} %bitcast.39, f32[256,128]{1,0:T(8,128)S(1)} %bitcast.27, ...), custom_call_target="tpu_custom_call" | custom-call | flops 100000000 | bytes 1000000 | tf_op jit(solution)/shard_map/finish/pallas_call | solution.py:799
  (27 shorter events, 0.2 us)
Async XLA Ops:
  1.3 30.6 %copy-start.20 = (f32[64,256]{1,0:T(8,128)S(1)}, f32[64,256]{1,0:T(8,128)}, u32[]{:S(2)}) copy-start(f32[64,256]{1,0:T(8,128)} %constant.202.clone.twist_cos) | copy-start | bytes 196612
  1.3 30.6 %copy-start.21 = (bf16[80,256]{1,0:T(8,128)(2,1)S(1)}, bf16[80,256]{1,0:T(8,128)(2,1)}, u32[]{:S(2)}) copy-start(bf16[80,256]{1,0:T(8,128)(2,1)} %constant.204.clone.inner_h) | copy-start | bytes 122884
  1.3 30.6 %copy-start.23 = (bf16[80,128]{1,0:T(8,128)(2,1)S(1)}, bf16[80,128]{1,0:T(8,128)(2,1)}, u32[]{:S(2)}) copy-start(bf16[80,128]{1,0:T(8,128)(2,1)} %constant.205.clone.inner_l) | copy-start | bytes 61444
  3.3 48.1 %copy-start.12 = (f32[256,128]{1,0:T(8,128)S(1)}, f32[256,128]{1,0:T(8,128)}, u32[]{:S(2)}) copy-start(f32[256,128]{1,0:T(8,128)} %constant.209.clone.radial_sin) | copy-start | bytes 393220
  3.3 48.1 %copy-start.13 = (f32[256,128]{1,0:T(8,128)S(1)}, f32[256,128]{1,0:T(8,128)}, u32[]{:S(2)}) copy-start(f32[256,128]{1,0:T(8,128)} %constant.208.clone.radial_cos) | copy-start | bytes 393220
  3.3 28.6 %all-to-all-start = ((f32[256,1,128]{2,1,0:T(1,128)}), f32[256,1,128]{2,1,0:T(1,128)S(1)}, u32[]{:S(2)}, u32[]{:S(2)}) async-start(f32[256,1,128]{2,1,0:T(1,128)} %bitcast.40), calls=%async_computation | async-start | bytes 262144 | tf_op jit(solution)/shard_map/all_to_all | solution.py:871
  19.0 12.9 %copy-start.19 = (f32[64,256]{1,0:T(8,128)S(1)}, f32[64,256]{1,0:T(8,128)}, u32[]{:S(2)}) copy-start(f32[64,256]{1,0:T(8,128)} %constant.203.clone.twist_sin) | copy-start | bytes 196612
  19.1 32.3 %copy-start.11 = (bf16[256,256]{1,0:T(8,128)(2,1)S(1)}, bf16[256,256]{1,0:T(8,128)(2,1)}, u32[]{:S(2)}) copy-start(bf16[256,256]{1,0:T(8,128)(2,1)} %constant.210.clone.cells) | copy-start | bytes 393220
  19.1 32.3 %copy-start.10 = (bf16[256,256]{1,0:T(8,128)(2,1)S(1)}, bf16[256,256]{1,0:T(8,128)(2,1)}, u32[]{:S(2)}) copy-start(bf16[256,256]{1,0:T(8,128)(2,1)} %constant.211.clone.cells_back) | copy-start | bytes 393220
  19.3 12.7 %copy-start.1 = (bf16[256,512]{1,0:T(8,128)(2,1)S(1)}, bf16[256,512]{1,0:T(8,128)(2,1)}, u32[]{:S(2)}) copy-start(bf16[256,512]{1,0:T(8,128)(2,1)} %constant.200.clone.blocks_h) | copy-start | bytes 786436
  19.3 32.1 %copy-start.9 = (f32[256,128]{1,0:T(8,128)S(1)}, f32[256,128]{1,0:T(8,128)}, u32[]{:S(2)}) copy-start(f32[256,128]{1,0:T(8,128)} %constant.214.clone.return_cos) | copy-start | bytes 393220
  19.9 12.0 %copy-start = (bf16[256,512]{1,0:T(8,128)(2,1)S(1)}, bf16[256,512]{1,0:T(8,128)(2,1)}, u32[]{:S(2)}) copy-start(bf16[256,512]{1,0:T(8,128)(2,1)} %constant.201.clone.blocks_l) | copy-start | bytes 786436
  20.0 31.4 %copy-start.8 = (f32[256,128]{1,0:T(8,128)S(1)}, f32[256,128]{1,0:T(8,128)}, u32[]{:S(2)}) copy-start(f32[256,128]{1,0:T(8,128)} %constant.215.clone.return_sin) | copy-start | bytes 393220
  31.9 19.5 %copy-start.5 = (bf16[512,256]{1,0:T(8,128)(2,1)S(1)}, bf16[512,256]{1,0:T(8,128)(2,1)}, u32[]{:S(2)}) copy-start(bf16[512,256]{1,0:T(8,128)(2,1)} %constant.212.clone.groups_back_h) | copy-start | bytes 786436
  32.0 19.5 %copy-start.6 = (bf16[512,256]{1,0:T(8,128)(2,1)S(1)}, bf16[512,256]{1,0:T(8,128)(2,1)}, u32[]{:S(2)}) copy-start(bf16[512,256]{1,0:T(8,128)(2,1)} %constant.207.clone.groups_l) | copy-start | bytes 786436
  32.0 19.5 %copy-start.7 = (bf16[512,256]{1,0:T(8,128)(2,1)S(1)}, bf16[512,256]{1,0:T(8,128)(2,1)}, u32[]{:S(2)}) copy-start(bf16[512,256]{1,0:T(8,128)(2,1)} %constant.206.clone.groups_h) | copy-start | bytes 786436
  32.8 18.6 %copy-start.4 = (bf16[512,256]{1,0:T(8,128)(2,1)S(1)}, bf16[512,256]{1,0:T(8,128)(2,1)}, u32[]{:S(2)}) copy-start(bf16[512,256]{1,0:T(8,128)(2,1)} %constant.213.clone.groups_back_l) | copy-start | bytes 786436
  51.4 20.5 %copy-start.3 = (bf16[256,512]{1,0:T(8,128)(2,1)S(1)}, bf16[256,512]{1,0:T(8,128)(2,1)}, u32[]{:S(2)}) copy-start(bf16[256,512]{1,0:T(8,128)(2,1)} %constant.219.clone.blocks_h) | copy-start | bytes 786436
  51.5 20.5 %copy-start.14 = (f32[64,512]{1,0:T(8,128)S(1)}, f32[64,512]{1,0:T(8,128)}, u32[]{:S(2)}) copy-start(f32[64,512]{1,0:T(8,128)} %constant.218.clone.back_sin) | copy-start | bytes 393220
  51.5 20.5 %copy-start.15 = (f32[64,512]{1,0:T(8,128)S(1)}, f32[64,512]{1,0:T(8,128)}, u32[]{:S(2)}) copy-start(f32[64,512]{1,0:T(8,128)} %constant.217.clone.back_cos) | copy-start | bytes 393220
  51.5 20.5 %copy-start.22 = (bf16[128,96]{1,0:T(8,128)(2,1)S(1)}, bf16[128,96]{1,0:T(8,128)(2,1)}, u32[]{:S(2)}) copy-start(bf16[128,96]{1,0:T(8,128)(2,1)} %constant.216.clone.inner) | copy-start | bytes 73732
  53.4 18.6 %copy-start.2 = (bf16[256,512]{1,0:T(8,128)(2,1)S(1)}, bf16[256,512]{1,0:T(8,128)(2,1)}, u32[]{:S(2)}) copy-start(bf16[256,512]{1,0:T(8,128)(2,1)} %constant.220.clone.blocks_l) | copy-start | bytes 786436
  72.0 12.6 %copy-start.18 = (f32[1,64,256]{2,1,0:T(8,128)S(1)}, f32[1,64,256]{2,1,0:T(8,128)}, u32[]{:S(2)}) copy-start(f32[1,64,256]{2,1,0:T(8,128)} %param.27) | copy-start | bytes 196612
  72.7 11.8 %copy-start.16 = (f32[1,64,256]{2,1,0:T(8,128)S(1)}, f32[1,64,256]{2,1,0:T(8,128)}, u32[]{:S(2)}) copy-start(f32[1,64,256]{2,1,0:T(8,128)} %param.25) | copy-start | bytes 196612
  72.8 11.8 %copy-start.17 = (f32[1,64,256]{2,1,0:T(8,128)S(1)}, f32[1,64,256]{2,1,0:T(8,128)}, u32[]{:S(2)}) copy-start(f32[1,64,256]{2,1,0:T(8,128)} %param.26) | copy-start | bytes 196612

commit v4 on v2

--- a/solution.py
+++ b/solution.py
@@ -162,6 +162,15 @@
     return block
 
 
+def turn_by_shift(block, shifts, way):
+    off = jnp.broadcast_to(shifts[0:1, :], (ROWS, 128)) & (ROWS - 1)
+    off = jnp.where(jnp.zeros((ROWS, 128), jnp.int32) + lax.axis_index("gx") == GX - 1, off, 0)
+    for bit in range(6):
+        moved = roll(block, way << bit, 0)
+        block = jnp.where((off >> bit) & 1 == 1, moved, block)
+    return block
+
+
 def interface(left, right, normal, parts=3):
     speed = jnp.maximum(jnp.abs(left[3]), jnp.abs(right[3])) + 1.0
     fluxes = []
@@ -189,17 +198,9 @@
     return [jnp.where(lane == 0, 0.0, v) for v in west], [jnp.where(row == 0, 0.0, v) for v in south]
 
 
-def pack_kernel(shift, rho, mx, my, out, held, shift_held, ready):
-    copies = [
-        pltpu.make_async_copy(source, held.at[f], ready.at[f])
-        for f, source in enumerate((rho, mx, my))
-    ]
-    copies.append(pltpu.make_async_copy(shift, shift_held, ready.at[3]))
-    for copy in copies:
-        copy.start()
-    for copy in copies:
-        copy.wait()
-    state = (held[0], held[1], held[2])
+def pack_kernel(shifts, rho, mx, my, after, out):
+    del after
+    state = (rho[...], mx[...], my[...])
     (west,), (south,) = inner_fluxes(state, 1)
     change = roll(west, -1, 1) - west + roll(south, -1, 0) - south
     partial = state[0] - time_step * change - middle
@@ -215,19 +216,18 @@
     for f in range(3):
         low = jnp.where(lane == 72 + f, state[f][:, 0:1], low)
         high = jnp.where(lane == 75 + f, state[f][:, COLS - 1 : COLS], high)
-    slide = jnp.where(lax.axis_index("gx") == GX - 1, (ROWS - (shift_held[0] & (ROWS - 1))) & (ROWS - 1), 0)
-    out[0:ROWS, :] = tall[0:ROWS] + low + pltpu.roll(high, slide, 0)
+    out[0:ROWS, :] = tall[0:ROWS] + low + turn_by_shift(high, shifts, -1)
     out[ROWS:, :] = tall[ROWS:]
 
 
-def finish_kernel(scalars, rho, mx, my, arrived, rho_out, mx_out, my_out):
+def finish_kernel(shifts, rho, mx, my, arrived, lines, rho_out, mx_out, my_out, potential):
     state = (rho[...], mx[...], my[...])
     lane = lanes_of((ROWS, COLS))
     row = rows_of((ROWS, COLS))
     west, south = inner_fluxes(state, 3)
     across = arrived[...].T[32:40]
     beside = arrived[0:ROWS, :]
-    beside_high = pltpu.roll(beside, scalars[0], 0)
+    beside_high = turn_by_shift(beside, shifts, 1)
     new = []
     for f in range(3):
         east = jnp.where(lane == COLS - 1, beside_high[:, 41 + f : 42 + f], roll(west[f], -1, 1))
@@ -237,7 +237,74 @@
         new.append(state[f] - time_step * (east - west_f + north - south_f))
     rho_out[...] = new[0]
     mx_out[...] = new[1] + time_step * 2.0 * omega_rate * state[2]
+    tall = lines[...].T
+    potential[:, :128] = tall[:ROWS]
+    potential[:, 128:] = tall[ROWS:]
     my_out[...] = new[2] - time_step * (2.0 - shear_rate) * omega_rate * state[1]
+
+
+def circle(turns):
+    quarter = jnp.floor(turns * 4.0 + 0.5)
+    x = (turns - quarter * 0.25) * (2.0 * np.pi)
+    y = x * x
+    s = x * (1.0 + y * (-1 / 6 + y * (1 / 120 + y * (-1 / 5040 + y * (1 / 362880)))))
+    c = 1.0 + y * (-1 / 2 + y * (1 / 24 + y * (-1 / 720 + y * (1 / 40320 - y * (1 / 3628800)))))
+    k = quarter.astype(jnp.int32)
+    swap = k & 1 == 1
+    sine = jnp.where(swap, c, s)
+    cosine = jnp.where(swap, s, c)
+    return jnp.where((k + 1) & 2 == 2, -cosine, cosine), jnp.where(k & 2 == 2, -sine, sine)
+
+
+def tables_kernel(shifts, there_cos, there_sin, back_cos, back_sin, weights, wrap_cos, wrap_sin):
+    def line_of(shape):
+        lane = lanes_of(shape)
+        line = (lane & 63) >> 3
+        wave = lax.axis_index("gx") * 4 + line + GY * lax.axis_index("gy")
+        return lane, jnp.where(line < 4, wave, NY // 2)
+
+    lane, wave = line_of((8, 128))
+    sigma = ((wave * shifts[...]) & (NY - 1)).astype(F32)[0:1]
+    sign = jnp.where(lane < 64, 1.0, -1.0)[0:1]
+
+    def phase(rows, of_row, of_lane):
+        shape = (rows, 128)
+        cell = of_row(rows_of(shape)) + of_lane * COLS * (lanes_of(shape) & 7)
+        return circle(sigma * cell.astype(F32) * (1.0 / (NX * NY)))
+
+    def fill(cos_out, sin_out, coarse, fine):
+        c1, s1 = coarse
+        c2, s2 = fine
+        size = c2.shape[0]
+        for k in range(256 // size):
+            at = slice(k * size, k * size + size)
+            ck, sk = c1[k : k + 1], s1[k : k + 1]
+            cos_out[at, :] = ck * c2 - sk * s2
+            sin_out[at, :] = (sk * c2 + ck * s2) * sign
+
+    fill(there_cos, there_sin, phase(16, lambda r: 16 * r, 0), phase(16, lambda r: r, 1))
+    fill(
+        back_cos,
+        back_sin,
+        phase(8, lambda r: (r >> 2) * 128 + (r & 3), 0),
+        phase(32, lambda r: 4 * r, 1),
+    )
+    shape = (256, 128)
+    lane, wave = line_of(shape)
+    n = (lane & 7) + 8 * rows_of(shape)
+    n = jnp.where(n < NX // 2, n, n - NX)
+    kx = 2.0 * np.pi / NX * (n.astype(F32) + sigma * (1.0 / NY))
+    ky = 2.0 * np.pi / NY * wave.astype(F32)
+    size = jnp.sqrt(kx * kx + ky * ky)
+    anchor = (wave == 0) & (n == 0)
+    size = jnp.where(anchor, 1.0, size)
+    single = (wave == 0) | (wave == NY // 2)
+    scale = jnp.where(single, 1.0, 2.0) / (NX * NY)
+    weights[...] = jnp.where(anchor, 0.0, -jnp.exp(-thickness * size) / size) * scale
+    c, s = circle(jnp.broadcast_to(sigma * (1.0 / NY), (8, 128)))
+    last = lanes_of((8, 128)) & 7 == 7
+    wrap_cos[...] = jnp.where(last, c, 1.0)
+    wrap_sin[...] = jnp.where(last, s * sign, 0.0)
 
 
 def edge_fluxes(shifts, arrived, parts):
@@ -269,30 +336,19 @@
     return tall, west, south, north
 
 
-def edges_kernel(shifts, arrived, ride):
-    _, west, south, north = edge_fluxes(shifts, arrived, 3)
-    east = [roll(v, -32, 1) for v in west]
+def forward_kernel(shifts, arrived, blocks_h, blocks_l, twist_cos, twist_sin, inner_h, inner_l, out, fluxes):
+    tall, west, south, north = edge_fluxes(shifts, arrived, 3)
+    rows16 = rows_of((16, 256))
+    held = jnp.zeros((16, 256), F32)
+    for at, value in enumerate(south + north + west + [roll(v, -32, 1) for v in west]):
+        held = jnp.where(rows16 == at, value, held)
+    fluxes[...] = held
     narrow = lanes_of((32, 128))
-    rows16 = rows_of((16, 256))
-    fluxes = jnp.zeros((16, 256), F32)
-    for at, value in enumerate(south + north + west + east):
-        fluxes = jnp.where(rows16 == at, value, fluxes)
-    back = jnp.concatenate([jnp.zeros((32, 256), F32), fluxes, jnp.zeros((80, 256), F32)], 0).T
-    last = back[224:256]
-    wrapped = turn_rows(last, wrap_hop(shifts), 1)
-    ride[0:224, :] = back[0:224]
-    ride[224:256, :] = jnp.where((narrow >= 41) & (narrow < 44), wrapped, last)
-
-
-def forward_kernel(shifts, arrived, blocks_h, blocks_l, twist_cos, twist_sin, inner_h, inner_l, out):
-    tall, west, south, north = edge_fluxes(shifts, arrived, 1)
-    narrow = lanes_of((32, 128))
-    rows8 = rows_of((8, 256))
     rows64 = rows_of((64, 256))
     density = tall[0:64]
     density = density + jnp.where(rows64 == 0, time_step * south[0], 0.0)
     density = density - jnp.where(rows64 == 63, time_step * north[0], 0.0)
-    edge = jnp.where(rows8 == 0, time_step * west[0], 0.0)
+    edge = jnp.where(rows16 == 0, time_step * west[0], 0.0)
     first = product_right(jnp.concatenate([density, edge], 0), blocks_h[...], blocks_l[...])
     tc = twist_cos[...]
     ts = twist_sin[...]
@@ -324,8 +380,9 @@
 
 
 def radial_kernel(
+    shifts,
     arrived,
-    ride,
+    fluxes,
     theta_cos,
     theta_sin,
     theta_cos_back,
@@ -382,8 +439,20 @@
     value = value * theta_cos_back[...] - half(value) * theta_sin_back[...]
     first = jnp.zeros(shape, jnp.int32) + position() == 0
     value = jnp.where((lane >= 64) & (lane < 72) & first, roll(value, 32, 1), value)
+    narrow = lanes_of((32, 128))
+    none = jnp.zeros((32, 128), F32)
+    back = jnp.concatenate(
+        [
+            jnp.concatenate([none, fluxes[:, k : k + 128], none, none, none[:16]], 0).T
+            for k in (0, 128)
+        ],
+        0,
+    )
+    last = back[224:256]
+    wrapped = turn_rows(last, wrap_hop(shifts), 1)
+    ride = [back[32 * k : 32 * k + 32] for k in range(7)]
+    ride.append(jnp.where((narrow >= 41) & (narrow < 44), wrapped, last))
     blocks = [value[32 * k : 32 * k + 32] for k in range(8)]
-    narrow = lanes_of((32, 128))
     for bit in (1, 2, 4):
         swapped = list(blocks)
         for k in range(8):
@@ -393,8 +462,9 @@
                 swapped[k] = jnp.where(low, a, roll(b, bit, 1))
                 swapped[k + bit] = jnp.where(low, roll(a, -bit, 1), b)
         blocks = swapped
-    value = jnp.concatenate(blocks, 0)
-    out[...] = jnp.where((lane >= 32) & (lane < 44), ride[...], value)
+    spare = (narrow >= 32) & (narrow < 44)
+    for k in range(8):
+        out[32 * k : 32 * k + 32, :] = jnp.where(spare, ride[k], blocks[k])
 
 
 def backward_kernel(arrived, inner, back_cos, back_sin, blocks_h, blocks_l, out):
@@ -428,96 +498,39 @@
     out[...] = jnp.where(square < 64, full[:128], full[128:])
 
 
-def last_kernel(arrived, out):
-    tall = arrived[...].T
-    out[:, :128] = tall[:ROWS]
-    out[:, 128:] = tall[ROWS:]
-
-
 VMEM = pl.BlockSpec(memory_space=pltpu.VMEM)
-SMEM = pl.BlockSpec(memory_space=pltpu.SMEM)
-HBM = pl.BlockSpec(memory_space=pltpu.HBM)
-
-
-def call(kernel, shapes, *args, name, smem=0, hbm=0, scratch=(), room=32):
+
+
+def call(kernel, shapes, *args, name):
     many = isinstance(shapes, list)
     outs = [jax.ShapeDtypeStruct(s, F32) for s in (shapes if many else [shapes])]
     return pl.pallas_call(
         kernel,
         out_shape=outs if many else outs[0],
-        in_specs=[SMEM] * smem + [HBM] * hbm + [VMEM] * (len(args) - smem - hbm),
+        in_specs=[VMEM] * len(args),
         out_specs=[VMEM] * len(outs) if many else VMEM,
-        scratch_shapes=scratch,
         name=name,
-        compiler_params=pltpu.CompilerParams(vmem_limit_bytes=room * 1024 * 1024),
-        cost_estimate=pl.CostEstimate(flops=100_000_000, bytes_accessed=1_000_000, transcendentals=0),
+        compiler_params=pltpu.CompilerParams(vmem_limit_bytes=32 * 1024 * 1024),
+        cost_estimate=pl.CostEstimate(
+            flops=20_000_000_000, bytes_accessed=1_000_000, transcendentals=0
+        ),
     )(*args)
-
-
-def radial_tables(shift):
-    shape = (256, 128)
-    row = lax.broadcasted_iota(jnp.int32, shape, 0)
-    lane = lax.broadcasted_iota(jnp.int32, shape, 1)
-    line = lane % 64 // 8
-    inside = lane % 8
-    wave = lax.axis_index("gx") * 4 + line + GY * lax.axis_index("gy")
-    wave = jnp.where(line < 4, wave, NY // 2)
-    sigma = wave * shift % NY
-    sign = jnp.where(lane < 64, 1.0, -1.0)
-
-    def phase(cell):
-        angle = (sigma * cell % (NX * NY)).astype(F32) * (2.0 * jnp.pi / (NX * NY))
-        return jnp.cos(angle), jnp.sin(angle) * sign
-
-    there = phase(row + COLS * inside)
-    back = phase(row // 128 * 128 + row // 32 % 4 + 4 * (row % 32) + COLS * inside)
-    n = inside + 8 * row
-    n = jnp.where(n < NX // 2, n, n - NX)
-    kx = 2.0 * jnp.pi / NX * (n.astype(F32) + sigma.astype(F32) / NY)
-    ky = 2.0 * jnp.pi / NY * wave.astype(F32)
-    size = jnp.sqrt(kx * kx + ky * ky)
-    anchor = (wave == 0) & (n == 0)
-    size = jnp.where(anchor, 1.0, size)
-    single = (wave == 0) | (wave == NY // 2)
-    scale = jnp.where(single, 1.0, 2.0) / (NX * NY)
-    weights = jnp.where(anchor, 0.0, -jnp.exp(-thickness * size) / size) * scale
-    angle = sigma[:8].astype(F32) * (2.0 * jnp.pi / NY)
-    last = inside[:8] == 7
-    wrap_cos = jnp.where(last, jnp.cos(angle), 1.0)
-    wrap_sin = jnp.where(last, jnp.sin(angle) * sign[:8], 0.0)
-    return *there, *back, weights, wrap_cos, wrap_sin
 
 
 def shards(density, xmomentum, ymomentum, shear_shift):
     t = host_tables()
     rho, mx, my = density[0], xmomentum[0], ymomentum[0]
-    shift = shear_shift[0]
-    radial = lax.axis_index("gx")
-    scalars = jnp.where(radial == GX - 1, shift % ROWS, 0).astype(jnp.int32).reshape(1)
-    shifts = jnp.broadcast_to(shift, (8, 128))
+    shifts = jnp.broadcast_to(shear_shift[0], (8, 128))
     everyone = ("gx", "gy")
     block = (ROWS, COLS)
     table = (256, 128)
-    columns = call(
-        pack_kernel,
-        table,
-        shear_shift,
-        rho,
-        mx,
-        my,
-        name="pack",
-        hbm=4,
-        room=62,
-        scratch=(
-            pltpu.VMEM((3, *block), F32),
-            pltpu.SMEM((1,), jnp.int32),
-            pltpu.SemaphoreType.DMA((4,)),
-        ),
-    )
+    small = (8, 128)
+    tables = call(tables_kernel, [table] * 5 + [small] * 2, shifts, name="tables")
+    columns = call(pack_kernel, table, shifts, rho, mx, my, tables[-1], name="pack")
     columns = lax.all_to_all(columns, everyone, 0, 0, tiled=True)
-    waves = call(
+    waves, fluxes = call(
         forward_kernel,
-        table,
+        [table, (16, 256)],
         shifts,
         columns,
         *t["blocks"],
@@ -527,13 +540,13 @@
         name="forward",
     )
     waves = lax.all_to_all(waves, everyone, 0, 0, tiled=True)
-    ride = call(edges_kernel, table, shifts, columns, name="edges")
     solved = call(
         radial_kernel,
         table,
+        shifts,
         waves,
-        ride,
-        *radial_tables(shift),
+        fluxes,
+        *tables,
         *t["groups"],
         t["radial_cos"],
         t["radial_sin"],
@@ -556,10 +569,9 @@
         name="backward",
     )
     lines = lax.all_to_all(lines, "gy", 0, 0, tiled=True)
-    rho_new, mx_new, my_new = call(
-        finish_kernel, [block, block, block], scalars, rho, mx, my, solved, name="finish", smem=1
-    )
-    potential = call(last_kernel, block, lines, name="last")
+    rho_new, mx_new, my_new, potential = call(
+        finish_kernel, [block] * 4, shifts, rho, mx, my, solved, lines, name="finish"
+    )
     return rho_new[None], mx_new[None], my_new[None], potential[None]
 
 

time: 87.5 us -> 84.8 us (0.969)
  blocking collectives: 18.5 us -> 77.2 us
  waiting for transfers between devices: 30.2 us -> 0 us
  starting transfers between devices: 25.7 us -> 0 us
  Pallas kernels: 8.75 us -> 5.08 us
  other arithmetic: 2.04 us -> 0 us
    all_to_all x0 -> x3, blocking collectives: none -> 58.6 us  [the longest x1 28.4 us: shards(): columns = lax.all_to_all(columns, everyone, 0, 0, tiled=True)]
    all_to_all x3 -> x0, waiting for transfers between devices: 30.2 us -> none  [the longest x1 12 us: shards(): columns = lax.all_to_all(columns, everyone, 0, 0, tiled=True)]
    all_to_all x3 -> x0, starting transfers between devices: 25.7 us -> none  [the longest x1 15.7 us: shards(): columns = lax.all_to_all(columns, everyone, 0, 0, tiled=True)]
    pallas_call x7 -> x6, Pallas kernels: 8.75 us -> 5.08 us  [call(): pl.pallas_call(kernel, out_shape=outs if many else outs[0], in_specs=[VME...]
    mul x3 -> x0, other arithmetic: 1.86 us -> none  [the longest x1 1.2 us: phase(): return (jnp.cos(angle), jnp.sin(angle) * sign)]
  transfers between devices with their start and end apart: 3 -> 0, of which waited for: 3 -> 0; matrix products, arithmetic and copies ran while one was open for 2% -> 0% of each run, Pallas kernels for 2% -> 0%
where the time goes in v4:
time: 84.8 us; the launch traced here: 84.6 us
  blocking collectives  77.2 us (91%)
  Pallas kernels  5.08 us (6%)
  between operations  1.58 us (2%)
    all_to_all x1, blocking collectives, shards(): columns = lax.all_to_all(columns, everyone, 0, 0, tiled=True)  28.4 us
    all_to_all x1, blocking collectives, shards(): solved = lax.all_to_all(solved, everyone, 0, 0, tiled=True)  18.5 us
    all_to_all x1, blocking collectives, shards(): waves = lax.all_to_all(waves, everyone, 0, 0, tiled=True)  18.5 us
    all_to_all x1, blocking collectives, shards(): lines = lax.all_to_all(lines, 'gy', 0, 0, tiled=True)  11.7 us
    pallas_call x6, Pallas kernels, call(): pl.pallas_call(kernel, out_shape=outs if many else outs[0], in_specs=[VME...  5.08 us

profile of v4, /device:TPU:1, one launch (start us, length us, event | category | flops | bytes accessed | tf_op | source)
XLA Modules:
  0.0 84.6 jit_solution(3690789653767119333)
XLA Ops:
  1.3 0.0 copy-start
  1.3 0.0 copy-start.1
  1.3 0.0 copy-start.2
  1.3 0.3 tables.1
  1.6 0.5 copy-done
  2.1 0.0 copy-done.1
  2.2 0.0 copy-done.2
  2.2 0.0 copy-start.23
  2.2 0.3 pack.1
  2.5 28.4 %all_to_all.44 = f32[256,1,128]{2,1,0:T(1,128)S(1)} all-to-all(f32[256,1,128]{2,1,0:T(1,128)S(1)} %bitcast.29), channel_id=1, replica_groups=mesh['gx'=8,'gy'=32] {'gx','gy'}, dimensions={0} | all-to-all | bytes 262144 | tf_op jit(solution)/shard_map/all_to_all | solution.py:530
  31.0 0.0 copy-done.10
  31.0 0.0 copy-done.19
  31.0 0.0 copy-done.20
  31.0 0.0 copy-done.21
  31.0 0.0 copy-done.23
  31.0 0.0 copy-done.9
  31.0 0.0 copy-start.6
  31.0 0.0 copy-start.7
  31.0 0.0 copy-start.8
  31.0 0.0 copy-start.13
  31.0 0.0 copy-start.14
  31.1 0.0 copy-start.15
  31.1 0.0 copy-start.16
  31.1 0.0 copy-start.17
  31.1 0.0 copy-start.18
  31.1 0.8 forward.1
  31.9 0.0 copy-start.5
  31.9 18.5 %all_to_all.45 = f32[256,1,128]{2,1,0:T(1,128)S(1)} all-to-all(f32[256,1,128]{2,1,0:T(1,128)S(1)} %bitcast.28), channel_id=1, replica_groups=mesh['gx'=8,'gy'=32] {'gx','gy'}, dimensions={0} | all-to-all | bytes 262144 | tf_op jit(solution)/shard_map/all_to_all | solution.py:542
  50.5 0.0 copy-done.6
  50.5 0.0 copy-done.7
  50.5 0.0 copy-done.8
  50.5 0.0 copy-done.13
  50.5 0.0 copy-done.14
  50.5 0.0 copy-done.15
  50.5 0.0 copy-done.16
  50.5 0.0 copy-done.17
  50.5 0.0 copy-done.18
  50.6 0.0 copy-start.4
  50.6 0.0 copy-start.11
  50.6 0.0 copy-start.12
  50.6 0.0 copy-start.22
  50.6 1.9 %radial.1 = f32[256,128]{1,0:T(8,128)S(1)} custom-call(s32[8,128]{1,0:T(8,128)S(1)} %broadcast_in_dim.15.shifts, f32[256,128]{1,0:T(8,128)S(1)} %bitcast.23, f32[16,256]{1,0:T(8,128)S(1)} %get-tuple-element.19.fluxes, f32[256,128]{1,0:T(8,128)S(1)} %get-tuple-element.20.theta_cos, f32[256,128]{1,0:T(8,128)S(1)} %get-tuple-element.21.theta_sin, ...), custom_call_target="tpu_custom_call" | custom-call | flops 20000000000 | bytes 1000000 | tf_op jit(solution)/shard_map/radial/pallas_call | solution.py:507
  52.5 0.0 copy-start.3
  52.5 18.5 %all_to_all.46 = f32[256,1,128]{2,1,0:T(1,128)S(1)} all-to-all(f32[256,1,128]{2,1,0:T(1,128)S(1)} %bitcast.24), channel_id=1, replica_groups=mesh['gx'=8,'gy'=32] {'gx','gy'}, dimensions={0} | all-to-all | bytes 262144 | tf_op jit(solution)/shard_map/all_to_all | solution.py:560
  71.0 0.0 copy-done.11
  71.1 0.8 backward.1
  71.8 11.7 %all_to_all.47 = f32[32,4,128]{2,1,0:T(4,128)S(1)} all-to-all(f32[32,4,128]{2,1,0:T(4,128)S(1)} %bitcast.31), channel_id=1, replica_groups=mesh['gx'=8,'gy'=32] {'gy'}, dimensions={0} | all-to-all | bytes 131072 | tf_op jit(solution)/shard_map/all_to_all | solution.py:571
  83.5 1.1 %finish.1 = (f32[64,256]{1,0:T(8,128)}, f32[64,256]{1,0:T(8,128)}, f32[64,256]{1,0:T(8,128)}, f32[64,256]{1,0:T(8,128)}) custom-call(s32[8,128]{1,0:T(8,128)S(1)} %broadcast_in_dim.15.shifts, f32[64,256]{1,0:T(8,128)S(1)} %bitcast.33, f32[64,256]{1,0:T(8,128)S(1)} %bitcast.35, f32[64,256]{1,0:T(8,128)S(1)} %bitcast.37, f32[256,128]{1,0:T(8,128)S(1)} %bitcast.26, ...), custom_call_target="tpu_custom_call" | custom-call | flops 20000000000 | bytes 1000000 | tf_op jit(solution)/shard_map/finish/pallas_call | solution.py:507
  (11 shorter events, 0.0 us)
Async XLA Ops:
  1.3 0.8 copy-start
  1.3 0.9 %copy-start.1 = (f32[1,64,256]{2,1,0:T(8,128)S(1)}, f32[1,64,256]{2,1,0:T(8,128)}, u32[]{:S(2)}) copy-start(f32[1,64,256]{2,1,0:T(8,128)} %param.26) | copy-start | bytes 196612
  1.3 0.9 %copy-start.2 = (f32[1,64,256]{2,1,0:T(8,128)S(1)}, f32[1,64,256]{2,1,0:T(8,128)}, u32[]{:S(2)}) copy-start(f32[1,64,256]{2,1,0:T(8,128)} %param.27) | copy-start | bytes 196612
  2.2 28.8 %copy-start.10 = (bf16[256,512]{1,0:T(8,128)(2,1)S(1)}, bf16[256,512]{1,0:T(8,128)(2,1)}, u32[]{:S(2)}) copy-start(bf16[256,512]{1,0:T(8,128)(2,1)} %constant.42.clone.blocks_h) | copy-start | bytes 786436
  2.2 28.8 %copy-start.19 = (f32[64,256]{1,0:T(8,128)S(1)}, f32[64,256]{1,0:T(8,128)}, u32[]{:S(2)}) copy-start(f32[64,256]{1,0:T(8,128)} %constant.45.clone.twist_sin) | copy-start | bytes 196612
  2.2 28.8 %copy-start.20 = (f32[64,256]{1,0:T(8,128)S(1)}, f32[64,256]{1,0:T(8,128)}, u32[]{:S(2)}) copy-start(f32[64,256]{1,0:T(8,128)} %constant.44.clone.twist_cos) | copy-start | bytes 196612
  2.2 28.8 %copy-start.21 = (bf16[80,256]{1,0:T(8,128)(2,1)S(1)}, bf16[80,256]{1,0:T(8,128)(2,1)}, u32[]{:S(2)}) copy-start(bf16[80,256]{1,0:T(8,128)(2,1)} %constant.46.clone.inner_h) | copy-start | bytes 122884
  2.2 28.8 %copy-start.23 = (bf16[80,128]{1,0:T(8,128)(2,1)S(1)}, bf16[80,128]{1,0:T(8,128)(2,1)}, u32[]{:S(2)}) copy-start(bf16[80,128]{1,0:T(8,128)(2,1)} %constant.47.clone.inner_l) | copy-start | bytes 61444
  2.5 28.4 %copy-start.9 = (bf16[256,512]{1,0:T(8,128)(2,1)S(1)}, bf16[256,512]{1,0:T(8,128)(2,1)}, u32[]{:S(2)}) copy-start(bf16[256,512]{1,0:T(8,128)(2,1)} %constant.43.clone.blocks_l) | copy-start | bytes 786436
  31.0 19.5 %copy-start.6 = (bf16[512,256]{1,0:T(8,128)(2,1)S(1)}, bf16[512,256]{1,0:T(8,128)(2,1)}, u32[]{:S(2)}) copy-start(bf16[512,256]{1,0:T(8,128)(2,1)} %constant.54.clone.groups_back_h) | copy-start | bytes 786436
  31.0 19.5 %copy-start.7 = (bf16[512,256]{1,0:T(8,128)(2,1)S(1)}, bf16[512,256]{1,0:T(8,128)(2,1)}, u32[]{:S(2)}) copy-start(bf16[512,256]{1,0:T(8,128)(2,1)} %constant.49.clone.groups_l) | copy-start | bytes 786436
  31.0 19.5 %copy-start.8 = (bf16[512,256]{1,0:T(8,128)(2,1)S(1)}, bf16[512,256]{1,0:T(8,128)(2,1)}, u32[]{:S(2)}) copy-start(bf16[512,256]{1,0:T(8,128)(2,1)} %constant.48.clone.groups_h) | copy-start | bytes 786436
  31.0 19.5 %copy-start.13 = (f32[256,128]{1,0:T(8,128)S(1)}, f32[256,128]{1,0:T(8,128)}, u32[]{:S(2)}) copy-start(f32[256,128]{1,0:T(8,128)} %constant.57.clone.return_sin) | copy-start | bytes 393220
  31.0 19.5 %copy-start.14 = (f32[256,128]{1,0:T(8,128)S(1)}, f32[256,128]{1,0:T(8,128)}, u32[]{:S(2)}) copy-start(f32[256,128]{1,0:T(8,128)} %constant.56.clone.return_cos) | copy-start | bytes 393220
  31.1 19.5 %copy-start.15 = (bf16[256,256]{1,0:T(8,128)(2,1)S(1)}, bf16[256,256]{1,0:T(8,128)(2,1)}, u32[]{:S(2)}) copy-start(bf16[256,256]{1,0:T(8,128)(2,1)} %constant.53.clone.cells_back) | copy-start | bytes 393220
  31.1 19.5 %copy-start.16 = (bf16[256,256]{1,0:T(8,128)(2,1)S(1)}, bf16[256,256]{1,0:T(8,128)(2,1)}, u32[]{:S(2)}) copy-start(bf16[256,256]{1,0:T(8,128)(2,1)} %constant.52.clone.cells) | copy-start | bytes 393220
  31.1 19.5 %copy-start.17 = (f32[256,128]{1,0:T(8,128)S(1)}, f32[256,128]{1,0:T(8,128)}, u32[]{:S(2)}) copy-start(f32[256,128]{1,0:T(8,128)} %constant.51.clone.radial_sin) | copy-start | bytes 393220
  31.1 19.5 %copy-start.18 = (f32[256,128]{1,0:T(8,128)S(1)}, f32[256,128]{1,0:T(8,128)}, u32[]{:S(2)}) copy-start(f32[256,128]{1,0:T(8,128)} %constant.50.clone.radial_cos) | copy-start | bytes 393220
  31.9 18.6 %copy-start.5 = (bf16[512,256]{1,0:T(8,128)(2,1)S(1)}, bf16[512,256]{1,0:T(8,128)(2,1)}, u32[]{:S(2)}) copy-start(bf16[512,256]{1,0:T(8,128)(2,1)} %constant.55.clone.groups_back_l) | copy-start | bytes 786436
  50.6 20.5 %copy-start.4 = (bf16[256,512]{1,0:T(8,128)(2,1)S(1)}, bf16[256,512]{1,0:T(8,128)(2,1)}, u32[]{:S(2)}) copy-start(bf16[256,512]{1,0:T(8,128)(2,1)} %constant.61.clone.blocks_h) | copy-start | bytes 786436
  50.6 20.5 %copy-start.11 = (f32[64,512]{1,0:T(8,128)S(1)}, f32[64,512]{1,0:T(8,128)}, u32[]{:S(2)}) copy-start(f32[64,512]{1,0:T(8,128)} %constant.60.clone.back_sin) | copy-start | bytes 393220
  50.6 20.5 %copy-start.12 = (f32[64,512]{1,0:T(8,128)S(1)}, f32[64,512]{1,0:T(8,128)}, u32[]{:S(2)}) copy-start(f32[64,512]{1,0:T(8,128)} %constant.59.clone.back_cos) | copy-start | bytes 393220
  50.6 20.5 %copy-start.22 = (bf16[128,96]{1,0:T(8,128)(2,1)S(1)}, bf16[128,96]{1,0:T(8,128)(2,1)}, u32[]{:S(2)}) copy-start(bf16[128,96]{1,0:T(8,128)(2,1)} %constant.58.clone.inner) | copy-start | bytes 73732
  52.5 18.6 %copy-start.3 = (bf16[256,512]{1,0:T(8,128)(2,1)S(1)}, bf16[256,512]{1,0:T(8,128)(2,1)}, u32[]{:S(2)}) copy-start(bf16[256,512]{1,0:T(8,128)(2,1)} %constant.62.clone.blocks_l) | copy-start | bytes 786436

commit v5 on v4

--- a/solution.py
+++ b/solution.py
@@ -256,15 +256,17 @@
     return jnp.where((k + 1) & 2 == 2, -cosine, cosine), jnp.where(k & 2 == 2, -sine, sine)
 
 
-def tables_kernel(shifts, there_cos, there_sin, back_cos, back_sin, weights, wrap_cos, wrap_sin):
-    def line_of(shape):
-        lane = lanes_of(shape)
-        line = (lane & 63) >> 3
-        wave = lax.axis_index("gx") * 4 + line + GY * lax.axis_index("gy")
-        return lane, jnp.where(line < 4, wave, NY // 2)
-
-    lane, wave = line_of((8, 128))
-    sigma = ((wave * shifts[...]) & (NY - 1)).astype(F32)[0:1]
+def waves_kernel(waves):
+    line = (lanes_of((8, 128)) & 63) >> 3
+    wave = lax.axis_index("gx") * 4 + line + GY * lax.axis_index("gy")
+    waves[...] = jnp.where(line < 4, wave, NY // 2)
+
+
+def tables_kernel(
+    shifts, waves, there_cos, there_sin, back_cos, back_sin, weights, wrap_cos, wrap_sin
+):
+    lane = lanes_of((8, 128))
+    sigma = ((waves[...] * shifts[...]) & (NY - 1)).astype(F32)[0:1]
     sign = jnp.where(lane < 64, 1.0, -1.0)[0:1]
 
     def phase(rows, of_row, of_lane):
@@ -290,7 +292,8 @@
         phase(32, lambda r: 4 * r, 1),
     )
     shape = (256, 128)
-    lane, wave = line_of(shape)
+    lane = lanes_of(shape)
+    wave = jnp.broadcast_to(waves[0:1, :], shape)
     n = (lane & 7) + 8 * rows_of(shape)
     n = jnp.where(n < NX // 2, n, n - NX)
     kx = 2.0 * np.pi / NX * (n.astype(F32) + sigma * (1.0 / NY))
@@ -501,9 +504,9 @@
 VMEM = pl.BlockSpec(memory_space=pltpu.VMEM)
 
 
-def call(kernel, shapes, *args, name):
+def call(kernel, shapes, *args, name, work=20_000, kind=F32):
     many = isinstance(shapes, list)
-    outs = [jax.ShapeDtypeStruct(s, F32) for s in (shapes if many else [shapes])]
+    outs = [jax.ShapeDtypeStruct(s, kind) for s in (shapes if many else [shapes])]
     return pl.pallas_call(
         kernel,
         out_shape=outs if many else outs[0],
@@ -512,7 +515,7 @@
         name=name,
         compiler_params=pltpu.CompilerParams(vmem_limit_bytes=32 * 1024 * 1024),
         cost_estimate=pl.CostEstimate(
-            flops=20_000_000_000, bytes_accessed=1_000_000, transcendentals=0
+            flops=work * 1_000_000, bytes_accessed=1_000_000, transcendentals=0
         ),
     )(*args)
 
@@ -525,7 +528,8 @@
     block = (ROWS, COLS)
     table = (256, 128)
     small = (8, 128)
-    tables = call(tables_kernel, [table] * 5 + [small] * 2, shifts, name="tables")
+    numbers = call(waves_kernel, small, name="waves", kind=jnp.int32)
+    tables = call(tables_kernel, [table] * 5 + [small] * 2, shifts, numbers, name="tables", work=1)
     columns = call(pack_kernel, table, shifts, rho, mx, my, tables[-1], name="pack")
     columns = lax.all_to_all(columns, everyone, 0, 0, tiled=True)
     waves, fluxes = call(

time: 84.8 us -> 84.3 us (level)
    pallas_call x6 -> x7, Pallas kernels: 5.08 us -> 5.08 us  [call(): pl.pallas_call(kernel, out_shape=outs if many else outs[0], in_specs=[VME...]
where the time goes in v5:
time: 84.3 us; the launch traced here: 84.1 us
  blocking collectives  77.2 us (92%)
  Pallas kernels  5.08 us (6%)
  between operations  1.68 us (2%)
    all_to_all x1, blocking collectives, shards(): columns = lax.all_to_all(columns, everyone, 0, 0, tiled=True)  28.4 us
    all_to_all x1, blocking collectives, shards(): solved = lax.all_to_all(solved, everyone, 0, 0, tiled=True)  18.6 us
    all_to_all x1, blocking collectives, shards(): waves = lax.all_to_all(waves, everyone, 0, 0, tiled=True)  18.5 us
    all_to_all x1, blocking collectives, shards(): lines = lax.all_to_all(lines, 'gy', 0, 0, tiled=True)  11.7 us
    pallas_call x7, Pallas kernels, call(): pl.pallas_call(kernel, out_shape=outs if many else outs[0], in_specs=[VME...  5.08 us

profile of v5, /device:TPU:1, one launch (start us, length us, event | category | flops | bytes accessed | tf_op | source)
XLA Modules:
  0.0 84.1 jit_solution(7115519692011144209)
XLA Ops:
  0.6 0.0 copy-start.2
  0.6 0.0 copy-start.1
  0.7 0.0 copy-start
  1.4 0.3 tables.1
  1.7 0.0 copy-done.2
  1.7 0.0 copy-done.1
  1.7 0.0 copy-done
  1.7 0.0 copy-start.10
  1.7 0.0 copy-start.19
  1.7 0.0 copy-start.20
  1.7 0.0 copy-start.21
  1.7 0.0 copy-start.23
  1.7 0.3 pack.1
  2.1 28.4 %all_to_all.44 = f32[256,1,128]{2,1,0:T(1,128)S(1)} all-to-all(f32[256,1,128]{2,1,0:T(1,128)S(1)} %bitcast.29), channel_id=1, replica_groups=mesh['gx'=8,'gy'=32] {'gx','gy'}, dimensions={0} | all-to-all | bytes 262144 | tf_op jit(solution)/shard_map/all_to_all | solution.py:534
  30.5 0.0 copy-done.10
  30.5 0.0 copy-done.19
  30.5 0.0 copy-done.20
  30.5 0.0 copy-done.21
  30.5 0.0 copy-done.23
  30.5 0.0 copy-done.9
  30.5 0.0 copy-start.6
  30.5 0.0 copy-start.7
  30.5 0.0 copy-start.8
  30.6 0.0 copy-start.13
  30.6 0.0 copy-start.14
  30.6 0.0 copy-start.15
  30.6 0.0 copy-start.16
  30.6 0.0 copy-start.17
  30.6 0.0 copy-start.18
  30.6 0.8 forward.1
  31.5 0.0 copy-start.5
  31.5 18.5 %all_to_all.45 = f32[256,1,128]{2,1,0:T(1,128)S(1)} all-to-all(f32[256,1,128]{2,1,0:T(1,128)S(1)} %bitcast.28), channel_id=1, replica_groups=mesh['gx'=8,'gy'=32] {'gx','gy'}, dimensions={0} | all-to-all | bytes 262144 | tf_op jit(solution)/shard_map/all_to_all | solution.py:546
  50.0 0.0 copy-done.6
  50.0 0.0 copy-done.7
  50.0 0.0 copy-done.8
  50.0 0.0 copy-done.13
  50.0 0.0 copy-done.14
  50.0 0.0 copy-done.15
  50.1 0.0 copy-start.4
  50.1 0.0 copy-start.11
  50.1 0.0 copy-start.12
  50.1 0.0 copy-start.22
  50.1 1.9 %radial.1 = f32[256,128]{1,0:T(8,128)S(1)} custom-call(s32[8,128]{1,0:T(8,128)S(1)} %broadcast_in_dim.15.shifts, f32[256,128]{1,0:T(8,128)S(1)} %bitcast.23, f32[16,256]{1,0:T(8,128)S(1)} %get-tuple-element.19.fluxes, f32[256,128]{1,0:T(8,128)S(1)} %get-tuple-element.20.theta_cos, f32[256,128]{1,0:T(8,128)S(1)} %get-tuple-element.21.theta_sin, ...), custom_call_target="tpu_custom_call" | custom-call | flops 20000000000 | bytes 1000000 | tf_op jit(solution)/shard_map/radial/pallas_call | solution.py:510
  52.0 0.0 copy-start.3
  52.0 18.6 %all_to_all.46 = f32[256,1,128]{2,1,0:T(1,128)S(1)} all-to-all(f32[256,1,128]{2,1,0:T(1,128)S(1)} %bitcast.24), channel_id=1, replica_groups=mesh['gx'=8,'gy'=32] {'gx','gy'}, dimensions={0} | all-to-all | bytes 262144 | tf_op jit(solution)/shard_map/all_to_all | solution.py:564
  70.6 0.8 backward.1
  71.4 11.7 %all_to_all.47 = f32[32,4,128]{2,1,0:T(4,128)S(1)} all-to-all(f32[32,4,128]{2,1,0:T(4,128)S(1)} %bitcast.31), channel_id=1, replica_groups=mesh['gx'=8,'gy'=32] {'gy'}, dimensions={0} | all-to-all | bytes 131072 | tf_op jit(solution)/shard_map/all_to_all | solution.py:575
  83.0 1.1 %finish.1 = (f32[64,256]{1,0:T(8,128)}, f32[64,256]{1,0:T(8,128)}, f32[64,256]{1,0:T(8,128)}, f32[64,256]{1,0:T(8,128)}) custom-call(s32[8,128]{1,0:T(8,128)S(1)} %broadcast_in_dim.15.shifts, f32[64,256]{1,0:T(8,128)S(1)} %bitcast.33, f32[64,256]{1,0:T(8,128)S(1)} %bitcast.35, f32[64,256]{1,0:T(8,128)S(1)} %bitcast.37, f32[256,128]{1,0:T(8,128)S(1)} %bitcast.26, ...), custom_call_target="tpu_custom_call" | custom-call | flops 20000000000 | bytes 1000000 | tf_op jit(solution)/shard_map/finish/pallas_call | solution.py:510
  (12 shorter events, 0.0 us)
Async XLA Ops:
  0.6 1.0 %copy-start.2 = (f32[1,64,256]{2,1,0:T(8,128)S(1)}, f32[1,64,256]{2,1,0:T(8,128)}, u32[]{:S(2)}) copy-start(f32[1,64,256]{2,1,0:T(8,128)} %param.27) | copy-start | bytes 196612
  0.6 1.0 %copy-start.1 = (f32[1,64,256]{2,1,0:T(8,128)S(1)}, f32[1,64,256]{2,1,0:T(8,128)}, u32[]{:S(2)}) copy-start(f32[1,64,256]{2,1,0:T(8,128)} %param.26) | copy-start | bytes 196612
  0.7 1.0 %copy-start = (f32[1,64,256]{2,1,0:T(8,128)S(1)}, f32[1,64,256]{2,1,0:T(8,128)}, u32[]{:S(2)}) copy-start(f32[1,64,256]{2,1,0:T(8,128)} %param.25) | copy-start | bytes 196612
  1.7 28.8 %copy-start.10 = (bf16[256,512]{1,0:T(8,128)(2,1)S(1)}, bf16[256,512]{1,0:T(8,128)(2,1)}, u32[]{:S(2)}) copy-start(bf16[256,512]{1,0:T(8,128)(2,1)} %constant.42.clone.blocks_h) | copy-start | bytes 786436
  1.7 28.8 %copy-start.19 = (f32[64,256]{1,0:T(8,128)S(1)}, f32[64,256]{1,0:T(8,128)}, u32[]{:S(2)}) copy-start(f32[64,256]{1,0:T(8,128)} %constant.45.clone.twist_sin) | copy-start | bytes 196612
  1.7 28.8 %copy-start.20 = (f32[64,256]{1,0:T(8,128)S(1)}, f32[64,256]{1,0:T(8,128)}, u32[]{:S(2)}) copy-start(f32[64,256]{1,0:T(8,128)} %constant.44.clone.twist_cos) | copy-start | bytes 196612
  1.7 28.8 %copy-start.21 = (bf16[80,256]{1,0:T(8,128)(2,1)S(1)}, bf16[80,256]{1,0:T(8,128)(2,1)}, u32[]{:S(2)}) copy-start(bf16[80,256]{1,0:T(8,128)(2,1)} %constant.46.clone.inner_h) | copy-start | bytes 122884
  1.7 28.8 %copy-start.23 = (bf16[80,128]{1,0:T(8,128)(2,1)S(1)}, bf16[80,128]{1,0:T(8,128)(2,1)}, u32[]{:S(2)}) copy-start(bf16[80,128]{1,0:T(8,128)(2,1)} %constant.47.clone.inner_l) | copy-start | bytes 61444
  2.1 28.4 %copy-start.9 = (bf16[256,512]{1,0:T(8,128)(2,1)S(1)}, bf16[256,512]{1,0:T(8,128)(2,1)}, u32[]{:S(2)}) copy-start(bf16[256,512]{1,0:T(8,128)(2,1)} %constant.43.clone.blocks_l) | copy-start | bytes 786436
  30.5 19.5 %copy-start.6 = (bf16[512,256]{1,0:T(8,128)(2,1)S(1)}, bf16[512,256]{1,0:T(8,128)(2,1)}, u32[]{:S(2)}) copy-start(bf16[512,256]{1,0:T(8,128)(2,1)} %constant.54.clone.groups_back_h) | copy-start | bytes 786436
  30.5 19.5 %copy-start.7 = (bf16[512,256]{1,0:T(8,128)(2,1)S(1)}, bf16[512,256]{1,0:T(8,128)(2,1)}, u32[]{:S(2)}) copy-start(bf16[512,256]{1,0:T(8,128)(2,1)} %constant.49.clone.groups_l) | copy-start | bytes 786436
  30.5 19.5 %copy-start.8 = (bf16[512,256]{1,0:T(8,128)(2,1)S(1)}, bf16[512,256]{1,0:T(8,128)(2,1)}, u32[]{:S(2)}) copy-start(bf16[512,256]{1,0:T(8,128)(2,1)} %constant.48.clone.groups_h) | copy-start | bytes 786436
  30.6 19.5 %copy-start.13 = (f32[256,128]{1,0:T(8,128)S(1)}, f32[256,128]{1,0:T(8,128)}, u32[]{:S(2)}) copy-start(f32[256,128]{1,0:T(8,128)} %constant.57.clone.return_sin) | copy-start | bytes 393220
  30.6 19.5 %copy-start.14 = (f32[256,128]{1,0:T(8,128)S(1)}, f32[256,128]{1,0:T(8,128)}, u32[]{:S(2)}) copy-start(f32[256,128]{1,0:T(8,128)} %constant.56.clone.return_cos) | copy-start | bytes 393220
  30.6 19.5 %copy-start.15 = (bf16[256,256]{1,0:T(8,128)(2,1)S(1)}, bf16[256,256]{1,0:T(8,128)(2,1)}, u32[]{:S(2)}) copy-start(bf16[256,256]{1,0:T(8,128)(2,1)} %constant.53.clone.cells_back) | copy-start | bytes 393220
  30.6 19.5 %copy-start.16 = (bf16[256,256]{1,0:T(8,128)(2,1)S(1)}, bf16[256,256]{1,0:T(8,128)(2,1)}, u32[]{:S(2)}) copy-start(bf16[256,256]{1,0:T(8,128)(2,1)} %constant.52.clone.cells) | copy-start | bytes 393220
  30.6 19.5 %copy-start.17 = (f32[256,128]{1,0:T(8,128)S(1)}, f32[256,128]{1,0:T(8,128)}, u32[]{:S(2)}) copy-start(f32[256,128]{1,0:T(8,128)} %constant.51.clone.radial_sin) | copy-start | bytes 393220
  30.6 19.5 %copy-start.18 = (f32[256,128]{1,0:T(8,128)S(1)}, f32[256,128]{1,0:T(8,128)}, u32[]{:S(2)}) copy-start(f32[256,128]{1,0:T(8,128)} %constant.50.clone.radial_cos) | copy-start | bytes 393220
  31.5 18.6 %copy-start.5 = (bf16[512,256]{1,0:T(8,128)(2,1)S(1)}, bf16[512,256]{1,0:T(8,128)(2,1)}, u32[]{:S(2)}) copy-start(bf16[512,256]{1,0:T(8,128)(2,1)} %constant.55.clone.groups_back_l) | copy-start | bytes 786436
  50.1 20.5 %copy-start.4 = (bf16[256,512]{1,0:T(8,128)(2,1)S(1)}, bf16[256,512]{1,0:T(8,128)(2,1)}, u32[]{:S(2)}) copy-start(bf16[256,512]{1,0:T(8,128)(2,1)} %constant.61.clone.blocks_h) | copy-start | bytes 786436
  50.1 20.5 %copy-start.11 = (f32[64,512]{1,0:T(8,128)S(1)}, f32[64,512]{1,0:T(8,128)}, u32[]{:S(2)}) copy-start(f32[64,512]{1,0:T(8,128)} %constant.60.clone.back_sin) | copy-start | bytes 393220
  50.1 20.5 %copy-start.12 = (f32[64,512]{1,0:T(8,128)S(1)}, f32[64,512]{1,0:T(8,128)}, u32[]{:S(2)}) copy-start(f32[64,512]{1,0:T(8,128)} %constant.59.clone.back_cos) | copy-start | bytes 393220
  50.1 20.5 %copy-start.22 = (bf16[128,96]{1,0:T(8,128)(2,1)S(1)}, bf16[128,96]{1,0:T(8,128)(2,1)}, u32[]{:S(2)}) copy-start(bf16[128,96]{1,0:T(8,128)(2,1)} %constant.58.clone.inner) | copy-start | bytes 73732
  52.0 18.6 %copy-start.3 = (bf16[256,512]{1,0:T(8,128)(2,1)S(1)}, bf16[256,512]{1,0:T(8,128)(2,1)}, u32[]{:S(2)}) copy-start(bf16[256,512]{1,0:T(8,128)(2,1)} %constant.62.clone.blocks_l) | copy-start | bytes 786436

commit v6 on v5

--- a/solution.py
+++ b/solution.py
@@ -411,10 +411,9 @@
     def apart(value):
         lane = lanes_of(value.shape)
         first = jnp.zeros(value.shape, jnp.int32) + position() == 0
-        value = jnp.where(lane % 64 < 32, value, 0.0)
         fifth = roll(value, -32, 1)
-        slot = (lane >= 64) & (lane < 72) & first
-        return jnp.where((lane >= 32) & (lane < 40), fifth, jnp.where(slot, 0.0, value))
+        none = ((lane >= 64) & (lane < 72) & first) | ((lane >= 96) & (lane < 104))
+        return jnp.where((lane >= 32) & (lane < 40), fifth, jnp.where(none, 0.0, value))
 
     lane = lanes_of(shape)
     row = rows_of(shape)

time: 84.3 us -> 84.3 us (level)
  no operation moved by 1% of the time
where the time goes in v6:
time: 84.3 us; the launch traced here: 84.1 us
  blocking collectives  77.2 us (92%)
  Pallas kernels  5.08 us (6%)
  between operations  1.68 us (2%)
    all_to_all x1, blocking collectives, shards(): columns = lax.all_to_all(columns, everyone, 0, 0, tiled=True)  28.4 us
    all_to_all x1, blocking collectives, shards(): solved = lax.all_to_all(solved, everyone, 0, 0, tiled=True)  18.6 us
    all_to_all x1, blocking collectives, shards(): waves = lax.all_to_all(waves, everyone, 0, 0, tiled=True)  18.5 us
    all_to_all x1, blocking collectives, shards(): lines = lax.all_to_all(lines, 'gy', 0, 0, tiled=True)  11.7 us
    pallas_call x7, Pallas kernels, call(): pl.pallas_call(kernel, out_shape=outs if many else outs[0], in_specs=[VME...  5.08 us

profile of v6, /device:TPU:1, one launch (start us, length us, event | category | flops | bytes accessed | tf_op | source)
XLA Modules:
  0.0 84.1 jit_solution(11606882375846005868)
XLA Ops:
  0.6 0.0 copy-start.2
  0.6 0.0 copy-start.1
  0.7 0.0 copy-start
  1.4 0.3 tables.1
  1.7 0.0 copy-done.2
  1.7 0.0 copy-done.1
  1.7 0.0 copy-done
  1.7 0.0 copy-start.10
  1.7 0.0 copy-start.19
  1.7 0.0 copy-start.20
  1.7 0.0 copy-start.21
  1.7 0.0 copy-start.23
  1.7 0.3 pack.1
  2.1 28.4 %all_to_all.44 = f32[256,1,128]{2,1,0:T(1,128)S(1)} all-to-all(f32[256,1,128]{2,1,0:T(1,128)S(1)} %bitcast.29), channel_id=1, replica_groups=mesh['gx'=8,'gy'=32] {'gx','gy'}, dimensions={0} | all-to-all | bytes 262144 | tf_op jit(solution)/shard_map/all_to_all | solution.py:533
  30.5 0.0 copy-done.10
  30.5 0.0 copy-done.19
  30.5 0.0 copy-done.20
  30.5 0.0 copy-done.21
  30.5 0.0 copy-done.23
  30.5 0.0 copy-done.9
  30.5 0.0 copy-start.6
  30.5 0.0 copy-start.7
  30.5 0.0 copy-start.8
  30.6 0.0 copy-start.13
  30.6 0.0 copy-start.14
  30.6 0.0 copy-start.15
  30.6 0.0 copy-start.16
  30.6 0.0 copy-start.17
  30.6 0.0 copy-start.18
  30.6 0.8 forward.1
  31.5 0.0 copy-start.5
  31.5 18.5 %all_to_all.45 = f32[256,1,128]{2,1,0:T(1,128)S(1)} all-to-all(f32[256,1,128]{2,1,0:T(1,128)S(1)} %bitcast.28), channel_id=1, replica_groups=mesh['gx'=8,'gy'=32] {'gx','gy'}, dimensions={0} | all-to-all | bytes 262144 | tf_op jit(solution)/shard_map/all_to_all | solution.py:545
  50.0 0.0 copy-done.6
  50.0 0.0 copy-done.7
  50.0 0.0 copy-done.8
  50.0 0.0 copy-done.13
  50.0 0.0 copy-done.14
  50.0 0.0 copy-done.15
  50.1 0.0 copy-start.4
  50.1 0.0 copy-start.11
  50.1 0.0 copy-start.12
  50.1 0.0 copy-start.22
  50.1 1.9 %radial.1 = f32[256,128]{1,0:T(8,128)S(1)} custom-call(s32[8,128]{1,0:T(8,128)S(1)} %broadcast_in_dim.15.shifts, f32[256,128]{1,0:T(8,128)S(1)} %bitcast.23, f32[16,256]{1,0:T(8,128)S(1)} %get-tuple-element.19.fluxes, f32[256,128]{1,0:T(8,128)S(1)} %get-tuple-element.20.theta_cos, f32[256,128]{1,0:T(8,128)S(1)} %get-tuple-element.21.theta_sin, ...), custom_call_target="tpu_custom_call" | custom-call | flops 20000000000 | bytes 1000000 | tf_op jit(solution)/shard_map/radial/pallas_call | solution.py:509
  52.0 0.0 copy-start.3
  52.0 18.6 %all_to_all.46 = f32[256,1,128]{2,1,0:T(1,128)S(1)} all-to-all(f32[256,1,128]{2,1,0:T(1,128)S(1)} %bitcast.24), channel_id=1, replica_groups=mesh['gx'=8,'gy'=32] {'gx','gy'}, dimensions={0} | all-to-all | bytes 262144 | tf_op jit(solution)/shard_map/all_to_all | solution.py:563
  70.6 0.8 backward.1
  71.4 11.7 %all_to_all.47 = f32[32,4,128]{2,1,0:T(4,128)S(1)} all-to-all(f32[32,4,128]{2,1,0:T(4,128)S(1)} %bitcast.31), channel_id=1, replica_groups=mesh['gx'=8,'gy'=32] {'gy'}, dimensions={0} | all-to-all | bytes 131072 | tf_op jit(solution)/shard_map/all_to_all | solution.py:574
  83.0 1.1 %finish.1 = (f32[64,256]{1,0:T(8,128)}, f32[64,256]{1,0:T(8,128)}, f32[64,256]{1,0:T(8,128)}, f32[64,256]{1,0:T(8,128)}) custom-call(s32[8,128]{1,0:T(8,128)S(1)} %broadcast_in_dim.15.shifts, f32[64,256]{1,0:T(8,128)S(1)} %bitcast.33, f32[64,256]{1,0:T(8,128)S(1)} %bitcast.35, f32[64,256]{1,0:T(8,128)S(1)} %bitcast.37, f32[256,128]{1,0:T(8,128)S(1)} %bitcast.26, ...), custom_call_target="tpu_custom_call" | custom-call | flops 20000000000 | bytes 1000000 | tf_op jit(solution)/shard_map/finish/pallas_call | solution.py:509
  (12 shorter events, 0.0 us)
Async XLA Ops:
  0.6 1.0 %copy-start.2 = (f32[1,64,256]{2,1,0:T(8,128)S(1)}, f32[1,64,256]{2,1,0:T(8,128)}, u32[]{:S(2)}) copy-start(f32[1,64,256]{2,1,0:T(8,128)} %param.27) | copy-start | bytes 196612
  0.6 1.0 %copy-start.1 = (f32[1,64,256]{2,1,0:T(8,128)S(1)}, f32[1,64,256]{2,1,0:T(8,128)}, u32[]{:S(2)}) copy-start(f32[1,64,256]{2,1,0:T(8,128)} %param.26) | copy-start | bytes 196612
  0.7 1.0 %copy-start = (f32[1,64,256]{2,1,0:T(8,128)S(1)}, f32[1,64,256]{2,1,0:T(8,128)}, u32[]{:S(2)}) copy-start(f32[1,64,256]{2,1,0:T(8,128)} %param.25) | copy-start | bytes 196612
  1.7 28.8 %copy-start.10 = (bf16[256,512]{1,0:T(8,128)(2,1)S(1)}, bf16[256,512]{1,0:T(8,128)(2,1)}, u32[]{:S(2)}) copy-start(bf16[256,512]{1,0:T(8,128)(2,1)} %constant.42.clone.blocks_h) | copy-start | bytes 786436
  1.7 28.8 %copy-start.19 = (f32[64,256]{1,0:T(8,128)S(1)}, f32[64,256]{1,0:T(8,128)}, u32[]{:S(2)}) copy-start(f32[64,256]{1,0:T(8,128)} %constant.45.clone.twist_sin) | copy-start | bytes 196612
  1.7 28.8 %copy-start.20 = (f32[64,256]{1,0:T(8,128)S(1)}, f32[64,256]{1,0:T(8,128)}, u32[]{:S(2)}) copy-start(f32[64,256]{1,0:T(8,128)} %constant.44.clone.twist_cos) | copy-start | bytes 196612
  1.7 28.8 %copy-start.21 = (bf16[80,256]{1,0:T(8,128)(2,1)S(1)}, bf16[80,256]{1,0:T(8,128)(2,1)}, u32[]{:S(2)}) copy-start(bf16[80,256]{1,0:T(8,128)(2,1)} %constant.46.clone.inner_h) | copy-start | bytes 122884
  1.7 28.8 %copy-start.23 = (bf16[80,128]{1,0:T(8,128)(2,1)S(1)}, bf16[80,128]{1,0:T(8,128)(2,1)}, u32[]{:S(2)}) copy-start(bf16[80,128]{1,0:T(8,128)(2,1)} %constant.47.clone.inner_l) | copy-start | bytes 61444
  2.1 28.4 %copy-start.9 = (bf16[256,512]{1,0:T(8,128)(2,1)S(1)}, bf16[256,512]{1,0:T(8,128)(2,1)}, u32[]{:S(2)}) copy-start(bf16[256,512]{1,0:T(8,128)(2,1)} %constant.43.clone.blocks_l) | copy-start | bytes 786436
  30.5 19.5 %copy-start.6 = (bf16[512,256]{1,0:T(8,128)(2,1)S(1)}, bf16[512,256]{1,0:T(8,128)(2,1)}, u32[]{:S(2)}) copy-start(bf16[512,256]{1,0:T(8,128)(2,1)} %constant.54.clone.groups_back_h) | copy-start | bytes 786436
  30.5 19.5 %copy-start.7 = (bf16[512,256]{1,0:T(8,128)(2,1)S(1)}, bf16[512,256]{1,0:T(8,128)(2,1)}, u32[]{:S(2)}) copy-start(bf16[512,256]{1,0:T(8,128)(2,1)} %constant.49.clone.groups_l) | copy-start | bytes 786436
  30.5 19.5 %copy-start.8 = (bf16[512,256]{1,0:T(8,128)(2,1)S(1)}, bf16[512,256]{1,0:T(8,128)(2,1)}, u32[]{:S(2)}) copy-start(bf16[512,256]{1,0:T(8,128)(2,1)} %constant.48.clone.groups_h) | copy-start | bytes 786436
  30.6 19.5 %copy-start.13 = (f32[256,128]{1,0:T(8,128)S(1)}, f32[256,128]{1,0:T(8,128)}, u32[]{:S(2)}) copy-start(f32[256,128]{1,0:T(8,128)} %constant.57.clone.return_sin) | copy-start | bytes 393220
  30.6 19.5 %copy-start.14 = (f32[256,128]{1,0:T(8,128)S(1)}, f32[256,128]{1,0:T(8,128)}, u32[]{:S(2)}) copy-start(f32[256,128]{1,0:T(8,128)} %constant.56.clone.return_cos) | copy-start | bytes 393220
  30.6 19.5 %copy-start.15 = (bf16[256,256]{1,0:T(8,128)(2,1)S(1)}, bf16[256,256]{1,0:T(8,128)(2,1)}, u32[]{:S(2)}) copy-start(bf16[256,256]{1,0:T(8,128)(2,1)} %constant.53.clone.cells_back) | copy-start | bytes 393220
  30.6 19.5 %copy-start.16 = (bf16[256,256]{1,0:T(8,128)(2,1)S(1)}, bf16[256,256]{1,0:T(8,128)(2,1)}, u32[]{:S(2)}) copy-start(bf16[256,256]{1,0:T(8,128)(2,1)} %constant.52.clone.cells) | copy-start | bytes 393220
  30.6 19.5 %copy-start.17 = (f32[256,128]{1,0:T(8,128)S(1)}, f32[256,128]{1,0:T(8,128)}, u32[]{:S(2)}) copy-start(f32[256,128]{1,0:T(8,128)} %constant.51.clone.radial_sin) | copy-start | bytes 393220
  30.6 19.5 %copy-start.18 = (f32[256,128]{1,0:T(8,128)S(1)}, f32[256,128]{1,0:T(8,128)}, u32[]{:S(2)}) copy-start(f32[256,128]{1,0:T(8,128)} %constant.50.clone.radial_cos) | copy-start | bytes 393220
  31.5 18.6 %copy-start.5 = (bf16[512,256]{1,0:T(8,128)(2,1)S(1)}, bf16[512,256]{1,0:T(8,128)(2,1)}, u32[]{:S(2)}) copy-start(bf16[512,256]{1,0:T(8,128)(2,1)} %constant.55.clone.groups_back_l) | copy-start | bytes 786436
  50.1 20.5 %copy-start.4 = (bf16[256,512]{1,0:T(8,128)(2,1)S(1)}, bf16[256,512]{1,0:T(8,128)(2,1)}, u32[]{:S(2)}) copy-start(bf16[256,512]{1,0:T(8,128)(2,1)} %constant.61.clone.blocks_h) | copy-start | bytes 786436
  50.1 20.5 %copy-start.11 = (f32[64,512]{1,0:T(8,128)S(1)}, f32[64,512]{1,0:T(8,128)}, u32[]{:S(2)}) copy-start(f32[64,512]{1,0:T(8,128)} %constant.60.clone.back_sin) | copy-start | bytes 393220
  50.1 20.5 %copy-start.12 = (f32[64,512]{1,0:T(8,128)S(1)}, f32[64,512]{1,0:T(8,128)}, u32[]{:S(2)}) copy-start(f32[64,512]{1,0:T(8,128)} %constant.59.clone.back_cos) | copy-start | bytes 393220
  50.1 20.5 %copy-start.22 = (bf16[128,96]{1,0:T(8,128)(2,1)S(1)}, bf16[128,96]{1,0:T(8,128)(2,1)}, u32[]{:S(2)}) copy-start(bf16[128,96]{1,0:T(8,128)(2,1)} %constant.58.clone.inner) | copy-start | bytes 73732
  52.0 18.6 %copy-start.3 = (bf16[256,512]{1,0:T(8,128)(2,1)S(1)}, bf16[256,512]{1,0:T(8,128)(2,1)}, u32[]{:S(2)}) copy-start(bf16[256,512]{1,0:T(8,128)(2,1)} %constant.62.clone.blocks_l) | copy-start | bytes 786436
